TPU v7x, 512 devices: a whole 4x8x8 slice. The times are simulated.
512 devices in a mesh: aux: 4 (over x), blk: 128 (over z, y, core).
Axes of the slice: x: 4, y: 8, z: 8, core: 2. Of those that a mesh axis runs over, the one named last changes fastest.
Arguments:
- slabs: bfloat16 [32768, 128, 128], P('blk', 'aux'), may hold values from -0.75 to 0.75
- orbital_start: int32 [128], P('blk'), may hold values from 0 to 4095, as said below
- orbital_count: int32 [128], P('blk'), may hold values from 32 to 128
- partners: int32 [128, 4], P('blk'), may hold values from -1 to 127, as said below
- density: bfloat16 [128, 4, 256, 256], P('blk', None, 'aux'), may hold values from -6 to 6
- direction: bfloat16 [128, 4, 256, 256], P('blk', None, 'aux'), may hold values from -6 to 6
- step_lengths: float32 [3], replicated, may hold values from 0.1 to 1
Outputs:
- exchange_tiles: bfloat16 [128, 4, 256, 256], P('blk', None, 'aux')
- energies: float32 [3], replicated
Inputs may be any that keep to these rules, and one draw needn't show every extreme that they name: orbital_start[i] lies in i * (32) to i * 32 + 128 // 4 - 1. Row i lists distinct partners j with i <= j <= i + 3 and j < 128 in ascending order, always i itself first, then -1 for the empty slots.
All inputs are finite; a program needn't handle non-finite values.
Results may differ from a plain program's by a relative error of at most 0.009.
Values may be sent and summed in bfloat16 or wider, within the bound.
No kernel may reach another device: no remote copies, remote signals or barrier semaphores. Data moves between devices by JAX's collectives and lax.ppermute only.
A program may use at most 64 MiB of HBM per device.

v0:
```python
import math

import jax
import jax.numpy as jnp
from jax import lax
from jax.sharding import PartitionSpec as P


def from_behind(value, axis, steps):
    count = lax.axis_size(axis)
    leading, last = (max(0, -steps), min(count, count - steps))
    return lax.ppermute(value, axis, [(source, source + steps) for source in range(leading, last)])


def pair_tile(left, own_start, own_count, own_width, fetched):
    piece, start_j, count_j = fetched
    rows, auxb, width = piece.shape
    own_lanes = jnp.arange(own_width, dtype=jnp.int32)
    far_lanes = jnp.arange(width, dtype=jnp.int32)
    match = (
        (own_start + own_lanes[:, None] == start_j[0] + far_lanes[None, :])
        & (own_lanes[:, None] < own_count)
        & (far_lanes[None, :] < count_j[0])
    )
    select = match.astype(jnp.bfloat16)
    moved = jnp.dot(
        piece.reshape(rows * auxb, width), select.T, preferred_element_type=jnp.float32
    ).astype(jnp.bfloat16)
    return lax.dot_general(
        left,
        moved.reshape(rows, auxb * own_width),
        (((1,), (1,)), ((), ())),
        preferred_element_type=jnp.float32,
    )


def weighted_terms(weight, dens, dirs, tiles):
    first = jnp.sum(weight * jnp.sum(dens.astype(jnp.float32) * tiles, axis=(1, 2)))
    second = jnp.sum(weight * jnp.sum(dirs.astype(jnp.float32) * tiles, axis=(1, 2)))
    return (first, second)


def body(slabs, orbital_start, orbital_count, partners, density, direction, step_lengths):
    rows, auxb, width = slabs.shape
    slots = partners.shape[1]
    reach = slots - 1
    own = (slabs, orbital_start, orbital_count)
    fetched = [own]
    for offset in range(1, reach + 1):
        fetched.append(from_behind((slabs, orbital_start, orbital_count), "blk", -offset))
    left = slabs.reshape(rows, auxb * width)
    tiles = jnp.stack(
        [pair_tile(left, orbital_start[0], orbital_count[0], width, item) for item in fetched]
    )
    block = lax.axis_index("blk")
    row = partners[0]
    offsets = jnp.arange(slots, dtype=jnp.int32)
    onehot = ((row[:, None] - block == offsets[None, :]) & (row[:, None] >= 0)).astype(jnp.float32)
    slot_partial = jnp.einsum("sk,kmn->smn", onehot, tiles)
    weight = jnp.where(row < 0, 0.0, jnp.where(row == block, 1.0, 2.0)).astype(jnp.float32)
    blocks_total = lax.axis_size("blk")
    scale = 1.0 / (rows * math.sqrt(blocks_total * slots))
    summed = lax.psum_scatter(slot_partial, "aux", scatter_dimension=1, tiled=True)
    first, second = weighted_terms(weight, density[0], direction[0], summed)
    totals = lax.psum(jnp.stack([first, second]), ("aux", "blk"))
    energies = -0.5 * (totals[0] + step_lengths * totals[1]) * scale
    return (summed.astype(jnp.bfloat16)[None], energies)


def solution(mesh):
    return jax.shard_map(
        body,
        mesh=mesh,
        in_specs=(
            P("blk", "aux", None),
            P("blk"),
            P("blk"),
            P("blk", None),
            P("blk", None, "aux", None),
            P("blk", None, "aux", None),
            P(),
        ),
        out_specs=(P("blk", None, "aux", None), P()),
        check_vma=False,
    )
```

profile of v0, /device:TPU:1, one launch (start us, length us, event | category | flops | bytes accessed | tf_op | source)
XLA Modules:
  0.0 373.4 jit_solution(17537656646573798837)
XLA Ops:
  7.2 0.0 all-reduce.3.cloned.1.call-start
  7.2 8.8 %collective-permute-start.2 = (bf16[256,32,128]{2,1,0:T(8,128)(2,1)}, bf16[256,32,128]{2,1,0:T(8,128)(2,1)}, u32[]{:S(2)}, u32[]{:S(2)}) collective-permute-start(bf16[256,32,128]{2,1,0:T(8,128)(2,1)} %param.7), channel_id=1, source_target_pairs={{1,0},{2,1},{3,2},{4,3},{5,4},{6,5},{7,6},{8,7},{9,8},{10,9},{11,1... | collective-permute-start | bytes 6291464 | tf_op jit(solution)/shard_map/ppermute | solution.py:12
  16.0 1.3 collective-permute-start.5
  17.3 1.3 collective-permute-start.8
  18.6 1.9 collective-permute-start
  20.5 1.9 collective-permute-start.1
  23.8 3.7 fusion
  27.5 3.2 copy.21
  30.7 0.0 copy-start.5
  30.7 2.3 reshape.113
  33.1 0.0 copy-done.5
  33.1 3.2 fusion.16
  36.3 59.9 %collective-permute-done = s32[1]{0:T(128)} collective-permute-done((s32[1]{0:T(128)}, s32[1]{0:T(128)}, u32[]{:S(2)}, u32[]{:S(2)}) %collective-permute-start) | collective-permute-done | bytes 36 | tf_op jit(solution)/shard_map/ppermute | solution.py:12
  96.2 1.3 collective-permute-start.3
  97.5 0.6 iota_add_fusion.2
  98.1 0.0 collective-permute-done.1
  98.1 1.3 collective-permute-start.4
  99.4 0.7 iota_compare_fusion.3
  100.1 52.4 %collective-permute-done.3 = s32[1]{0:T(128)} collective-permute-done((s32[1]{0:T(128)}, s32[1]{0:T(128)}, u32[]{:S(2)}, u32[]{:S(2)}) %collective-permute-start.3) | collective-permute-done | bytes 36 | tf_op jit(solution)/shard_map/ppermute | solution.py:12
  152.5 1.3 collective-permute-start.6
  153.8 0.7 iota_add_fusion.1
  154.5 0.6 collective-permute-done.4
  155.1 1.3 collective-permute-start.7
  156.4 0.6 iota_compare_fusion.2
  157.0 1.3 collective-permute-done.6
  158.4 0.6 iota_add_fusion
  159.0 2.2 collective-permute-done.7
  161.2 0.7 iota_compare_fusion.1
  161.9 0.0 collective-permute-done.2
  161.9 2.3 fusion.1
  164.2 2.5 copy.22
  166.7 4.2 %reshape.116 = bf16[256,4096]{1,0:T(8,128)(2,1)} reshape(bf16[8192,128]{1,0:T(8,128)(2,1)} %copy.22) | data formatting | bytes 4194304 | tf_op jit(solution)/shard_map/reshape | solution.py:31
  170.9 0.0 collective-permute-done.5
  170.9 2.3 fusion.2
  173.2 2.5 copy.23
  175.7 4.3 %reshape.118 = bf16[256,4096]{1,0:T(8,128)(2,1)} reshape(bf16[8192,128]{1,0:T(8,128)(2,1)} %copy.23) | data formatting | bytes 4194304 | tf_op jit(solution)/shard_map/reshape | solution.py:31
  180.0 0.0 copy-done
  180.0 2.7 fusion.19
  182.8 0.0 copy-done.1
  182.8 0.1 copy-done.2
  182.9 1.0 fusion.22
  183.9 0.0 collective-permute-done.8
  183.9 2.3 fusion.3
  186.2 2.4 copy.24
  188.7 2.8 reshape.120
  191.5 2.6 fusion.25
  194.1 0.1 pad_maximum_fusion
  194.2 0.0 copy-start.3
  194.2 0.0 copy-start.4
  194.2 0.3 copy.25
  194.5 0.0 copy-start.6
  194.5 1.5 fusion.61
  196.0 0.0 all-reduce.3.cloned.1.call-update
  196.0 1.3 dynamic-slice
  197.9 62.1 %all-reduce.3.cloned.1.call-done = f32[4,256,256]{2,0,1:T(4,128)} async-done(((f32[4,256,256]{2,0,1:T(4,128)}), f32[4,256,256]{2,0,1:T(4,128)}) %all-reduce.3.cloned.1.call-update) | async-done | bytes 1048592
  260.1 0.0 copy-done.3
  260.1 1.3 fusion.29
  261.4 0.6 multiply_reduce_fusion.1
  262.0 1.4 pad_maximum_fusion.1
  263.3 99.0 %psum.7 = f32[2]{0:T(128)S(1)} all-reduce(f32[2]{0:T(128)S(1)} %pad_maximum_fusion.1), channel_id=1, replica_groups=mesh['aux'=4,'blk'=128] {'aux','blk'}, use_global_device_ids=true, to_apply=%region_5.6 | all-reduce | flops 2 | bytes 16 | tf_op jit(solution)/shard_map/psum | solution.py:65
  362.4 0.6 fusion.66
  363.0 1.0 fusion.30
  364.0 0.7 copy.28
  364.7 1.8 add_multiply_fusion
  (9 shorter events, 0.0 us)
Async XLA Ops:
  7.2 252.9 %all-reduce.3.cloned.1.call-start = ((), (), s32[]{:S(2)}) async-start(), calls=%async_computation | async-start | bytes 2097152
  7.2 154.7 %collective-permute-start.2 = (bf16[256,32,128]{2,1,0:T(8,128)(2,1)}, bf16[256,32,128]{2,1,0:T(8,128)(2,1)}, u32[]{:S(2)}, u32[]{:S(2)}) collective-permute-start(bf16[256,32,128]{2,1,0:T(8,128)(2,1)} %param.7), channel_id=1, source_target_pairs={{1,0},{2,1},{3,2},{4,3},{5,4},{6,5},{7,6},{8,7},{9,8},{10,9},{11,1... | collective-permute-start | bytes 6291464 | tf_op jit(solution)/shard_map/ppermute | solution.py:12
  16.0 154.9 %collective-permute-start.5 = (bf16[256,32,128]{2,1,0:T(8,128)(2,1)}, bf16[256,32,128]{2,1,0:T(8,128)(2,1)}, u32[]{:S(2)}, u32[]{:S(2)}) collective-permute-start(bf16[256,32,128]{2,1,0:T(8,128)(2,1)} %param.7), channel_id=1, source_target_pairs={{2,0},{3,1},{4,2},{5,3},{6,4},{7,5},{8,6},{9,7},{10,8},{11,9},{12,... | collective-permute-start | bytes 6291464 | tf_op jit(solution)/shard_map/ppermute | solution.py:12
  17.3 166.6 %collective-permute-start.8 = (bf16[256,32,128]{2,1,0:T(8,128)(2,1)}, bf16[256,32,128]{2,1,0:T(8,128)(2,1)}, u32[]{:S(2)}, u32[]{:S(2)}) collective-permute-start(bf16[256,32,128]{2,1,0:T(8,128)(2,1)} %param.7), channel_id=1, source_target_pairs={{3,0},{4,1},{5,2},{6,3},{7,4},{8,5},{9,6},{10,7},{11,8},{12,9},{13... | collective-permute-start | bytes 6291464 | tf_op jit(solution)/shard_map/ppermute | solution.py:12
  18.6 77.6 %collective-permute-start = (s32[1]{0:T(128)}, s32[1]{0:T(128)}, u32[]{:S(2)}, u32[]{:S(2)}) collective-permute-start(s32[1]{0:T(128)} %param.8), channel_id=1, source_target_pairs={{1,0},{2,1},{3,2},{4,3},{5,4},{6,5},{7,6},{8,7},{9,8},{10,9},{11,1... | collective-permute-start | bytes 20 | tf_op jit(solution)/shard_map/ppermute | solution.py:12
  20.5 77.6 %collective-permute-start.1 = (s32[1]{0:T(128)}, s32[1]{0:T(128)}, u32[]{:S(2)}, u32[]{:S(2)}) collective-permute-start(s32[1]{0:T(128)} %param.9), channel_id=1, source_target_pairs={{1,0},{2,1},{3,2},{4,3},{5,4},{6,5},{7,6},{8,7},{9,8},{10,9},{11,1... | collective-permute-start | bytes 20 | tf_op jit(solution)/shard_map/ppermute | solution.py:12
  30.7 2.4 copy-start.5
  96.2 56.3 %collective-permute-start.3 = (s32[1]{0:T(128)}, s32[1]{0:T(128)}, u32[]{:S(2)}, u32[]{:S(2)}) collective-permute-start(s32[1]{0:T(128)} %param.8), channel_id=1, source_target_pairs={{2,0},{3,1},{4,2},{5,3},{6,4},{7,5},{8,6},{9,7},{10,8},{11,9},{12,... | collective-permute-start | bytes 20 | tf_op jit(solution)/shard_map/ppermute | solution.py:12
  98.1 57.0 %collective-permute-start.4 = (s32[1]{0:T(128)}, s32[1]{0:T(128)}, u32[]{:S(2)}, u32[]{:S(2)}) collective-permute-start(s32[1]{0:T(128)} %param.9), channel_id=1, source_target_pairs={{2,0},{3,1},{4,2},{5,3},{6,4},{7,5},{8,6},{9,7},{10,8},{11,9},{12,... | collective-permute-start | bytes 20 | tf_op jit(solution)/shard_map/ppermute | solution.py:12
  152.5 5.8 %collective-permute-start.6 = (s32[1]{0:T(128)}, s32[1]{0:T(128)}, u32[]{:S(2)}, u32[]{:S(2)}) collective-permute-start(s32[1]{0:T(128)} %param.8), channel_id=1, source_target_pairs={{3,0},{4,1},{5,2},{6,3},{7,4},{8,5},{9,6},{10,7},{11,8},{12,9},{13... | collective-permute-start | bytes 20 | tf_op jit(solution)/shard_map/ppermute | solution.py:12
  155.1 6.1 %collective-permute-start.7 = (s32[1]{0:T(128)}, s32[1]{0:T(128)}, u32[]{:S(2)}, u32[]{:S(2)}) collective-permute-start(s32[1]{0:T(128)} %param.9), channel_id=1, source_target_pairs={{3,0},{4,1},{5,2},{6,3},{7,4},{8,5},{9,6},{10,7},{11,8},{12,9},{13... | collective-permute-start | bytes 20 | tf_op jit(solution)/shard_map/ppermute | solution.py:12
  175.7 4.3 %copy-start = (bf16[256,4096]{1,0:T(8,128)(2,1)S(1)}, bf16[256,4096]{1,0:T(8,128)(2,1)}, u32[]{:S(2)}) copy-start(bf16[256,4096]{1,0:T(8,128)(2,1)} %reshape.116) | copy-start | bytes 6291460
  180.0 2.8 copy-start.1
  180.0 2.9 copy-start.2
  194.2 65.9 %copy-start.3 = (bf16[1,4,64,256]{3,2,1,0:T(8,128)(2,1)S(1)}, bf16[1,4,64,256]{3,2,1,0:T(8,128)(2,1)}, u32[]{:S(2)}) copy-start(bf16[1,4,64,256]{3,2,1,0:T(8,128)(2,1)} %param.11) | copy-start | bytes 393220
  194.2 65.9 %copy-start.4 = (bf16[1,4,64,256]{3,2,1,0:T(8,128)(2,1)S(1)}, bf16[1,4,64,256]{3,2,1,0:T(8,128)(2,1)}, u32[]{:S(2)}) copy-start(bf16[1,4,64,256]{3,2,1,0:T(8,128)(2,1)} %param.12) | copy-start | bytes 393220
  194.5 170.2 %copy-start.6 = (f32[3]{0:T(128)S(1)}, f32[3]{0:T(128)}, u32[]{:S(2)}) copy-start(f32[3]{0:T(128)} %param.13) | copy-start | bytes 40
Sparse Core Ops, SparseCore 0:
  196.1 63.8 all-reduce.2
where the time goes:
time: 374 us; the launch traced here: 373 us
  waiting for transfers between devices  179 us (48%)
  blocking collectives  99 us (26%)
  local copies, waits for them, and re-layouts  28.3 us (8%)
  matrix products  21.7 us (6%)
  starting transfers between devices  20.4 us (5%)
  between operations  16.3 us (4%)
  other arithmetic  9.13 us (2%)
    ppermute x9, waiting for transfers between devices, from_behind(): lax.ppermute(value, axis, [(source, source + steps) for source in range(l...  116 us
    psum x1, blocking collectives, body(): totals = lax.psum(jnp.stack([first, second]), ('aux', 'blk'))  99 us
    unnamed x2, waiting for transfers between devices  62.1 us
    ppermute x9, starting transfers between devices, from_behind(): lax.ppermute(value, axis, [(source, source + steps) for source in range(l...  20.4 us
    reshape x4, local copies, waits for them, and re-layouts, pair_tile(): moved.reshape(rows, auxb * own_width)  13.6 us
    dot_general x4, matrix products, pair_tile(): jnp.dot(piece.reshape(rows * auxb, width), select.T, preferred_element_ty...  10.7 us
    convert_element_type x4, local copies, waits for them, and re-layouts, pair_tile(): moved = jnp.dot(piece.reshape(rows * auxb, width), select.T, preferred_el...  10.6 us
    dot_general x4, matrix products, pair_tile(): lax.dot_general(left, moved.reshape(rows, auxb * own_width), (((1,), (1,)...  9.51 us
  transfers between devices with their start and end apart: 10, of which 6 were waited for; matrix products, arithmetic and copies ran while one was open for 11% of the time, Pallas kernels for 0%

commit v1 on v0

v1 whole, which is shorter than its diff:
```python
import functools
import math

import jax
import jax.numpy as jnp
from jax import lax
from jax.experimental import pallas as pl
from jax.experimental.pallas import tpu as pltpu
from jax.sharding import PartitionSpec as P

VMEM = pltpu.VMEM
SMEM = pltpu.SMEM
NT = (((1,), (1,)), ((), ()))
LIMIT = 40 * 1024 * 1024


def spec(space):
    return pl.BlockSpec(memory_space=space)


def moved_by(value, axis, steps):
    count = lax.axis_size(axis)
    pairs = [(source, source + steps) for source in range(count) if 0 <= source + steps < count]
    return lax.ppermute(value, axis, pairs)


def align_kernel(chunk, auxb, start_ref, count_ref, row_ref, slab_ref, high_ref, low_ref, wide_ref, packed_ref, select_ref):
    groups = auxb // 4

    @pl.when(pl.program_id(0) == 0)
    def _():
        shift = start_ref[0] - 32 * row_ref[0, 0]
        lane = lax.broadcasted_iota(jnp.int32, (512, 640), 0)
        out = lax.broadcasted_iota(jnp.int32, (512, 640), 1)
        a = lane & 127
        place = ((out >> 7) << 5) + (out & 31)
        same = (lane >> 7) == ((out & 127) >> 5)
        hit = same & (a + shift == place) & (a < count_ref[0])
        select_ref[...] = jnp.where(hit, 1.0, 0.0).astype(jnp.bfloat16)

    wide_ref[...] = slab_ref[...].astype(jnp.float32).reshape(chunk * auxb, 128)
    for p in range(auxb):
        g, m = divmod(p, 4)
        rows = wide_ref[pl.ds(p, chunk, stride=auxb), :]
        packed_ref[g * chunk:(g + 1) * chunk, m * 128:(m + 1) * 128] = rows.astype(jnp.bfloat16)
    placed = jnp.dot(packed_ref[...], select_ref[...], preferred_element_type=jnp.float32).astype(jnp.bfloat16)
    for g in range(groups):
        part = placed[g * chunk:(g + 1) * chunk]
        for q in range(5):
            piece = part[:, q * 128:(q + 1) * 128]
            if q >= 1:
                high_ref[q - 1, :, g * 128:(g + 1) * 128] = piece
            if q <= 2:
                low_ref[q, :, g * 128:(g + 1) * 128] = piece


def align(slabs, start, count, row):
    rows, auxb, _ = slabs.shape
    chunk = 64
    depth = auxb * 32
    groups = auxb // 4
    return pl.pallas_call(
        functools.partial(align_kernel, chunk, auxb),
        grid=(rows // chunk,),
        in_specs=[
            spec(SMEM),
            spec(SMEM),
            spec(SMEM),
            pl.BlockSpec((chunk, auxb, 128), lambda n: (n, 0, 0)),
        ],
        out_specs=[
            pl.BlockSpec((4, chunk, depth), lambda n: (0, n, 0)),
            pl.BlockSpec((3, chunk, depth), lambda n: (0, n, 0)),
        ],
        out_shape=[
            jax.ShapeDtypeStruct((4, rows, depth), jnp.bfloat16),
            jax.ShapeDtypeStruct((3, rows, depth), jnp.bfloat16),
        ],
        scratch_shapes=[
            VMEM((chunk * auxb, 128), jnp.float32),
            VMEM((groups * chunk, 512), jnp.bfloat16),
            VMEM((512, 640), jnp.bfloat16),
        ],
        compiler_params=pltpu.CompilerParams(vmem_limit_bytes=LIMIT),
    )(start, count, row, slabs)


def by_offset_kernel(row_ref, density_ref, direction_ref, even_ref, odd_ref):
    block = row_ref[0, 0]
    for k in range(4):
        out = even_ref if k % 2 == 0 else odd_ref
        for which, source in enumerate((density_ref, direction_ref)):
            total = jnp.zeros(source.shape[2:], jnp.float32)
            for s in range(4):
                other = row_ref[0, s]
                full = 1.0 if s == 0 else 2.0
                weight = jnp.where((other >= 0) & (other - block == k), full, 0.0)
                total = total + weight * source[0, s].astype(jnp.float32)
            out[k // 2, which] = total.astype(jnp.bfloat16)


def by_offset(row, density, direction):
    shape = jax.ShapeDtypeStruct((2, 2) + density.shape[2:], jnp.bfloat16)
    return pl.pallas_call(
        by_offset_kernel,
        in_specs=[spec(SMEM), spec(VMEM), spec(VMEM)],
        out_specs=[spec(VMEM), spec(VMEM)],
        out_shape=[shape, shape],
    )(row, density, direction)


def product(left, right):
    total = None
    for a, b in zip(left, right):
        term = lax.dot_general(a, b, NT, preferred_element_type=jnp.float32)
        total = term if total is None else total + term
    return total


def tile_sums(tile, k, weights_ref):
    parts = []
    for which in range(2):
        total = jnp.zeros((8, 256), jnp.float32)
        for source in range(4):
            piece = weights_ref[source, k, which].astype(jnp.float32) * tile[source * 64:(source + 1) * 64]
            total = total + jnp.sum(piece.reshape(8, 8, 256), axis=0)
        parts.append(total)
    return parts


def near_kernel(high_ref, low_ref, before_ref, weights_ref, out_ref, sums_ref):
    own = [low_ref[0]] + [high_ref[q] for q in range(4)]
    t0 = product(own, own)
    t1 = product([before_ref[q] for q in range(4)], own[:4])
    sums = [jnp.zeros((8, 256), jnp.float32)] * 2
    for k, tile in enumerate((t0, t1)):
        sums = [a + b for a, b in zip(sums, tile_sums(tile, k, weights_ref))]
        for to in range(4):
            out_ref[to, k] = tile[to * 64:(to + 1) * 64].astype(jnp.bfloat16)
    for which in range(2):
        sums_ref[which] = sums[which]


def far_kernel(high_ref, before_ref, after_ref, weights_ref, sums_in_ref, out_ref):
    t2 = product([high_ref[q + 1] for q in range(3)], [after_ref[q] for q in range(3)])
    t3 = product([before_ref[q + 2] for q in range(2)], [after_ref[q] for q in range(2)])
    sums = [sums_in_ref[0], sums_in_ref[1]]
    for n, tile in enumerate((t2, t3)):
        sums = [a + b for a, b in zip(sums, tile_sums(tile, n + 2, weights_ref))]
        for to in range(4):
            out_ref[to, n * 64:(n + 1) * 64] = tile[to * 64:(to + 1) * 64].astype(jnp.bfloat16)
    lines = []
    for total in sums:
        value = jnp.broadcast_to(jnp.sum(total, keepdims=True), (8, 256))
        high = value.astype(jnp.bfloat16).astype(jnp.float32)
        rest = value - high
        middle = rest.astype(jnp.bfloat16).astype(jnp.float32)
        lines.append((high, middle, rest - middle))
    line = lax.broadcasted_iota(jnp.int32, (16, 256), 0)
    block = jnp.zeros((16, 256), jnp.float32)
    for which in range(2):
        for part in range(3):
            twice = jnp.concatenate([lines[which][part]] * 2, axis=0)
            block = jnp.where(line == which * 3 + part, twice, block)
    for to in range(4):
        out_ref[to, 128:144] = block.astype(jnp.bfloat16)


def near_sum_kernel(parts_ref, own_ref, before_ref):
    for k, out in enumerate((own_ref, before_ref)):
        total = parts_ref[0, k].astype(jnp.float32)
        for source in range(1, 4):
            total = total + parts_ref[source, k].astype(jnp.float32)
        out[...] = total.astype(jnp.bfloat16)


def far_sum_kernel(parts_ref, own_ref, before_ref, energy_ref):
    for n, out in enumerate((own_ref, before_ref)):
        total = parts_ref[0, n * 64:(n + 1) * 64].astype(jnp.float32)
        for source in range(1, 4):
            total = total + parts_ref[source, n * 64:(n + 1) * 64].astype(jnp.float32)
        out[...] = total.astype(jnp.bfloat16)
    extra = parts_ref[0, 128:144].astype(jnp.float32)
    for source in range(1, 4):
        extra = extra + parts_ref[source, 128:144].astype(jnp.float32)
    first = extra[0:1] + extra[1:2] + extra[2:3]
    second = extra[3:4] + extra[4:5] + extra[5:6]
    lane = lax.broadcasted_iota(jnp.int32, (1, 128), 1)
    both = jnp.where(lane < 64, first[:, :128], second[:, :128])
    count = energy_ref.shape[0]
    energy_ref[...] = jnp.broadcast_to(both[None], (count, 1, 128))


def finish_kernel(scale, row_ref, steps_ref, t0_ref, t1_ref, t2_ref, t3_ref, energy_ref, tiles_ref, out_ref):
    block = row_ref[0, 0]
    tiles = [t0_ref, t1_ref, t2_ref, t3_ref]
    for s in range(4):
        other = row_ref[0, s]
        total = jnp.zeros(t0_ref.shape, jnp.float32)
        for k in range(4):
            chosen = (other >= 0) & (other - block == k)
            total = jnp.where(chosen, tiles[k][...].astype(jnp.float32), total)
        tiles_ref[0, s] = total.astype(jnp.bfloat16)
    total = jnp.sum(energy_ref[...], axis=0)
    first = total[0, 0]
    second = total[0, 64]
    for n in range(3):
        out_ref[n] = -0.5 * (first + steps_ref[n] * second) * scale


def body(slabs, orbital_start, orbital_count, partners, density, direction, step_lengths):
    rows = slabs.shape[0]
    aux = lax.axis_size("aux")
    blocks = lax.axis_size("blk")
    slots = partners.shape[1]
    part = rows // aux
    bf16 = jnp.bfloat16
    params = pltpu.CompilerParams(vmem_limit_bytes=LIMIT)

    high, low = align(slabs, orbital_start, orbital_count, partners)
    after = moved_by(low, "blk", -2)
    before = moved_by(high, "blk", 1)
    even, odd = by_offset(partners, density, direction)
    odd = moved_by(odd, "blk", 1)
    weights = jnp.stack([even[0], odd[0], even[1], odd[1]])
    weights = jnp.broadcast_to(weights[None], (aux,) + weights.shape)
    weights = lax.all_to_all(weights, "aux", 0, 0, tiled=True)

    near, sums = pl.pallas_call(
        near_kernel,
        in_specs=[spec(VMEM)] * 4,
        out_specs=[spec(VMEM)] * 2,
        out_shape=[
            jax.ShapeDtypeStruct((aux, 2, part, rows), bf16),
            jax.ShapeDtypeStruct((2, 8, rows), jnp.float32),
        ],
        compiler_params=params,
    )(high, low, before, weights)
    near = lax.all_to_all(near, "aux", 0, 0, tiled=True)
    tile = jax.ShapeDtypeStruct((part, rows), bf16)
    t0, t1 = pl.pallas_call(
        near_sum_kernel, in_specs=[spec(VMEM)], out_specs=[spec(VMEM)] * 2, out_shape=[tile, tile]
    )(near)
    t1 = moved_by(t1, "blk", -1)

    far = pl.pallas_call(
        far_kernel,
        in_specs=[spec(VMEM)] * 5,
        out_specs=spec(VMEM),
        out_shape=jax.ShapeDtypeStruct((aux, 2 * part + 16, rows), bf16),
        compiler_params=params,
    )(high, before, after, weights, sums)
    far = lax.all_to_all(far, "aux", 0, 0, tiled=True)
    t2, t3, energy = pl.pallas_call(
        far_sum_kernel,
        in_specs=[spec(VMEM)],
        out_specs=[spec(VMEM)] * 3,
        out_shape=[tile, tile, jax.ShapeDtypeStruct((blocks, 1, 128), jnp.float32)],
    )(far)
    t3 = moved_by(t3, "blk", -1)
    energy = lax.all_to_all(energy, "blk", 0, 0, tiled=True)

    scale = 1.0 / (rows * math.sqrt(blocks * slots))
    return pl.pallas_call(
        functools.partial(finish_kernel, scale),
        in_specs=[spec(SMEM)] * 2 + [spec(VMEM)] * 5,
        out_specs=[spec(VMEM), spec(SMEM)],
        out_shape=[
            jax.ShapeDtypeStruct((1, slots, part, rows), bf16),
            jax.ShapeDtypeStruct((3,), jnp.float32),
        ],
    )(partners, step_lengths, t0, t1, t2, t3, energy)


def solution(mesh):
    return jax.shard_map(
        body,
        mesh=mesh,
        in_specs=(
            P("blk", "aux", None),
            P("blk"),
            P("blk"),
            P("blk", None),
            P("blk", None, "aux", None),
            P("blk", None, "aux", None),
            P(),
        ),
        out_specs=(P("blk", None, "aux", None), P()),
        check_vma=False,
    )
```

time: 374 us -> 118 us (0.32)
  waiting for transfers between devices: 179 us -> 21 us
  blocking collectives: 99 us -> 22.3 us
  starting transfers between devices: 20.4 us -> 47 us
  local copies, waits for them, and re-layouts: 28.3 us -> 3.87 us
  matrix products: 21.7 us -> 0 us
  Pallas kernels: 0 us -> 20.9 us
  between operations: 16.3 us -> 2.03 us
  other arithmetic: 9.13 us -> 0.04 us
    ppermute x9 -> x5, waiting for transfers between devices: 116 us -> 15.2 us  [moved_by(): return lax.ppermute(value, axis, pairs)]
    psum x1 -> x0, blocking collectives: 99 us -> none  [body(): totals = lax.psum(jnp.stack([first, second]), ('aux', 'blk'))]
    unnamed x2 -> x0, waiting for transfers between devices: 62.1 us -> none
    all_to_all x0 -> x2, starting transfers between devices: none -> 27.3 us  [the longest x1 23.9 us: body(): energy = lax.all_to_all(energy, 'blk', 0, 0, tiled=True)]
    all_to_all x0 -> x2, blocking collectives: none -> 22.3 us  [the longest x1 13.6 us: body(): weights = lax.all_to_all(weights, 'aux', 0, 0, tiled=True)]
    dot_general x9 -> x0, matrix products: 21.7 us -> none  [the longest x4 10.7 us: pair_tile(): jnp.dot(piece.reshape(rows * auxb, width), select.T, preferred_element_ty...]
    pallas_call x0 -> x7, Pallas kernels: none -> 20.9 us  [the longest x1 6.69 us: align(): pl.pallas_call(functools.partial(align_kernel, chunk, auxb), grid=(rows /...]
    reshape x4 -> x0, local copies, waits for them, and re-layouts: 13.6 us -> none  [pair_tile(): moved.reshape(rows, auxb * own_width)]
  transfers between devices with their start and end apart: 10 -> 7, of which waited for: 6 -> 5; matrix products, arithmetic and copies ran while one was open for 11% -> 1% of each run, Pallas kernels for 0% -> 8%
where the time goes in v1:
time: 118 us; the launch traced here: 117 us
  starting transfers between devices  47 us (40%)
  blocking collectives  22.3 us (19%)
  waiting for transfers between devices  21 us (18%)
  Pallas kernels  20.9 us (18%)
  local copies, waits for them, and re-layouts  3.87 us (3%)
  between operations  2.03 us (2%)
    all_to_all x1, starting transfers between devices, body(): energy = lax.all_to_all(energy, 'blk', 0, 0, tiled=True)  23.9 us
    ppermute x5, starting transfers between devices, moved_by(): return lax.ppermute(value, axis, pairs)  19.6 us
    ppermute x5, waiting for transfers between devices, moved_by(): return lax.ppermute(value, axis, pairs)  15.2 us
    all_to_all x1, blocking collectives, body(): weights = lax.all_to_all(weights, 'aux', 0, 0, tiled=True)  13.6 us
    all_to_all x1, blocking collectives, body(): far = lax.all_to_all(far, 'aux', 0, 0, tiled=True)  8.79 us
    pallas_call x1, Pallas kernels, align(): pl.pallas_call(functools.partial(align_kernel, chunk, auxb), grid=(rows /...  6.69 us
    all_to_all x1, waiting for transfers between devices, body(): near = lax.all_to_all(near, 'aux', 0, 0, tiled=True)  4.52 us
    pallas_call x1, Pallas kernels, body(): pl.pallas_call(near_kernel, in_specs=[spec(VMEM)] * 4, out_specs=[spec(VM...  4.25 us
  transfers between devices with their start and end apart: 7, of which 5 were waited for; matrix products, arithmetic and copies ran while one was open for 1% of the time, Pallas kernels for 8%

profile of v1, /device:TPU:1, one launch (start us, length us, event | category | flops | bytes accessed | tf_op | source)
XLA Modules:
  0.0 117.1 jit_solution(14671515203447242309)
XLA Ops:
  1.9 0.0 copy-start
  1.9 1.6 %copy-done = bf16[256,32,128]{2,1,0:T(8,128)(2,1)S(1)} copy-done((bf16[256,32,128]{2,1,0:T(8,128)(2,1)S(1)}, bf16[256,32,128]{2,1,0:T(8,128)(2,1)}, u32[]{:S(2)}) %copy-start) | copy-done | bytes 2097176
  3.5 0.0 copy-start.1
  3.5 0.7 copy-done.1
  4.2 6.7 %shard_map.86 = (bf16[4,256,1024]{2,1,0:T(8,128)(2,1)S(1)}, bf16[3,256,1024]{2,1,0:T(8,128)(2,1)}) custom-call(s32[1]{0:T(128)S(6)} %copy.9.start_ref, s32[1]{0:T(128)S(6)} %copy.10.count_ref, s32[1,4]{1,0:T(1,128)S(1)} %copy-done.1, bf16[256,32,128]{2,1,0:T(8,128)(2,1)S(1)} %copy-done), custom_call_target="tpu_custom_call" | custom-call | tf_op jit(solution)/shard_map/pallas_call | solution.py:62
  10.9 4.6 %collective-permute-start = (bf16[4,256,1024]{2,1,0:T(8,128)(2,1)S(1)}, bf16[4,256,1024]{2,1,0:T(8,128)(2,1)}, u32[]{:S(2)}, u32[]{:S(2)}) collective-permute-start(bf16[4,256,1024]{2,1,0:T(8,128)(2,1)S(1)} %get-tuple-element.13.high_ref), channel_id=1, source_target_pairs={{0,1},{1,2},{2,3},{3,4},{4,5},{5,6},{6,7},{7,8},{8,9},{9,10},{10,1... | collective-permute-start | bytes 6291464 | tf_op jit(solution)/shard_map/ppermute | solution.py:24
  15.4 1.3 %collective-permute-start.3 = (bf16[3,256,1024]{2,1,0:T(8,128)(2,1)}, bf16[3,256,1024]{2,1,0:T(8,128)(2,1)}, u32[]{:S(2)}, u32[]{:S(2)}) collective-permute-start(bf16[3,256,1024]{2,1,0:T(8,128)(2,1)} %get-tuple-element.14.low_ref), channel_id=1, source_target_pairs={{2,0},{3,1},{4,2},{5,3},{6,4},{7,5},{8,6},{9,7},{10,8},{11,9},{12,... | collective-permute-start | bytes 4718600 | tf_op jit(solution)/shard_map/ppermute | solution.py:24
  16.7 1.8 %shard_map.87 = (bf16[2,2,64,256]{3,2,1,0:T(8,128)(2,1)}, bf16[2,2,64,256]{3,2,1,0:T(8,128)(2,1)}) custom-call(s32[1,4]{1,0:T(1,128)} %row_ref.5, bf16[1,4,64,256]{3,2,1,0:T(8,128)(2,1)} %density_ref.1, bf16[1,4,64,256]{3,2,1,0:T(8,128)(2,1)} %direction_ref.1), custom_call_target="tpu_custom_call" | custom-call | tf_op jit(solution)/shard_map/pallas_call | solution.py:104
  18.6 9.0 %collective-permute-start.1 = (bf16[2,2,64,256]{3,2,1,0:T(8,128)(2,1)}, bf16[2,2,64,256]{3,2,1,0:T(8,128)(2,1)S(1)}, u32[]{:S(2)}, u32[]{:S(2)}) collective-permute-start(bf16[2,2,64,256]{3,2,1,0:T(8,128)(2,1)} %get-tuple-element.16), channel_id=1, source_target_pairs={{0,1},{1,2},{2,3},{3,4},{4,5},{5,6},{6,7},{7,8},{8,9},{9,10},{10,1... | collective-permute-start | bytes 393224 | tf_op jit(solution)/shard_map/ppermute | solution.py:24
  27.6 0.9 fusion
  28.5 11.4 %collective-permute-done.1 = bf16[2,2,64,256]{3,2,1,0:T(8,128)(2,1)S(1)} collective-permute-done((bf16[2,2,64,256]{3,2,1,0:T(8,128)(2,1)}, bf16[2,2,64,256]{3,2,1,0:T(8,128)(2,1)S(1)}, u32[]{:S(2)}, u32[]{:S(2)}) %collective-permute-start.1) | collective-permute-done | bytes 131104 | tf_op jit(solution)/shard_map/ppermute | solution.py:24
  40.0 0.1 broadcast_in_dim.2
  40.1 13.6 %all_to_all.20.weights_ref = bf16[4,4,2,64,256]{4,3,2,1,0:T(8,128)(2,1)S(1)} all-to-all(bf16[4,4,2,64,256]{4,3,2,1,0:T(8,128)(2,1)S(1)} %broadcast_in_dim.2), channel_id=1, replica_groups=mesh['aux'=4,'blk'=128] {'aux'}, dimensions={0} | all-to-all | bytes 2097152 | tf_op jit(solution)/shard_map/all_to_all | solution.py:227
  53.6 0.0 collective-permute-done.before_ref
  53.6 4.2 %shard_map.88 = (bf16[4,2,64,256]{3,2,1,0:T(8,128)(2,1)}, f32[2,8,256]{2,1,0:T(8,128)S(1)}) custom-call(bf16[4,256,1024]{2,1,0:T(8,128)(2,1)S(1)} %get-tuple-element.13.high_ref, bf16[3,256,1024]{2,1,0:T(8,128)(2,1)} %get-tuple-element.14.low_ref, bf16[4,256,1024]{2,1,0:T(8,128)(2,1)} %collective-permute-done.before_ref, ...), custom_call_target="tpu_custom_call" | custom-call | tf_op jit(solution)/shard_map/pallas_call | solution.py:229
  57.9 0.0 collective-permute-done.3.after_ref
  57.9 3.1 %shard_map.90 = bf16[4,144,256]{2,1,0:T(8,128)(2,1)S(1)} custom-call(bf16[4,256,1024]{2,1,0:T(8,128)(2,1)S(1)} %get-tuple-element.13.high_ref, bf16[4,256,1024]{2,1,0:T(8,128)(2,1)} %collective-permute-done.before_ref, bf16[3,256,1024]{2,1,0:T(8,128)(2,1)} %collective-permute-done.3.after_ref, bf16[4,4,2,64,256]{4,3,2,1,0:T(8,128)(2,1)S(1)} %all_to_all.20.weights_ref, ...), custom_call_target="tpu_custom_call" | custom-call | tf_op jit(solution)/shard_map/pallas_call | solution.py:246
  61.0 8.8 %all_to_all.21.parts_ref = bf16[4,144,256]{2,1,0:T(8,128)(2,1)} all-to-all(bf16[4,144,256]{2,1,0:T(8,128)(2,1)S(1)} %shard_map.90), channel_id=1, replica_groups=mesh['aux'=4,'blk'=128] {'aux'}, dimensions={0} | all-to-all | bytes 589824 | tf_op jit(solution)/shard_map/all_to_all | solution.py:253
  69.8 3.4 %all-to-all-start.1 = ((bf16[4,2,64,256]{3,2,1,0:T(8,128)(2,1)}), bf16[4,2,64,256]{3,2,1,0:T(8,128)(2,1)S(1)}, u32[]{:S(2)}, u32[]{:S(2)}) async-start(bf16[4,2,64,256]{3,2,1,0:T(8,128)(2,1)} %get-tuple-element.17), calls=%async_computation.1 | async-start | bytes 524288 | tf_op jit(solution)/shard_map/all_to_all | solution.py:239
  73.2 1.7 %shard_map.91 = (bf16[64,256]{1,0:T(8,128)(2,1)}, bf16[64,256]{1,0:T(8,128)(2,1)}, f32[128,1,128]{2,1,0:T(1,128)}) custom-call(bf16[4,144,256]{2,1,0:T(8,128)(2,1)} %all_to_all.21.parts_ref), custom_call_target="tpu_custom_call" | custom-call | tf_op jit(solution)/shard_map/pallas_call | solution.py:254
  74.9 4.5 %all-to-all-done.1.parts_ref = bf16[4,2,64,256]{3,2,1,0:T(8,128)(2,1)S(1)} async-done(((bf16[4,2,64,256]{3,2,1,0:T(8,128)(2,1)}), bf16[4,2,64,256]{3,2,1,0:T(8,128)(2,1)S(1)}, u32[]{:S(2)}, u32[]{:S(2)}) %all-to-all-start.1) | async-done | bytes 262176 | tf_op jit(solution)/shard_map/all_to_all | solution.py:239
  79.4 0.0 copy-start.2
  79.4 23.9 %all-to-all-start.3 = ((f32[128,1,128]{2,1,0:T(1,128)}), f32[128,1,128]{2,1,0:T(1,128)S(1)}, u32[]{:S(2)}, u32[]{:S(2)}) async-start(f32[128,1,128]{2,1,0:T(1,128)} %get-tuple-element.23), calls=%async_computation.3 | async-start | bytes 131072 | tf_op jit(solution)/shard_map/all_to_all | solution.py:261
  103.3 0.0 copy-done.2
  103.3 1.6 %shard_map.89 = (bf16[64,256]{1,0:T(8,128)(2,1)}, bf16[64,256]{1,0:T(8,128)(2,1)}) custom-call(bf16[4,2,64,256]{3,2,1,0:T(8,128)(2,1)} %copy-done.2), custom_call_target="tpu_custom_call" | custom-call | tf_op jit(solution)/shard_map/pallas_call | solution.py:241
  104.9 2.8 %collective-permute-start.2 = (bf16[64,256]{1,0:T(8,128)(2,1)}, bf16[64,256]{1,0:T(8,128)(2,1)S(1)}, u32[]{:S(2)}, u32[]{:S(2)}) collective-permute-start(bf16[64,256]{1,0:T(8,128)(2,1)} %get-tuple-element.19), channel_id=1, source_target_pairs={{1,0},{2,1},{3,2},{4,3},{5,4},{6,5},{7,6},{8,7},{9,8},{10,9},{11,1... | collective-permute-start | bytes 98312 | tf_op jit(solution)/shard_map/ppermute | solution.py:24
  107.7 1.9 %collective-permute-start.4 = (bf16[64,256]{1,0:T(8,128)(2,1)}, bf16[64,256]{1,0:T(8,128)(2,1)S(1)}, u32[]{:S(2)}, u32[]{:S(2)}) collective-permute-start(bf16[64,256]{1,0:T(8,128)(2,1)} %get-tuple-element.22), channel_id=1, source_target_pairs={{1,0},{2,1},{3,2},{4,3},{5,4},{6,5},{7,6},{8,7},{9,8},{10,9},{11,1... | collective-permute-start | bytes 98312 | tf_op jit(solution)/shard_map/ppermute | solution.py:24
  109.7 1.0 collective-permute-done.2.t1_ref
  110.7 0.0 copy-start.4
  110.7 2.8 %collective-permute-done.4.t3_ref = bf16[64,256]{1,0:T(8,128)(2,1)S(1)} collective-permute-done((bf16[64,256]{1,0:T(8,128)(2,1)}, bf16[64,256]{1,0:T(8,128)(2,1)S(1)}, u32[]{:S(2)}, u32[]{:S(2)}) %collective-permute-start.4) | collective-permute-done | bytes 32800 | tf_op jit(solution)/shard_map/ppermute | solution.py:24
  113.5 0.0 copy-start.5
  113.5 1.2 %all-to-all-done.3.energy_ref = f32[128,1,128]{2,1,0:T(1,128)S(1)} async-done(((f32[128,1,128]{2,1,0:T(1,128)}), f32[128,1,128]{2,1,0:T(1,128)S(1)}, u32[]{:S(2)}, u32[]{:S(2)}) %all-to-all-start.3) | async-done | bytes 65568 | tf_op jit(solution)/shard_map/all_to_all | solution.py:261
  114.7 0.0 copy-start.3
  114.7 0.0 copy-done.4
  114.7 0.0 copy-done.5
  114.7 0.6 copy-done.3
  115.3 1.8 %shard_map.92 = (bf16[1,4,64,256]{3,2,1,0:T(8,128)(2,1)}, f32[3]{0:T(128)}) custom-call(s32[1,4]{1,0:T(1,128)} %row_ref.5, f32[3]{0:T(128)} %steps_ref.1, bf16[64,256]{1,0:T(8,128)(2,1)} %get-tuple-element.18.t0_ref, bf16[64,256]{1,0:T(8,128)(2,1)} %copy-done.4, bf16[64,256]{1,0:T(8,128)(2,1)} %get-tuple-element.21.t2_ref, bf16[64,256]{1,0:T(8,128)(2,1)} %copy-done.5, ...), custom_call_target="tpu_custom_call" | custom-call | tf_op jit(solution)/shard_map/pallas_call | solution.py:264
  (2 shorter events, 0.0 us)
Async XLA Ops:
  1.9 1.6 %copy-start = (bf16[256,32,128]{2,1,0:T(8,128)(2,1)S(1)}, bf16[256,32,128]{2,1,0:T(8,128)(2,1)}, u32[]{:S(2)}) copy-start(bf16[256,32,128]{2,1,0:T(8,128)(2,1)} %slab_ref.1) | copy-start | bytes 6291460
  3.5 0.7 copy-start.1
  10.9 42.8 %collective-permute-start = (bf16[4,256,1024]{2,1,0:T(8,128)(2,1)S(1)}, bf16[4,256,1024]{2,1,0:T(8,128)(2,1)}, u32[]{:S(2)}, u32[]{:S(2)}) collective-permute-start(bf16[4,256,1024]{2,1,0:T(8,128)(2,1)S(1)} %get-tuple-element.13.high_ref), channel_id=1, source_target_pairs={{0,1},{1,2},{2,3},{3,4},{4,5},{5,6},{6,7},{7,8},{8,9},{9,10},{10,1... | collective-permute-start | bytes 6291464 | tf_op jit(solution)/shard_map/ppermute | solution.py:24
  15.4 42.5 %collective-permute-start.3 = (bf16[3,256,1024]{2,1,0:T(8,128)(2,1)}, bf16[3,256,1024]{2,1,0:T(8,128)(2,1)}, u32[]{:S(2)}, u32[]{:S(2)}) collective-permute-start(bf16[3,256,1024]{2,1,0:T(8,128)(2,1)} %get-tuple-element.14.low_ref), channel_id=1, source_target_pairs={{2,0},{3,1},{4,2},{5,3},{6,4},{7,5},{8,6},{9,7},{10,8},{11,9},{12,... | collective-permute-start | bytes 4718600 | tf_op jit(solution)/shard_map/ppermute | solution.py:24
  18.6 21.3 %collective-permute-start.1 = (bf16[2,2,64,256]{3,2,1,0:T(8,128)(2,1)}, bf16[2,2,64,256]{3,2,1,0:T(8,128)(2,1)S(1)}, u32[]{:S(2)}, u32[]{:S(2)}) collective-permute-start(bf16[2,2,64,256]{3,2,1,0:T(8,128)(2,1)} %get-tuple-element.16), channel_id=1, source_target_pairs={{0,1},{1,2},{2,3},{3,4},{4,5},{5,6},{6,7},{7,8},{8,9},{9,10},{10,1... | collective-permute-start | bytes 393224 | tf_op jit(solution)/shard_map/ppermute | solution.py:24
  69.8 9.6 %all-to-all-start.1 = ((bf16[4,2,64,256]{3,2,1,0:T(8,128)(2,1)}), bf16[4,2,64,256]{3,2,1,0:T(8,128)(2,1)S(1)}, u32[]{:S(2)}, u32[]{:S(2)}) async-start(bf16[4,2,64,256]{3,2,1,0:T(8,128)(2,1)} %get-tuple-element.17), calls=%async_computation.1 | async-start | bytes 524288 | tf_op jit(solution)/shard_map/all_to_all | solution.py:239
  79.4 23.9 %copy-start.2 = (bf16[4,2,64,256]{3,2,1,0:T(8,128)(2,1)}, bf16[4,2,64,256]{3,2,1,0:T(8,128)(2,1)S(1)}, u32[]{:S(2)}) copy-start(bf16[4,2,64,256]{3,2,1,0:T(8,128)(2,1)S(1)} %all-to-all-done.1.parts_ref) | copy-start | bytes 786436
  79.4 35.3 %all-to-all-start.3 = ((f32[128,1,128]{2,1,0:T(1,128)}), f32[128,1,128]{2,1,0:T(1,128)S(1)}, u32[]{:S(2)}, u32[]{:S(2)}) async-start(f32[128,1,128]{2,1,0:T(1,128)} %get-tuple-element.23), calls=%async_computation.3 | async-start | bytes 131072 | tf_op jit(solution)/shard_map/all_to_all | solution.py:261
  104.9 5.7 %collective-permute-start.2 = (bf16[64,256]{1,0:T(8,128)(2,1)}, bf16[64,256]{1,0:T(8,128)(2,1)S(1)}, u32[]{:S(2)}, u32[]{:S(2)}) collective-permute-start(bf16[64,256]{1,0:T(8,128)(2,1)} %get-tuple-element.19), channel_id=1, source_target_pairs={{1,0},{2,1},{3,2},{4,3},{5,4},{6,5},{7,6},{8,7},{9,8},{10,9},{11,1... | collective-permute-start | bytes 98312 | tf_op jit(solution)/shard_map/ppermute | solution.py:24
  107.7 5.7 %collective-permute-start.4 = (bf16[64,256]{1,0:T(8,128)(2,1)}, bf16[64,256]{1,0:T(8,128)(2,1)S(1)}, u32[]{:S(2)}, u32[]{:S(2)}) collective-permute-start(bf16[64,256]{1,0:T(8,128)(2,1)} %get-tuple-element.22), channel_id=1, source_target_pairs={{1,0},{2,1},{3,2},{4,3},{5,4},{6,5},{7,6},{8,7},{9,8},{10,9},{11,1... | collective-permute-start | bytes 98312 | tf_op jit(solution)/shard_map/ppermute | solution.py:24
  110.7 4.1 %copy-start.4 = (bf16[64,256]{1,0:T(8,128)(2,1)}, bf16[64,256]{1,0:T(8,128)(2,1)S(1)}, u32[]{:S(2)}) copy-start(bf16[64,256]{1,0:T(8,128)(2,1)S(1)} %collective-permute-done.2.t1_ref) | copy-start | bytes 98308
  113.5 1.3 %copy-start.5 = (bf16[64,256]{1,0:T(8,128)(2,1)}, bf16[64,256]{1,0:T(8,128)(2,1)S(1)}, u32[]{:S(2)}) copy-start(bf16[64,256]{1,0:T(8,128)(2,1)S(1)} %collective-permute-done.4.t3_ref) | copy-start | bytes 98308
  114.7 0.6 copy-start.3

commit v2 on v0

v2 whole, which is shorter than its diff:
```python
import functools
import math

import jax
import jax.numpy as jnp
from jax import lax
from jax.experimental import pallas as pl
from jax.experimental.pallas import tpu as pltpu
from jax.sharding import PartitionSpec as P

VMEM = pltpu.VMEM
SMEM = pltpu.SMEM
NT = (((1,), (1,)), ((), ()))
MIB = 1024 * 1024


def spec(space):
    return pl.BlockSpec(memory_space=space)


def moved_by(value, axis, steps):
    count = lax.axis_size(axis)
    pairs = [(source, source + steps) for source in range(count) if 0 <= source + steps < count]
    return lax.ppermute(value, axis, pairs)


def by_offset(row_ref, tiles_ref, even_ref, odd_ref):
    block = row_ref[0, 0]
    for k in range(4):
        out = even_ref if k % 2 == 0 else odd_ref
        for which in range(2):
            total = jnp.zeros(tiles_ref.shape[2:], jnp.float32)
            for s in range(4):
                other = row_ref[0, s]
                full = 1.0 if s == 0 else 2.0
                weight = jnp.where((other >= 0) & (other - block == k), full, 0.0)
                total = total + weight * tiles_ref[which, s].astype(jnp.float32)
            out[k // 2 * 2 + which] = total.astype(jnp.bfloat16)


def align_kernel(
    chunk,
    start_hbm,
    count_hbm,
    row_hbm,
    slab_hbm,
    density_hbm,
    direction_hbm,
    high_hbm,
    low_hbm,
    even_hbm,
    odd_hbm,
    start_ref,
    count_ref,
    row_ref,
    slab_ref,
    select_ref,
    high_ref,
    low_ref,
    tiles_ref,
    even_ref,
    odd_ref,
    small_sem,
    in_sem,
    out_sem,
    tile_sem,
):
    steps, _, auxb, _ = slab_ref.shape
    bf16 = jnp.bfloat16
    small = [
        pltpu.make_async_copy(source, target, small_sem.at[n])
        for n, (source, target) in enumerate(((start_hbm, start_ref), (count_hbm, count_ref), (row_hbm, row_ref)))
    ]
    loads = [
        pltpu.make_async_copy(slab_hbm.at[pl.ds(n * chunk, chunk)], slab_ref.at[n], in_sem.at[n]) for n in range(steps)
    ]
    tiles = [
        pltpu.make_async_copy(source.at[0], tiles_ref.at[n], tile_sem.at[n])
        for n, source in enumerate((density_hbm, direction_hbm))
    ]
    for copy in small + loads + tiles:
        copy.start()
    for copy in small:
        copy.wait()
    shift = start_ref[0] - 32 * row_ref[0, 0]
    count = count_ref[0]
    a = lax.broadcasted_iota(jnp.int32, (128, 256), 0)
    to = lax.broadcasted_iota(jnp.int32, (128, 256), 1)
    hit = (a < count) & (((a + shift) & 127) == ((to >> 6) << 5) + (to & 31))
    for m in range(2):
        select_ref[m * 128:(m + 1) * 128] = jnp.where(hit & (((to >> 5) & 1) == m), 1.0, 0.0).astype(bf16)
    first = (lax.broadcasted_iota(jnp.int32, (chunk, 128), 1) & 31) >= shift
    zero = jnp.zeros((chunk, 128), bf16)
    stores = []
    for n in range(steps):
        loads[n].wait()
        by_function = jnp.swapaxes(slab_ref[n], 0, 1)
        rows = slice(n * chunk, (n + 1) * chunk)
        for g in range(auxb // 4):
            parts = []
            for p in (4 * g, 4 * g + 2):
                pair = jnp.concatenate([by_function[p], by_function[p + 1]], axis=1)
                parts.append(jnp.dot(pair, select_ref[...], preferred_element_type=jnp.float32).astype(bf16))
            lanes = slice(g * 128, (g + 1) * 128)
            for q in range(4):
                piece = jnp.concatenate([part[:, q * 64:(q + 1) * 64] for part in parts], axis=1)
                if q == 0:
                    low_ref[0, rows, lanes] = jnp.where(first, piece, zero)
                    high_ref[3, rows, lanes] = jnp.where(first, zero, piece)
                    continue
                high_ref[q - 1, rows, lanes] = piece
                if q <= 2:
                    low_ref[q, rows, lanes] = piece
        for m, (source, target) in enumerate(((low_ref, low_hbm), (high_ref, high_hbm))):
            part = pl.ds(n * chunk, chunk)
            copy = pltpu.make_async_copy(source.at[:, part], target.at[:, part], out_sem.at[n, m])
            copy.start()
            stores.append(copy)
    for copy in tiles:
        copy.wait()
    by_offset(row_ref, tiles_ref, even_ref, odd_ref)
    targets = [even_hbm] + [odd_hbm.at[to] for to in range(4)]
    for n, target in enumerate(targets):
        copy = pltpu.make_async_copy(odd_ref if n else even_ref, target, tile_sem.at[2 + n])
        copy.start()
        stores.append(copy)
    for copy in stores:
        copy.wait()


def align(slabs, start, count, row, density, direction):
    rows, auxb, _ = slabs.shape
    chunk = 128
    steps = rows // chunk
    depth = auxb * 32
    high = (4, rows, depth)
    low = (3, rows, depth)
    tiles = (4,) + density.shape[2:]
    bf16 = jnp.bfloat16
    dma = pltpu.SemaphoreType.DMA
    return pl.pallas_call(
        functools.partial(align_kernel, chunk),
        in_specs=[spec(pl.ANY)] * 6,
        out_specs=[spec(pl.ANY)] * 4,
        out_shape=[jax.ShapeDtypeStruct(shape, bf16) for shape in (high, low, tiles, (4,) + tiles)],
        scratch_shapes=[
            SMEM((1,), jnp.int32),
            SMEM((1,), jnp.int32),
            SMEM(row.shape, jnp.int32),
            VMEM((steps, chunk, auxb, 128), bf16),
            VMEM((256, 256), bf16),
            VMEM(high, bf16),
            VMEM(low, bf16),
            VMEM((2,) + density.shape[1:], bf16),
            VMEM(tiles, bf16),
            VMEM(tiles, bf16),
            dma((3,)),
            dma((steps,)),
            dma((steps, 2)),
            dma((7,)),
        ],
        compiler_params=pltpu.CompilerParams(vmem_limit_bytes=60 * MIB),
    )(start, count, row, slabs, density, direction)


def product(left, right):
    total = None
    for a, b in zip(left, right):
        term = lax.dot_general(a, b, NT, preferred_element_type=jnp.float32)
        total = term if total is None else total + term
    return total


def tile_sums(tile, place, weights_ref):
    parts = []
    for which in range(2):
        total = jnp.zeros((8, 256), jnp.float32)
        for source in range(4):
            weight = weights_ref[source, place * 2 + which].astype(jnp.float32)
            piece = weight * tile[source * 64:(source + 1) * 64]
            total = total + jnp.sum(piece.reshape(8, 8, 256), axis=0)
        parts.append(total)
    return parts


def own_kernel(high_ref, low_ref, even_ref, tile_ref, out_ref):
    own = [low_ref[0]] + [high_ref[q] for q in range(4)]
    tile = product(own, own)
    tile_ref[...] = tile
    for to in range(4):
        out_ref[to, 0:4] = even_ref[...]
        out_ref[to, 4] = tile[to * 64:(to + 1) * 64].astype(jnp.bfloat16)


def near_kernel(high_ref, low_ref, before_ref, tile_ref, even_ref, out_ref, own_ref, sums_ref):
    own = [low_ref[0]] + [high_ref[q] for q in range(3)]
    out_ref[...] = product([before_ref[q] for q in range(4)], own)
    sums = tile_sums(tile_ref, 0, even_ref)
    for which in range(2):
        sums_ref[which] = sums[which]
    total = even_ref[0, 4].astype(jnp.float32)
    for source in range(1, 4):
        total = total + even_ref[source, 4].astype(jnp.float32)
    own_ref[...] = total.astype(jnp.bfloat16)


def far_kernel(high_ref, before_ref, after_ref, even_ref, odd_ref, near_ref, sums_in_ref, out_ref):
    t2 = product([high_ref[q + 1] for q in range(3)], [after_ref[q] for q in range(3)])
    t3 = product([before_ref[q + 2] for q in range(2)], [after_ref[q] for q in range(2)])
    sums = [sums_in_ref[0], sums_in_ref[1]]
    for tile, place, weights_ref in ((near_ref, 0, odd_ref), (t2, 1, even_ref), (t3, 1, odd_ref)):
        sums = [a + b for a, b in zip(sums, tile_sums(tile, place, weights_ref))]
    for to in range(4):
        part = slice(to * 64, (to + 1) * 64)
        for n, tile in enumerate((near_ref[part], t3[part], t2[part])):
            out_ref[to, n * 64:(n + 1) * 64] = tile.astype(jnp.bfloat16)
    lines = []
    for total in sums:
        value = jnp.broadcast_to(jnp.sum(total, keepdims=True), (8, 256))
        high = value.astype(jnp.bfloat16).astype(jnp.float32)
        rest = value - high
        middle = rest.astype(jnp.bfloat16).astype(jnp.float32)
        lines.append((high, middle, rest - middle))
    line = lax.broadcasted_iota(jnp.int32, (16, 256), 0)
    block = jnp.zeros((16, 256), jnp.float32)
    for which in range(2):
        for part in range(3):
            twice = jnp.concatenate([lines[which][part]] * 2, axis=0)
            block = jnp.where(line == which * 3 + part, twice, block)
    for to in range(4):
        out_ref[to, 192:208] = block.astype(jnp.bfloat16)


def sum_kernel(parts_ref, before_ref, own_ref, energy_ref):
    for n in range(3):
        rows = slice(n * 64, (n + 1) * 64)
        total = parts_ref[0, rows].astype(jnp.float32)
        for source in range(1, 4):
            total = total + parts_ref[source, rows].astype(jnp.float32)
        if n < 2:
            before_ref[n] = total.astype(jnp.bfloat16)
        else:
            own_ref[...] = total.astype(jnp.bfloat16)
    extra = parts_ref[0, 192:208].astype(jnp.float32)
    for source in range(1, 4):
        extra = extra + parts_ref[source, 192:208].astype(jnp.float32)
    first = extra[0:1] + extra[1:2] + extra[2:3]
    second = extra[3:4] + extra[4:5] + extra[5:6]
    lane = lax.broadcasted_iota(jnp.int32, (1, 128), 1)
    both = jnp.where(lane < 64, first[:, :128], second[:, :128])
    energy_ref[...] = jnp.broadcast_to(both[None], energy_ref.shape)


def energy_kernel(scale, steps_ref, energy_ref, out_ref):
    total = jnp.sum(energy_ref[...], axis=0)
    first = total[0, 0]
    second = total[0, 64]
    for n in range(3):
        out_ref[n] = -0.5 * (first + steps_ref[n] * second) * scale


def slot_kernel(row_ref, t0_ref, t2_ref, odd_ref, tiles_ref):
    block = row_ref[0, 0]
    tiles = [t0_ref[...], odd_ref[0], t2_ref[...], odd_ref[1]]
    for s in range(4):
        other = row_ref[0, s]
        total = jnp.zeros(t0_ref.shape, jnp.float32)
        for k in range(4):
            chosen = (other >= 0) & (other - block == k)
            total = jnp.where(chosen, tiles[k].astype(jnp.float32), total)
        tiles_ref[0, s] = total.astype(jnp.bfloat16)


def kernel_call(kernel, in_specs, out_shape, limit=16, out_specs=None):
    return pl.pallas_call(
        kernel,
        in_specs=in_specs,
        out_specs=out_specs or [spec(VMEM)] * len(out_shape),
        out_shape=out_shape,
        compiler_params=pltpu.CompilerParams(vmem_limit_bytes=limit * MIB),
    )


def body(slabs, orbital_start, orbital_count, partners, density, direction, step_lengths):
    rows = slabs.shape[0]
    aux = lax.axis_size("aux")
    blocks = lax.axis_size("blk")
    slots = partners.shape[1]
    part = rows // aux

    def half(*shape):
        return jax.ShapeDtypeStruct(shape, jnp.bfloat16)

    def single(*shape):
        return jax.ShapeDtypeStruct(shape, jnp.float32)

    high, low, even, odd = align(slabs, orbital_start, orbital_count, partners, density, direction)
    after = moved_by(low, "blk", -2)
    before = moved_by(high, "blk", 1)
    odd = lax.all_to_all(odd, "aux", 0, 0, tiled=True)
    odd = moved_by(odd, "blk", 1)

    t0, even = kernel_call(own_kernel, [spec(VMEM)] * 3, [single(rows, rows), half(aux, 5, part, rows)])(
        high, low, even
    )
    even = lax.all_to_all(even, "aux", 0, 0, tiled=True)
    t1, t0, sums = kernel_call(
        near_kernel, [spec(VMEM)] * 5, [single(rows, rows), half(part, rows), single(2, 8, rows)]
    )(high, low, before, t0, even)
    (far,) = kernel_call(far_kernel, [spec(VMEM)] * 7, [half(aux, 3 * part + 16, rows)])(
        high, before, after, even, odd, t1, sums
    )
    far = lax.all_to_all(far, "aux", 0, 0, tiled=True)
    odd, t2, energy = kernel_call(
        sum_kernel, [spec(VMEM)], [half(2, part, rows), half(part, rows), single(blocks, 1, 128)]
    )(far)
    odd = moved_by(odd, "blk", -1)
    energy = lax.all_to_all(energy, "blk", 0, 0, tiled=True)

    scale = 1.0 / (rows * math.sqrt(blocks * slots))
    (energies,) = kernel_call(
        functools.partial(energy_kernel, scale),
        [spec(SMEM), spec(VMEM)],
        [single(3)],
        out_specs=[spec(SMEM)],
    )(step_lengths, energy)
    t2, energies = lax.optimization_barrier((t2, energies))
    (tiles,) = kernel_call(
        slot_kernel, [spec(SMEM)] + [spec(VMEM)] * 3, [half(1, slots, part, rows)]
    )(partners, t0, t2, odd)
    return tiles, energies


def solution(mesh):
    return jax.shard_map(
        body,
        mesh=mesh,
        in_specs=(
            P("blk", "aux", None),
            P("blk"),
            P("blk"),
            P("blk", None),
            P("blk", None, "aux", None),
            P("blk", None, "aux", None),
            P(),
        ),
        out_specs=(P("blk", None, "aux", None), P()),
        check_vma=False,
    )
```

time: 374 us -> 94.9 us (0.25)
  waiting for transfers between devices: 179 us -> 8.58 us
  blocking collectives: 99 us -> 34 us
  local copies, waits for them, and re-layouts: 28.3 us -> 3.91 us
  matrix products: 21.7 us -> 0 us
  starting transfers between devices: 20.4 us -> 35.3 us
  between operations: 16.3 us -> 2.06 us
  Pallas kernels: 0 us -> 10.6 us
  other arithmetic: 9.13 us -> 0 us
    ppermute x9 -> x4, waiting for transfers between devices: 116 us -> 0.01 us  [moved_by(): return lax.ppermute(value, axis, pairs)]
    psum x1 -> x0, blocking collectives: 99 us -> none  [body(): totals = lax.psum(jnp.stack([first, second]), ('aux', 'blk'))]
    unnamed x2 -> x0, waiting for transfers between devices: 62.1 us -> none
    all_to_all x0 -> x3, blocking collectives: none -> 34 us  [the longest x1 11.9 us: body(): far = lax.all_to_all(far, 'aux', 0, 0, tiled=True)]
    dot_general x9 -> x0, matrix products: 21.7 us -> none  [the longest x4 10.7 us: pair_tile(): jnp.dot(piece.reshape(rows * auxb, width), select.T, preferred_element_ty...]
    all_to_all x0 -> x1, starting transfers between devices: none -> 18.2 us  [body(): energy = lax.all_to_all(energy, 'blk', 0, 0, tiled=True)]
    reshape x4 -> x0, local copies, waits for them, and re-layouts: 13.6 us -> none  [pair_tile(): moved.reshape(rows, auxb * own_width)]
    convert_element_type x4 -> x0, local copies, waits for them, and re-layouts: 10.6 us -> none  [pair_tile(): moved = jnp.dot(piece.reshape(rows * auxb, width), select.T, preferred_el...]
  transfers between devices with their start and end apart: 10 -> 5, of which waited for: 6 -> 1; matrix products, arithmetic and copies ran while one was open for 11% -> 0% of each run, Pallas kernels for 0% -> 3%
where the time goes in v2:
time: 94.9 us; the launch traced here: 94.4 us
  starting transfers between devices  35.3 us (37%)
  blocking collectives  34 us (36%)
  Pallas kernels  10.6 us (11%)
  waiting for transfers between devices  8.58 us (9%)
  local copies, waits for them, and re-layouts  3.91 us (4%)
  between operations  2.06 us (2%)
    all_to_all x1, starting transfers between devices, body(): energy = lax.all_to_all(energy, 'blk', 0, 0, tiled=True)  18.2 us
    ppermute x4, starting transfers between devices, moved_by(): return lax.ppermute(value, axis, pairs)  17.1 us
    all_to_all x1, blocking collectives, body(): far = lax.all_to_all(far, 'aux', 0, 0, tiled=True)  11.9 us
    all_to_all x1, blocking collectives, body(): even = lax.all_to_all(even, 'aux', 0, 0, tiled=True)  11.2 us
    all_to_all x1, blocking collectives, body(): odd = lax.all_to_all(odd, 'aux', 0, 0, tiled=True)  11 us
    all_to_all x1, waiting for transfers between devices, body(): energy = lax.all_to_all(energy, 'blk', 0, 0, tiled=True)  8.57 us
    pallas_call x1, Pallas kernels, align(): pl.pallas_call(functools.partial(align_kernel, chunk), in_specs=[spec(pl....  4.62 us
    unnamed x10, local copies, waits for them, and re-layouts  3.91 us
  transfers between devices with their start and end apart: 5, of which 1 were waited for; matrix products, arithmetic and copies ran while one was open for 0% of the time, Pallas kernels for 3%

profile of v2, /device:TPU:1, one launch (start us, length us, event | category | flops | bytes accessed | tf_op | source)
XLA Modules:
  0.0 94.4 jit_solution(2937632061412336146)
XLA Ops:
  1.9 4.6 %shard_map.86 = (bf16[4,256,1024]{2,1,0:T(8,128)(2,1)}, bf16[3,256,1024]{2,1,0:T(8,128)(2,1)}, bf16[4,64,256]{2,1,0:T(8,128)(2,1)}, bf16[4,4,64,256]{3,2,1,0:T(8,128)(2,1)}) custom-call(s32[1]{0:T(128)S(6)} %copy.9.start_hbm, s32[1]{0:T(128)S(6)} %copy.10.count_hbm, s32[1,4]{1,0:T(1,128)} %row_ref.1, bf16[256,32,128]{2,1,0:T(8,128)(2,1)} %slab_hbm.1, ...), custom_call_target="tpu_custom_call" | custom-call | tf_op jit(solution)/shard_map/pallas_call | solution.py:141
  6.5 4.6 %collective-permute-start = (bf16[4,256,1024]{2,1,0:T(8,128)(2,1)}, bf16[4,256,1024]{2,1,0:T(8,128)(2,1)S(1)}, u32[]{:S(2)}, u32[]{:S(2)}) collective-permute-start(bf16[4,256,1024]{2,1,0:T(8,128)(2,1)} %get-tuple-element.16.high_ref), channel_id=1, source_target_pairs={{0,1},{1,2},{2,3},{3,4},{4,5},{5,6},{6,7},{7,8},{8,9},{9,10},{10,1... | collective-permute-start | bytes 6291464 | tf_op jit(solution)/shard_map/ppermute | solution.py:24
  11.1 1.3 %collective-permute-start.1 = (bf16[3,256,1024]{2,1,0:T(8,128)(2,1)}, bf16[3,256,1024]{2,1,0:T(8,128)(2,1)S(1)}, u32[]{:S(2)}, u32[]{:S(2)}) collective-permute-start(bf16[3,256,1024]{2,1,0:T(8,128)(2,1)} %get-tuple-element.17.low_ref), channel_id=1, source_target_pairs={{2,0},{3,1},{4,2},{5,3},{6,4},{7,5},{8,6},{9,7},{10,8},{11,9},{12,... | collective-permute-start | bytes 4718600 | tf_op jit(solution)/shard_map/ppermute | solution.py:24
  12.4 11.0 %all_to_all.20 = bf16[4,4,64,256]{3,2,1,0:T(8,128)(2,1)S(1)} all-to-all(bf16[4,4,64,256]{3,2,1,0:T(8,128)(2,1)} %get-tuple-element.22), channel_id=1, replica_groups=mesh['aux'=4,'blk'=128] {'aux'}, dimensions={0} | all-to-all | bytes 1048576 | tf_op jit(solution)/shard_map/all_to_all | solution.py:300
  23.4 8.4 %collective-permute-start.2 = (bf16[4,4,64,256]{3,2,1,0:T(8,128)(2,1)S(1)}, bf16[4,4,64,256]{3,2,1,0:T(8,128)(2,1)S(1)}, u32[]{:S(2)}, u32[]{:S(2)}) collective-permute-start(bf16[4,4,64,256]{3,2,1,0:T(8,128)(2,1)S(1)} %all_to_all.20), channel_id=1, source_target_pairs={{0,1},{1,2},{2,3},{3,4},{4,5},{5,6},{6,7},{7,8},{8,9},{9,10},{10,1... | collective-permute-start | bytes 1572872 | tf_op jit(solution)/shard_map/ppermute | solution.py:24
  31.8 0.0 copy-start
  31.8 1.6 %copy-done = bf16[4,256,1024]{2,1,0:T(8,128)(2,1)S(1)} copy-done((bf16[4,256,1024]{2,1,0:T(8,128)(2,1)S(1)}, bf16[4,256,1024]{2,1,0:T(8,128)(2,1)}, u32[]{:S(2)}) %copy-start) | copy-done | bytes 2097176
  33.4 0.0 copy-start.1
  33.4 1.4 %copy-done.1 = bf16[3,256,1024]{2,1,0:T(8,128)(2,1)S(1)} copy-done((bf16[3,256,1024]{2,1,0:T(8,128)(2,1)S(1)}, bf16[3,256,1024]{2,1,0:T(8,128)(2,1)}, u32[]{:S(2)}) %copy-start.1) | copy-done | bytes 1572888
  34.8 0.0 copy-start.2
  34.8 0.9 copy-done.2
  35.7 0.9 shard_map.87
  36.6 11.2 %all_to_all.21.even_ref = bf16[4,5,64,256]{3,2,1,0:T(8,128)(2,1)S(1)} all-to-all(bf16[4,5,64,256]{3,2,1,0:T(8,128)(2,1)S(1)} %get-tuple-element.20), channel_id=1, replica_groups=mesh['aux'=4,'blk'=128] {'aux'}, dimensions={0} | all-to-all | bytes 1310720 | tf_op jit(solution)/shard_map/all_to_all | solution.py:306
  47.8 0.0 collective-permute-done.before_ref
  47.8 0.7 shard_map.88
  48.5 0.0 collective-permute-done.2.odd_ref
  48.6 0.0 collective-permute-done.1.after_ref
  48.6 0.0 copy-start.4
  48.6 0.0 copy-start.3
  48.6 1.1 %shard_map.89 = bf16[4,208,256]{2,1,0:T(8,128)(2,1)S(1)} custom-call(bf16[4,256,1024]{2,1,0:T(8,128)(2,1)S(1)} %copy-done, bf16[4,256,1024]{2,1,0:T(8,128)(2,1)S(1)} %collective-permute-done.before_ref, bf16[3,256,1024]{2,1,0:T(8,128)(2,1)S(1)} %collective-permute-done.1.after_ref, bf16[4,5,64,256]{3,2,1,0:T(8,128)(2,1)S(1)} %all_to_all.21.even_ref, ...), custom_call_target="tpu_custom_call" | custom-call | tf_op jit(solution)/shard_map/pallas_call | solution.py:310
  49.7 11.9 %all_to_all.22.parts_ref = bf16[4,208,256]{2,1,0:T(8,128)(2,1)S(1)} all-to-all(bf16[4,208,256]{2,1,0:T(8,128)(2,1)S(1)} %shard_map.89), channel_id=1, replica_groups=mesh['aux'=4,'blk'=128] {'aux'}, dimensions={0} | all-to-all | bytes 851968 | tf_op jit(solution)/shard_map/all_to_all | solution.py:313
  61.6 0.7 shard_map.90
  62.3 18.2 %all-to-all-start.3 = ((f32[128,1,128]{2,1,0:T(1,128)}), f32[128,1,128]{2,1,0:T(1,128)S(1)}, u32[]{:S(2)}, u32[]{:S(2)}) async-start(f32[128,1,128]{2,1,0:T(1,128)} %get-tuple-element.26), calls=%async_computation.3 | async-start | bytes 131072 | tf_op jit(solution)/shard_map/all_to_all | solution.py:318
  80.5 2.8 %collective-permute-start.3 = (bf16[2,64,256]{2,1,0:T(8,128)(2,1)S(1)}, bf16[2,64,256]{2,1,0:T(8,128)(2,1)S(1)}, u32[]{:S(2)}, u32[]{:S(2)}) collective-permute-start(bf16[2,64,256]{2,1,0:T(8,128)(2,1)S(1)} %get-tuple-element.28), channel_id=1, source_target_pairs={{1,0},{2,1},{3,2},{4,3},{5,4},{6,5},{7,6},{8,7},{9,8},{10,9},{11,1... | collective-permute-start | bytes 196616 | tf_op jit(solution)/shard_map/ppermute | solution.py:24
  83.3 8.6 %all-to-all-done.3.energy_ref = f32[128,1,128]{2,1,0:T(1,128)S(1)} async-done(((f32[128,1,128]{2,1,0:T(1,128)}), f32[128,1,128]{2,1,0:T(1,128)S(1)}, u32[]{:S(2)}, u32[]{:S(2)}) %all-to-all-start.3) | async-done | bytes 65568 | tf_op jit(solution)/shard_map/all_to_all | solution.py:318
  91.9 0.0 copy-done.4
  91.9 1.3 %shard_map.91 = f32[3]{0:T(128)} custom-call(f32[3]{0:T(128)S(1)} %copy-done.4, f32[128,1,128]{2,1,0:T(1,128)S(1)} %all-to-all-done.3.energy_ref), custom_call_target="tpu_custom_call" | custom-call | tf_op jit(solution)/shard_map/pallas_call | solution.py:321
  93.2 0.0 collective-permute-done.3.odd_ref
  93.2 0.0 copy-done.3
  93.2 1.2 %shard_map.92 = bf16[1,4,64,256]{3,2,1,0:T(8,128)(2,1)} custom-call(s32[1,4]{1,0:T(1,128)S(1)} %copy-done.3, bf16[64,256]{1,0:T(8,128)(2,1)S(1)} %get-tuple-element.21.t0_ref, bf16[64,256]{1,0:T(8,128)(2,1)S(1)} %get-tuple-element.27.t2_ref, bf16[2,64,256]{2,1,0:T(8,128)(2,1)S(1)} %collective-permute-done.3.odd_ref), custom_call_target="tpu_custom_call" | custom-call | tf_op jit(solution)/shard_map/pallas_call | solution.py:328
Async XLA Ops:
  6.5 41.3 %collective-permute-start = (bf16[4,256,1024]{2,1,0:T(8,128)(2,1)}, bf16[4,256,1024]{2,1,0:T(8,128)(2,1)S(1)}, u32[]{:S(2)}, u32[]{:S(2)}) collective-permute-start(bf16[4,256,1024]{2,1,0:T(8,128)(2,1)} %get-tuple-element.16.high_ref), channel_id=1, source_target_pairs={{0,1},{1,2},{2,3},{3,4},{4,5},{5,6},{6,7},{7,8},{8,9},{9,10},{10,1... | collective-permute-start | bytes 6291464 | tf_op jit(solution)/shard_map/ppermute | solution.py:24
  11.1 37.4 %collective-permute-start.1 = (bf16[3,256,1024]{2,1,0:T(8,128)(2,1)}, bf16[3,256,1024]{2,1,0:T(8,128)(2,1)S(1)}, u32[]{:S(2)}, u32[]{:S(2)}) collective-permute-start(bf16[3,256,1024]{2,1,0:T(8,128)(2,1)} %get-tuple-element.17.low_ref), channel_id=1, source_target_pairs={{2,0},{3,1},{4,2},{5,3},{6,4},{7,5},{8,6},{9,7},{10,8},{11,9},{12,... | collective-permute-start | bytes 4718600 | tf_op jit(solution)/shard_map/ppermute | solution.py:24
  23.4 25.1 %collective-permute-start.2 = (bf16[4,4,64,256]{3,2,1,0:T(8,128)(2,1)S(1)}, bf16[4,4,64,256]{3,2,1,0:T(8,128)(2,1)S(1)}, u32[]{:S(2)}, u32[]{:S(2)}) collective-permute-start(bf16[4,4,64,256]{3,2,1,0:T(8,128)(2,1)S(1)} %all_to_all.20), channel_id=1, source_target_pairs={{0,1},{1,2},{2,3},{3,4},{4,5},{5,6},{6,7},{7,8},{8,9},{9,10},{10,1... | collective-permute-start | bytes 1572872 | tf_op jit(solution)/shard_map/ppermute | solution.py:24
  31.8 1.6 %copy-start = (bf16[4,256,1024]{2,1,0:T(8,128)(2,1)S(1)}, bf16[4,256,1024]{2,1,0:T(8,128)(2,1)}, u32[]{:S(2)}) copy-start(bf16[4,256,1024]{2,1,0:T(8,128)(2,1)} %get-tuple-element.16.high_ref) | copy-start | bytes 6291460
  33.4 1.4 %copy-start.1 = (bf16[3,256,1024]{2,1,0:T(8,128)(2,1)S(1)}, bf16[3,256,1024]{2,1,0:T(8,128)(2,1)}, u32[]{:S(2)}) copy-start(bf16[3,256,1024]{2,1,0:T(8,128)(2,1)} %get-tuple-element.17.low_ref) | copy-start | bytes 4718596
  34.8 0.9 copy-start.2
  48.6 43.3 %copy-start.4 = (f32[3]{0:T(128)S(1)}, f32[3]{0:T(128)}, u32[]{:S(2)}) copy-start(f32[3]{0:T(128)} %steps_ref.1) | copy-start | bytes 40
  48.6 44.6 %copy-start.3 = (s32[1,4]{1,0:T(1,128)S(1)}, s32[1,4]{1,0:T(1,128)}, u32[]{:S(2)}) copy-start(s32[1,4]{1,0:T(1,128)} %row_ref.1) | copy-start | bytes 52
  62.3 29.6 %all-to-all-start.3 = ((f32[128,1,128]{2,1,0:T(1,128)}), f32[128,1,128]{2,1,0:T(1,128)S(1)}, u32[]{:S(2)}, u32[]{:S(2)}) async-start(f32[128,1,128]{2,1,0:T(1,128)} %get-tuple-element.26), calls=%async_computation.3 | async-start | bytes 131072 | tf_op jit(solution)/shard_map/all_to_all | solution.py:318
  80.5 12.7 %collective-permute-start.3 = (bf16[2,64,256]{2,1,0:T(8,128)(2,1)S(1)}, bf16[2,64,256]{2,1,0:T(8,128)(2,1)S(1)}, u32[]{:S(2)}, u32[]{:S(2)}) collective-permute-start(bf16[2,64,256]{2,1,0:T(8,128)(2,1)S(1)} %get-tuple-element.28), channel_id=1, source_target_pairs={{1,0},{2,1},{3,2},{4,3},{5,4},{6,5},{7,6},{8,7},{9,8},{10,9},{11,1... | collective-permute-start | bytes 196616 | tf_op jit(solution)/shard_map/ppermute | solution.py:24

commit v3 on v2

--- a/solution.py
+++ b/solution.py
@@ -12,6 +12,7 @@
 SMEM = pltpu.SMEM
 NT = (((1,), (1,)), ((), ()))
 MIB = 1024 * 1024
+CHUNKS = (64, 128, 64)
 
 
 def spec(space):
@@ -39,7 +40,7 @@
 
 
 def align_kernel(
-    chunk,
+    chunks,
     start_hbm,
     count_hbm,
     row_hbm,
@@ -65,14 +66,16 @@
     out_sem,
     tile_sem,
 ):
-    steps, _, auxb, _ = slab_ref.shape
+    _, auxb, _ = slab_ref.shape
+    begins = [sum(chunks[:n]) for n in range(len(chunks))]
     bf16 = jnp.bfloat16
     small = [
         pltpu.make_async_copy(source, target, small_sem.at[n])
         for n, (source, target) in enumerate(((start_hbm, start_ref), (count_hbm, count_ref), (row_hbm, row_ref)))
     ]
     loads = [
-        pltpu.make_async_copy(slab_hbm.at[pl.ds(n * chunk, chunk)], slab_ref.at[n], in_sem.at[n]) for n in range(steps)
+        pltpu.make_async_copy(slab_hbm.at[pl.ds(begin, chunk)], slab_ref.at[pl.ds(begin, chunk)], in_sem.at[n])
+        for n, (begin, chunk) in enumerate(zip(begins, chunks))
     ]
     tiles = [
         pltpu.make_async_copy(source.at[0], tiles_ref.at[n], tile_sem.at[n])
@@ -82,25 +85,25 @@
         copy.start()
     for copy in small:
         copy.wait()
-    shift = start_ref[0] - 32 * row_ref[0, 0]
-    count = count_ref[0]
+    shift = start_ref[0, 0] - 32 * row_ref[0, 0]
+    count = count_ref[0, 0]
     a = lax.broadcasted_iota(jnp.int32, (128, 256), 0)
     to = lax.broadcasted_iota(jnp.int32, (128, 256), 1)
     hit = (a < count) & (((a + shift) & 127) == ((to >> 6) << 5) + (to & 31))
     for m in range(2):
         select_ref[m * 128:(m + 1) * 128] = jnp.where(hit & (((to >> 5) & 1) == m), 1.0, 0.0).astype(bf16)
-    first = (lax.broadcasted_iota(jnp.int32, (chunk, 128), 1) & 31) >= shift
-    zero = jnp.zeros((chunk, 128), bf16)
     stores = []
-    for n in range(steps):
+    for n, (begin, chunk) in enumerate(zip(begins, chunks)):
+        first = (lax.broadcasted_iota(jnp.int32, (chunk, 128), 1) & 31) >= shift
+        zero = jnp.zeros((chunk, 128), bf16)
         loads[n].wait()
-        by_function = jnp.swapaxes(slab_ref[n], 0, 1)
-        rows = slice(n * chunk, (n + 1) * chunk)
+        rows = slice(begin, begin + chunk)
+        by_function = jnp.swapaxes(slab_ref[rows], 0, 1)
+        pairs = [jnp.concatenate([by_function[p], by_function[p + 1]], axis=1) for p in range(0, auxb, 2)]
+        placed = jnp.dot(jnp.concatenate(pairs, axis=0), select_ref[...], preferred_element_type=jnp.float32)
+        placed = placed.astype(bf16)
         for g in range(auxb // 4):
-            parts = []
-            for p in (4 * g, 4 * g + 2):
-                pair = jnp.concatenate([by_function[p], by_function[p + 1]], axis=1)
-                parts.append(jnp.dot(pair, select_ref[...], preferred_element_type=jnp.float32).astype(bf16))
+            parts = [placed[h * chunk:(h + 1) * chunk] for h in (2 * g, 2 * g + 1)]
             lanes = slice(g * 128, (g + 1) * 128)
             for q in range(4):
                 piece = jnp.concatenate([part[:, q * 64:(q + 1) * 64] for part in parts], axis=1)
@@ -111,8 +114,8 @@
                 high_ref[q - 1, rows, lanes] = piece
                 if q <= 2:
                     low_ref[q, rows, lanes] = piece
+        part = pl.ds(begin, chunk)
         for m, (source, target) in enumerate(((low_ref, low_hbm), (high_ref, high_hbm))):
-            part = pl.ds(n * chunk, chunk)
             copy = pltpu.make_async_copy(source.at[:, part], target.at[:, part], out_sem.at[n, m])
             copy.start()
             stores.append(copy)
@@ -130,8 +133,7 @@
 
 def align(slabs, start, count, row, density, direction):
     rows, auxb, _ = slabs.shape
-    chunk = 128
-    steps = rows // chunk
+    steps = len(CHUNKS)
     depth = auxb * 32
     high = (4, rows, depth)
     low = (3, rows, depth)
@@ -139,15 +141,15 @@
     bf16 = jnp.bfloat16
     dma = pltpu.SemaphoreType.DMA
     return pl.pallas_call(
-        functools.partial(align_kernel, chunk),
+        functools.partial(align_kernel, CHUNKS),
         in_specs=[spec(pl.ANY)] * 6,
         out_specs=[spec(pl.ANY)] * 4,
         out_shape=[jax.ShapeDtypeStruct(shape, bf16) for shape in (high, low, tiles, (4,) + tiles)],
         scratch_shapes=[
-            SMEM((1,), jnp.int32),
-            SMEM((1,), jnp.int32),
+            SMEM((1, 1), jnp.int32),
+            SMEM((1, 1), jnp.int32),
             SMEM(row.shape, jnp.int32),
-            VMEM((steps, chunk, auxb, 128), bf16),
+            VMEM(slabs.shape, bf16),
             VMEM((256, 256), bf16),
             VMEM(high, bf16),
             VMEM(low, bf16),
@@ -160,7 +162,7 @@
             dma((7,)),
         ],
         compiler_params=pltpu.CompilerParams(vmem_limit_bytes=60 * MIB),
-    )(start, count, row, slabs, density, direction)
+    )(start[None], count[None], row, slabs, density, direction)
 
 
 def product(left, right):
@@ -251,15 +253,7 @@
     energy_ref[...] = jnp.broadcast_to(both[None], energy_ref.shape)
 
 
-def energy_kernel(scale, steps_ref, energy_ref, out_ref):
-    total = jnp.sum(energy_ref[...], axis=0)
-    first = total[0, 0]
-    second = total[0, 64]
-    for n in range(3):
-        out_ref[n] = -0.5 * (first + steps_ref[n] * second) * scale
-
-
-def slot_kernel(row_ref, t0_ref, t2_ref, odd_ref, tiles_ref):
+def finish_kernel(scale, row_ref, steps_ref, t0_ref, t2_ref, odd_ref, energy_ref, tiles_ref, out_ref):
     block = row_ref[0, 0]
     tiles = [t0_ref[...], odd_ref[0], t2_ref[...], odd_ref[1]]
     for s in range(4):
@@ -269,6 +263,11 @@
             chosen = (other >= 0) & (other - block == k)
             total = jnp.where(chosen, tiles[k].astype(jnp.float32), total)
         tiles_ref[0, s] = total.astype(jnp.bfloat16)
+    total = jnp.sum(energy_ref[...], axis=0)
+    first = total[0, 0]
+    second = total[0, 64]
+    for n in range(3):
+        out_ref[n] = -0.5 * (first + steps_ref[n] * second) * scale
 
 
 def kernel_call(kernel, in_specs, out_shape, limit=16, out_specs=None):
@@ -318,17 +317,12 @@
     energy = lax.all_to_all(energy, "blk", 0, 0, tiled=True)
 
     scale = 1.0 / (rows * math.sqrt(blocks * slots))
-    (energies,) = kernel_call(
-        functools.partial(energy_kernel, scale),
-        [spec(SMEM), spec(VMEM)],
-        [single(3)],
-        out_specs=[spec(SMEM)],
-    )(step_lengths, energy)
-    t2, energies = lax.optimization_barrier((t2, energies))
-    (tiles,) = kernel_call(
-        slot_kernel, [spec(SMEM)] + [spec(VMEM)] * 3, [half(1, slots, part, rows)]
-    )(partners, t0, t2, odd)
-    return tiles, energies
+    return kernel_call(
+        functools.partial(finish_kernel, scale),
+        [spec(SMEM)] * 2 + [spec(VMEM)] * 4,
+        [half(1, slots, part, rows), single(3)],
+        out_specs=[spec(VMEM), spec(SMEM)],
+    )(partners, step_lengths, t0, t2, odd, energy)
 
 
 def solution(mesh):

time: 94.9 us -> 93.4 us (0.984)
  Pallas kernels: 10.6 us -> 9.09 us
    all_to_all x1, waiting for transfers between devices: 8.57 us -> 5.5 us  [body(): energy = lax.all_to_all(energy, 'blk', 0, 0, tiled=True)]
    ppermute x4, waiting for transfers between devices: 0.01 us -> 3.08 us  [moved_by(): return lax.ppermute(value, axis, pairs)]
    pallas_call x3 -> x2, Pallas kernels: 7.16 us -> 5.68 us  [the longest x1 4.29 us: align(): pl.pallas_call(functools.partial(align_kernel, CHUNKS), in_specs=[spec(pl...]
  transfers between devices with their start and end apart: 5 -> 5, of which waited for: 1 -> 2; matrix products, arithmetic and copies ran while one was open for 0% -> 0% of each run, Pallas kernels for 3% -> 2%
where the time goes in v3:
time: 93.4 us; the launch traced here: 92.9 us
  starting transfers between devices  35.3 us (38%)
  blocking collectives  34 us (36%)
  Pallas kernels  9.09 us (10%)
  waiting for transfers between devices  8.58 us (9%)
  local copies, waits for them, and re-layouts  3.91 us (4%)
  between operations  2.03 us (2%)
    all_to_all x1, starting transfers between devices, body(): energy = lax.all_to_all(energy, 'blk', 0, 0, tiled=True)  18.2 us
    ppermute x4, starting transfers between devices, moved_by(): return lax.ppermute(value, axis, pairs)  17.1 us
    all_to_all x1, blocking collectives, body(): far = lax.all_to_all(far, 'aux', 0, 0, tiled=True)  11.9 us
    all_to_all x1, blocking collectives, body(): even = lax.all_to_all(even, 'aux', 0, 0, tiled=True)  11.2 us
    all_to_all x1, blocking collectives, body(): odd = lax.all_to_all(odd, 'aux', 0, 0, tiled=True)  11 us
    all_to_all x1, waiting for transfers between devices, body(): energy = lax.all_to_all(energy, 'blk', 0, 0, tiled=True)  5.5 us
    pallas_call x1, Pallas kernels, align(): pl.pallas_call(functools.partial(align_kernel, CHUNKS), in_specs=[spec(pl...  4.29 us
    unnamed x10, local copies, waits for them, and re-layouts  3.91 us
  transfers between devices with their start and end apart: 5, of which 2 were waited for; matrix products, arithmetic and copies ran while one was open for 0% of the time, Pallas kernels for 2%

profile of v3, /device:TPU:1, one launch (start us, length us, event | category | flops | bytes accessed | tf_op | source)
XLA Modules:
  0.0 92.9 jit_solution(11713845977383792564)
XLA Ops:
  1.9 4.3 %shard_map.86 = (bf16[4,256,1024]{2,1,0:T(8,128)(2,1)}, bf16[3,256,1024]{2,1,0:T(8,128)(2,1)}, bf16[4,64,256]{2,1,0:T(8,128)(2,1)}, bf16[4,4,64,256]{3,2,1,0:T(8,128)(2,1)}) custom-call(s32[1,1]{1,0:T(1,128)} %bitcast.2.start_hbm, s32[1,1]{1,0:T(1,128)} %bitcast.3.count_hbm, s32[1,4]{1,0:T(1,128)} %row_ref.1, bf16[256,32,128]{2,1,0:T(8,128)(2,1)} %slab_hbm.1, ...), custom_call_target="tpu_custom_call" | custom-call | tf_op jit(solution)/shard_map/pallas_call | solution.py:143
  6.2 4.6 %collective-permute-start = (bf16[4,256,1024]{2,1,0:T(8,128)(2,1)}, bf16[4,256,1024]{2,1,0:T(8,128)(2,1)S(1)}, u32[]{:S(2)}, u32[]{:S(2)}) collective-permute-start(bf16[4,256,1024]{2,1,0:T(8,128)(2,1)} %get-tuple-element.14.high_ref), channel_id=1, source_target_pairs={{0,1},{1,2},{2,3},{3,4},{4,5},{5,6},{6,7},{7,8},{8,9},{9,10},{10,1... | collective-permute-start | bytes 6291464 | tf_op jit(solution)/shard_map/ppermute | solution.py:25
  10.8 1.3 %collective-permute-start.1 = (bf16[3,256,1024]{2,1,0:T(8,128)(2,1)}, bf16[3,256,1024]{2,1,0:T(8,128)(2,1)S(1)}, u32[]{:S(2)}, u32[]{:S(2)}) collective-permute-start(bf16[3,256,1024]{2,1,0:T(8,128)(2,1)} %get-tuple-element.15.low_ref), channel_id=1, source_target_pairs={{2,0},{3,1},{4,2},{5,3},{6,4},{7,5},{8,6},{9,7},{10,8},{11,9},{12,... | collective-permute-start | bytes 4718600 | tf_op jit(solution)/shard_map/ppermute | solution.py:25
  12.1 11.0 %all_to_all.20 = bf16[4,4,64,256]{3,2,1,0:T(8,128)(2,1)S(1)} all-to-all(bf16[4,4,64,256]{3,2,1,0:T(8,128)(2,1)} %get-tuple-element.20), channel_id=1, replica_groups=mesh['aux'=4,'blk'=128] {'aux'}, dimensions={0} | all-to-all | bytes 1048576 | tf_op jit(solution)/shard_map/all_to_all | solution.py:299
  23.1 8.4 %collective-permute-start.2 = (bf16[4,4,64,256]{3,2,1,0:T(8,128)(2,1)S(1)}, bf16[4,4,64,256]{3,2,1,0:T(8,128)(2,1)S(1)}, u32[]{:S(2)}, u32[]{:S(2)}) collective-permute-start(bf16[4,4,64,256]{3,2,1,0:T(8,128)(2,1)S(1)} %all_to_all.20), channel_id=1, source_target_pairs={{0,1},{1,2},{2,3},{3,4},{4,5},{5,6},{6,7},{7,8},{8,9},{9,10},{10,1... | collective-permute-start | bytes 1572872 | tf_op jit(solution)/shard_map/ppermute | solution.py:25
  31.5 0.0 copy-start
  31.5 1.6 %copy-done = bf16[4,256,1024]{2,1,0:T(8,128)(2,1)S(1)} copy-done((bf16[4,256,1024]{2,1,0:T(8,128)(2,1)S(1)}, bf16[4,256,1024]{2,1,0:T(8,128)(2,1)}, u32[]{:S(2)}) %copy-start) | copy-done | bytes 2097176
  33.1 0.0 copy-start.1
  33.1 1.4 %copy-done.1 = bf16[3,256,1024]{2,1,0:T(8,128)(2,1)S(1)} copy-done((bf16[3,256,1024]{2,1,0:T(8,128)(2,1)S(1)}, bf16[3,256,1024]{2,1,0:T(8,128)(2,1)}, u32[]{:S(2)}) %copy-start.1) | copy-done | bytes 1572888
  34.5 0.0 copy-start.2
  34.5 0.9 copy-done.2
  35.4 0.9 shard_map.87
  36.3 11.2 %all_to_all.21.even_ref = bf16[4,5,64,256]{3,2,1,0:T(8,128)(2,1)S(1)} all-to-all(bf16[4,5,64,256]{3,2,1,0:T(8,128)(2,1)S(1)} %get-tuple-element.18), channel_id=1, replica_groups=mesh['aux'=4,'blk'=128] {'aux'}, dimensions={0} | all-to-all | bytes 1310720 | tf_op jit(solution)/shard_map/all_to_all | solution.py:305
  47.5 0.0 collective-permute-done.before_ref
  47.5 0.7 shard_map.88
  48.2 0.0 collective-permute-done.2.odd_ref
  48.2 0.0 collective-permute-done.1.after_ref
  48.2 0.0 copy-start.3
  48.3 0.0 copy-start.4
  48.3 1.1 %shard_map.89 = bf16[4,208,256]{2,1,0:T(8,128)(2,1)S(1)} custom-call(bf16[4,256,1024]{2,1,0:T(8,128)(2,1)S(1)} %copy-done, bf16[4,256,1024]{2,1,0:T(8,128)(2,1)S(1)} %collective-permute-done.before_ref, bf16[3,256,1024]{2,1,0:T(8,128)(2,1)S(1)} %collective-permute-done.1.after_ref, bf16[4,5,64,256]{3,2,1,0:T(8,128)(2,1)S(1)} %all_to_all.21.even_ref, ...), custom_call_target="tpu_custom_call" | custom-call | tf_op jit(solution)/shard_map/pallas_call | solution.py:309
  49.4 11.9 %all_to_all.22.parts_ref = bf16[4,208,256]{2,1,0:T(8,128)(2,1)S(1)} all-to-all(bf16[4,208,256]{2,1,0:T(8,128)(2,1)S(1)} %shard_map.89), channel_id=1, replica_groups=mesh['aux'=4,'blk'=128] {'aux'}, dimensions={0} | all-to-all | bytes 851968 | tf_op jit(solution)/shard_map/all_to_all | solution.py:312
  61.3 0.7 shard_map.90
  61.9 18.2 %all-to-all-start.3 = ((f32[128,1,128]{2,1,0:T(1,128)}), f32[128,1,128]{2,1,0:T(1,128)S(1)}, u32[]{:S(2)}, u32[]{:S(2)}) async-start(f32[128,1,128]{2,1,0:T(1,128)} %get-tuple-element.25), calls=%async_computation.3 | async-start | bytes 131072 | tf_op jit(solution)/shard_map/all_to_all | solution.py:317
  80.2 2.8 %collective-permute-start.3 = (bf16[2,64,256]{2,1,0:T(8,128)(2,1)S(1)}, bf16[2,64,256]{2,1,0:T(8,128)(2,1)S(1)}, u32[]{:S(2)}, u32[]{:S(2)}) collective-permute-start(bf16[2,64,256]{2,1,0:T(8,128)(2,1)S(1)} %get-tuple-element.24), channel_id=1, source_target_pairs={{1,0},{2,1},{3,2},{4,3},{5,4},{6,5},{7,6},{8,7},{9,8},{10,9},{11,1... | collective-permute-start | bytes 196616 | tf_op jit(solution)/shard_map/ppermute | solution.py:25
  83.0 3.1 %collective-permute-done.3.odd_ref = bf16[2,64,256]{2,1,0:T(8,128)(2,1)S(1)} collective-permute-done((bf16[2,64,256]{2,1,0:T(8,128)(2,1)S(1)}, bf16[2,64,256]{2,1,0:T(8,128)(2,1)S(1)}, u32[]{:S(2)}, u32[]{:S(2)}) %collective-permute-start.3) | collective-permute-done | bytes 65568 | tf_op jit(solution)/shard_map/ppermute | solution.py:25
  86.0 5.5 %all-to-all-done.3.energy_ref = f32[128,1,128]{2,1,0:T(1,128)S(1)} async-done(((f32[128,1,128]{2,1,0:T(1,128)}), f32[128,1,128]{2,1,0:T(1,128)S(1)}, u32[]{:S(2)}, u32[]{:S(2)}) %all-to-all-start.3) | async-done | bytes 65568 | tf_op jit(solution)/shard_map/all_to_all | solution.py:317
  91.5 0.0 copy-done.3
  91.6 0.0 copy-done.4
  91.6 1.4 %shard_map.91 = (bf16[1,4,64,256]{3,2,1,0:T(8,128)(2,1)}, f32[3]{0:T(128)}) custom-call(s32[1,4]{1,0:T(1,128)S(1)} %copy-done.3, f32[3]{0:T(128)S(1)} %copy-done.4, bf16[64,256]{1,0:T(8,128)(2,1)S(1)} %get-tuple-element.19.t0_ref, bf16[64,256]{1,0:T(8,128)(2,1)S(1)} %get-tuple-element.23.t2_ref, bf16[2,64,256]{2,1,0:T(8,128)(2,1)S(1)} %collective-permute-done.3.odd_ref, ...), custom_call_target="tpu_custom_call" | custom-call | tf_op jit(solution)/shard_map/pallas_call | solution.py:320
Async XLA Ops:
  6.2 41.3 %collective-permute-start = (bf16[4,256,1024]{2,1,0:T(8,128)(2,1)}, bf16[4,256,1024]{2,1,0:T(8,128)(2,1)S(1)}, u32[]{:S(2)}, u32[]{:S(2)}) collective-permute-start(bf16[4,256,1024]{2,1,0:T(8,128)(2,1)} %get-tuple-element.14.high_ref), channel_id=1, source_target_pairs={{0,1},{1,2},{2,3},{3,4},{4,5},{5,6},{6,7},{7,8},{8,9},{9,10},{10,1... | collective-permute-start | bytes 6291464 | tf_op jit(solution)/shard_map/ppermute | solution.py:25
  10.8 37.4 %collective-permute-start.1 = (bf16[3,256,1024]{2,1,0:T(8,128)(2,1)}, bf16[3,256,1024]{2,1,0:T(8,128)(2,1)S(1)}, u32[]{:S(2)}, u32[]{:S(2)}) collective-permute-start(bf16[3,256,1024]{2,1,0:T(8,128)(2,1)} %get-tuple-element.15.low_ref), channel_id=1, source_target_pairs={{2,0},{3,1},{4,2},{5,3},{6,4},{7,5},{8,6},{9,7},{10,8},{11,9},{12,... | collective-permute-start | bytes 4718600 | tf_op jit(solution)/shard_map/ppermute | solution.py:25
  23.1 25.1 %collective-permute-start.2 = (bf16[4,4,64,256]{3,2,1,0:T(8,128)(2,1)S(1)}, bf16[4,4,64,256]{3,2,1,0:T(8,128)(2,1)S(1)}, u32[]{:S(2)}, u32[]{:S(2)}) collective-permute-start(bf16[4,4,64,256]{3,2,1,0:T(8,128)(2,1)S(1)} %all_to_all.20), channel_id=1, source_target_pairs={{0,1},{1,2},{2,3},{3,4},{4,5},{5,6},{6,7},{7,8},{8,9},{9,10},{10,1... | collective-permute-start | bytes 1572872 | tf_op jit(solution)/shard_map/ppermute | solution.py:25
  31.5 1.6 %copy-start = (bf16[4,256,1024]{2,1,0:T(8,128)(2,1)S(1)}, bf16[4,256,1024]{2,1,0:T(8,128)(2,1)}, u32[]{:S(2)}) copy-start(bf16[4,256,1024]{2,1,0:T(8,128)(2,1)} %get-tuple-element.14.high_ref) | copy-start | bytes 6291460
  33.1 1.4 %copy-start.1 = (bf16[3,256,1024]{2,1,0:T(8,128)(2,1)S(1)}, bf16[3,256,1024]{2,1,0:T(8,128)(2,1)}, u32[]{:S(2)}) copy-start(bf16[3,256,1024]{2,1,0:T(8,128)(2,1)} %get-tuple-element.15.low_ref) | copy-start | bytes 4718596
  34.5 0.9 copy-start.2
  48.2 43.3 %copy-start.3 = (s32[1,4]{1,0:T(1,128)S(1)}, s32[1,4]{1,0:T(1,128)}, u32[]{:S(2)}) copy-start(s32[1,4]{1,0:T(1,128)} %row_ref.1) | copy-start | bytes 52
  48.3 43.3 %copy-start.4 = (f32[3]{0:T(128)S(1)}, f32[3]{0:T(128)}, u32[]{:S(2)}) copy-start(f32[3]{0:T(128)} %steps_ref.1) | copy-start | bytes 40
  61.9 29.6 %all-to-all-start.3 = ((f32[128,1,128]{2,1,0:T(1,128)}), f32[128,1,128]{2,1,0:T(1,128)S(1)}, u32[]{:S(2)}, u32[]{:S(2)}) async-start(f32[128,1,128]{2,1,0:T(1,128)} %get-tuple-element.25), calls=%async_computation.3 | async-start | bytes 131072 | tf_op jit(solution)/shard_map/all_to_all | solution.py:317
  80.2 5.9 %collective-permute-start.3 = (bf16[2,64,256]{2,1,0:T(8,128)(2,1)S(1)}, bf16[2,64,256]{2,1,0:T(8,128)(2,1)S(1)}, u32[]{:S(2)}, u32[]{:S(2)}) collective-permute-start(bf16[2,64,256]{2,1,0:T(8,128)(2,1)S(1)} %get-tuple-element.24), channel_id=1, source_target_pairs={{1,0},{2,1},{3,2},{4,3},{5,4},{6,5},{7,6},{8,7},{9,8},{10,9},{11,1... | collective-permute-start | bytes 196616 | tf_op jit(solution)/shard_map/ppermute | solution.py:25

commit v4 on v3

--- a/solution.py
+++ b/solution.py
@@ -25,79 +25,30 @@
     return lax.ppermute(value, axis, pairs)
 
 
-def by_offset(row_ref, tiles_ref, even_ref, odd_ref):
-    block = row_ref[0, 0]
-    for k in range(4):
-        out = even_ref if k % 2 == 0 else odd_ref
-        for which in range(2):
-            total = jnp.zeros(tiles_ref.shape[2:], jnp.float32)
-            for s in range(4):
-                other = row_ref[0, s]
-                full = 1.0 if s == 0 else 2.0
-                weight = jnp.where((other >= 0) & (other - block == k), full, 0.0)
-                total = total + weight * tiles_ref[which, s].astype(jnp.float32)
-            out[k // 2 * 2 + which] = total.astype(jnp.bfloat16)
-
-
-def align_kernel(
-    chunks,
-    start_hbm,
-    count_hbm,
-    row_hbm,
-    slab_hbm,
-    density_hbm,
-    direction_hbm,
-    high_hbm,
-    low_hbm,
-    even_hbm,
-    odd_hbm,
-    start_ref,
-    count_ref,
-    row_ref,
-    slab_ref,
-    select_ref,
-    high_ref,
-    low_ref,
-    tiles_ref,
-    even_ref,
-    odd_ref,
-    small_sem,
-    in_sem,
-    out_sem,
-    tile_sem,
-):
+def align_kernel(chunks, start_hbm, count_hbm, slab_ref, mid_ref, top_ref, low_ref, start_ref, count_ref, select_ref, sem):
     _, auxb, _ = slab_ref.shape
-    begins = [sum(chunks[:n]) for n in range(len(chunks))]
     bf16 = jnp.bfloat16
     small = [
-        pltpu.make_async_copy(source, target, small_sem.at[n])
-        for n, (source, target) in enumerate(((start_hbm, start_ref), (count_hbm, count_ref), (row_hbm, row_ref)))
+        pltpu.make_async_copy(source, target, sem.at[n])
+        for n, (source, target) in enumerate(((start_hbm, start_ref), (count_hbm, count_ref)))
     ]
-    loads = [
-        pltpu.make_async_copy(slab_hbm.at[pl.ds(begin, chunk)], slab_ref.at[pl.ds(begin, chunk)], in_sem.at[n])
-        for n, (begin, chunk) in enumerate(zip(begins, chunks))
-    ]
-    tiles = [
-        pltpu.make_async_copy(source.at[0], tiles_ref.at[n], tile_sem.at[n])
-        for n, source in enumerate((density_hbm, direction_hbm))
-    ]
-    for copy in small + loads + tiles:
+    for copy in small:
         copy.start()
     for copy in small:
         copy.wait()
-    shift = start_ref[0, 0] - 32 * row_ref[0, 0]
-    count = count_ref[0, 0]
+    shift = start_ref[0] & 31
+    count = count_ref[0]
     a = lax.broadcasted_iota(jnp.int32, (128, 256), 0)
     to = lax.broadcasted_iota(jnp.int32, (128, 256), 1)
     hit = (a < count) & (((a + shift) & 127) == ((to >> 6) << 5) + (to & 31))
     for m in range(2):
         select_ref[m * 128:(m + 1) * 128] = jnp.where(hit & (((to >> 5) & 1) == m), 1.0, 0.0).astype(bf16)
-    stores = []
-    for n, (begin, chunk) in enumerate(zip(begins, chunks)):
+    begin = 0
+    for chunk in chunks:
         first = (lax.broadcasted_iota(jnp.int32, (chunk, 128), 1) & 31) >= shift
         zero = jnp.zeros((chunk, 128), bf16)
-        loads[n].wait()
         rows = slice(begin, begin + chunk)
+        begin += chunk
         by_function = jnp.swapaxes(slab_ref[rows], 0, 1)
         pairs = [jnp.concatenate([by_function[p], by_function[p + 1]], axis=1) for p in range(0, auxb, 2)]
         placed = jnp.dot(jnp.concatenate(pairs, axis=0), select_ref[...], preferred_element_type=jnp.float32)
@@ -109,60 +60,51 @@
                 piece = jnp.concatenate([part[:, q * 64:(q + 1) * 64] for part in parts], axis=1)
                 if q == 0:
                     low_ref[0, rows, lanes] = jnp.where(first, piece, zero)
-                    high_ref[3, rows, lanes] = jnp.where(first, zero, piece)
+                    top_ref[1, rows, lanes] = jnp.where(first, zero, piece)
                     continue
-                high_ref[q - 1, rows, lanes] = piece
-                if q <= 2:
+                if q == 3:
+                    top_ref[0, rows, lanes] = piece
+                else:
+                    mid_ref[q - 1, rows, lanes] = piece
                     low_ref[q, rows, lanes] = piece
-        part = pl.ds(begin, chunk)
-        for m, (source, target) in enumerate(((low_ref, low_hbm), (high_ref, high_hbm))):
-            copy = pltpu.make_async_copy(source.at[:, part], target.at[:, part], out_sem.at[n, m])
-            copy.start()
-            stores.append(copy)
-    for copy in tiles:
-        copy.wait()
-    by_offset(row_ref, tiles_ref, even_ref, odd_ref)
-    targets = [even_hbm] + [odd_hbm.at[to] for to in range(4)]
-    for n, target in enumerate(targets):
-        copy = pltpu.make_async_copy(odd_ref if n else even_ref, target, tile_sem.at[2 + n])
-        copy.start()
-        stores.append(copy)
-    for copy in stores:
-        copy.wait()
-
-
-def align(slabs, start, count, row, density, direction):
+
+
+def align(slabs, start, count):
     rows, auxb, _ = slabs.shape
-    steps = len(CHUNKS)
     depth = auxb * 32
-    high = (4, rows, depth)
-    low = (3, rows, depth)
-    tiles = (4,) + density.shape[2:]
     bf16 = jnp.bfloat16
-    dma = pltpu.SemaphoreType.DMA
     return pl.pallas_call(
         functools.partial(align_kernel, CHUNKS),
-        in_specs=[spec(pl.ANY)] * 6,
-        out_specs=[spec(pl.ANY)] * 4,
-        out_shape=[jax.ShapeDtypeStruct(shape, bf16) for shape in (high, low, tiles, (4,) + tiles)],
+        in_specs=[spec(pl.ANY)] * 2 + [spec(VMEM)],
+        out_specs=[spec(VMEM)] * 3,
+        out_shape=[jax.ShapeDtypeStruct((groups, rows, depth), bf16) for groups in (2, 2, 3)],
         scratch_shapes=[
-            SMEM((1, 1), jnp.int32),
-            SMEM((1, 1), jnp.int32),
-            SMEM(row.shape, jnp.int32),
-            VMEM(slabs.shape, bf16),
+            SMEM((1,), jnp.int32),
+            SMEM((1,), jnp.int32),
             VMEM((256, 256), bf16),
-            VMEM(high, bf16),
-            VMEM(low, bf16),
-            VMEM((2,) + density.shape[1:], bf16),
-            VMEM(tiles, bf16),
-            VMEM(tiles, bf16),
-            dma((3,)),
-            dma((steps,)),
-            dma((steps, 2)),
-            dma((7,)),
+            pltpu.SemaphoreType.DMA((2,)),
         ],
-        compiler_params=pltpu.CompilerParams(vmem_limit_bytes=60 * MIB),
-    )(start[None], count[None], row, slabs, density, direction)
+        compiler_params=pltpu.CompilerParams(vmem_limit_bytes=24 * MIB),
+    )(start, count, slabs)
+
+
+def by_offset_kernel(row_ref, density_ref, direction_ref, even_ref, odd_ref):
+    block = row_ref[0, 0]
+    for k in range(4):
+        for which, source in enumerate((density_ref, direction_ref)):
+            total = jnp.zeros(source.shape[2:], jnp.float32)
+            for s in range(4):
+                other = row_ref[0, s]
+                full = 1.0 if s == 0 else 2.0
+                weight = jnp.where((other >= 0) & (other - block == k), full, 0.0)
+                total = total + weight * source[0, s].astype(jnp.float32)
+            total = total.astype(jnp.bfloat16)
+            place = k // 2 * 2 + which
+            if k % 2 == 0:
+                even_ref[place] = total
+            else:
+                for to in range(4):
+                    odd_ref[to, place] = total
 
 
 def product(left, right):
@@ -185,8 +127,8 @@
     return parts
 
 
-def own_kernel(high_ref, low_ref, even_ref, tile_ref, out_ref):
-    own = [low_ref[0]] + [high_ref[q] for q in range(4)]
+def own_kernel(mid_ref, top_ref, low_ref, even_ref, tile_ref, out_ref):
+    own = [low_ref[0], mid_ref[0], mid_ref[1], top_ref[0], top_ref[1]]
     tile = product(own, own)
     tile_ref[...] = tile
     for to in range(4):
@@ -194,9 +136,10 @@
         out_ref[to, 4] = tile[to * 64:(to + 1) * 64].astype(jnp.bfloat16)
 
 
-def near_kernel(high_ref, low_ref, before_ref, tile_ref, even_ref, out_ref, own_ref, sums_ref):
-    own = [low_ref[0]] + [high_ref[q] for q in range(3)]
-    out_ref[...] = product([before_ref[q] for q in range(4)], own)
+def near_kernel(mid_ref, top_ref, low_ref, before_mid_ref, before_top_ref, tile_ref, even_ref, out_ref, own_ref, sums_ref):
+    own = [low_ref[0], mid_ref[0], mid_ref[1], top_ref[0]]
+    before = [before_mid_ref[0], before_mid_ref[1], before_top_ref[0], before_top_ref[1]]
+    out_ref[...] = product(before, own)
     sums = tile_sums(tile_ref, 0, even_ref)
     for which in range(2):
         sums_ref[which] = sums[which]
@@ -206,9 +149,10 @@
     own_ref[...] = total.astype(jnp.bfloat16)
 
 
-def far_kernel(high_ref, before_ref, after_ref, even_ref, odd_ref, near_ref, sums_in_ref, out_ref):
-    t2 = product([high_ref[q + 1] for q in range(3)], [after_ref[q] for q in range(3)])
-    t3 = product([before_ref[q + 2] for q in range(2)], [after_ref[q] for q in range(2)])
+def far_kernel(mid_ref, top_ref, before_ref, after_ref, even_ref, odd_ref, near_ref, sums_in_ref, out_ref):
+    after = [after_ref[q] for q in range(3)]
+    t2 = product([mid_ref[1], top_ref[0], top_ref[1]], after)
+    t3 = product([before_ref[q] for q in range(2)], after)
     sums = [sums_in_ref[0], sums_in_ref[1]]
     for tile, place, weights_ref in ((near_ref, 0, odd_ref), (t2, 1, even_ref), (t3, 1, odd_ref)):
         sums = [a + b for a, b in zip(sums, tile_sums(tile, place, weights_ref))]
@@ -293,21 +237,26 @@
     def single(*shape):
         return jax.ShapeDtypeStruct(shape, jnp.float32)
 
-    high, low, even, odd = align(slabs, orbital_start, orbital_count, partners, density, direction)
+    mid, top, low = align(slabs, orbital_start, orbital_count)
     after = moved_by(low, "blk", -2)
-    before = moved_by(high, "blk", 1)
+    before_mid = moved_by(mid, "blk", 1)
+    before_top = moved_by(top, "blk", 1)
+    low, density, direction = lax.optimization_barrier((low, density, direction))
+    even, odd = kernel_call(by_offset_kernel, [spec(SMEM)] + [spec(VMEM)] * 2, [half(4, part, rows), half(aux, 4, part, rows)])(
+        partners, density, direction
+    )
     odd = lax.all_to_all(odd, "aux", 0, 0, tiled=True)
     odd = moved_by(odd, "blk", 1)
 
-    t0, even = kernel_call(own_kernel, [spec(VMEM)] * 3, [single(rows, rows), half(aux, 5, part, rows)])(
-        high, low, even
+    t0, even = kernel_call(own_kernel, [spec(VMEM)] * 4, [single(rows, rows), half(aux, 5, part, rows)])(
+        mid, top, low, even
     )
     even = lax.all_to_all(even, "aux", 0, 0, tiled=True)
     t1, t0, sums = kernel_call(
-        near_kernel, [spec(VMEM)] * 5, [single(rows, rows), half(part, rows), single(2, 8, rows)]
-    )(high, low, before, t0, even)
-    (far,) = kernel_call(far_kernel, [spec(VMEM)] * 7, [half(aux, 3 * part + 16, rows)])(
-        high, before, after, even, odd, t1, sums
+        near_kernel, [spec(VMEM)] * 7, [single(rows, rows), half(part, rows), single(2, 8, rows)]
+    )(mid, top, low, before_mid, before_top, t0, even)
+    (far,) = kernel_call(far_kernel, [spec(VMEM)] * 8, [half(aux, 3 * part + 16, rows)])(
+        mid, top, before_top, after, even, odd, t1, sums
     )
     far = lax.all_to_all(far, "aux", 0, 0, tiled=True)
     odd, t2, energy = kernel_call(

time: 93.4 us -> 90.7 us (0.971)
  starting transfers between devices: 35.3 us -> 37.9 us
  local copies, waits for them, and re-layouts: 3.91 us -> 1.6 us
  blocking collectives: 34 us -> 32.5 us
  Pallas kernels: 9.09 us -> 7.64 us
    all_to_all x1, blocking collectives: 11.9 us -> 8.78 us  [body(): far = lax.all_to_all(far, 'aux', 0, 0, tiled=True)]
    unnamed x10, local copies, waits for them, and re-layouts: 3.91 us -> 1.6 us
    pallas_call x1, Pallas kernels: 4.29 us -> 2.06 us  [align(): pl.pallas_call(functools.partial(align_kernel, CHUNKS), in_specs=[spec(pl...]
    ppermute x4 -> x5, starting transfers between devices: 17.1 us -> 19 us  [moved_by(): return lax.ppermute(value, axis, pairs)]
    all_to_all x1, blocking collectives: 11.2 us -> 12.3 us  [body(): even = lax.all_to_all(even, 'aux', 0, 0, tiled=True)]
    pallas_call x3 -> x4, Pallas kernels: 2.73 us -> 3.51 us  [the longest x1 1.14 us: body(): kernel_call(far_kernel, [spec(VMEM)] * 8, [half(aux, 3 * part + 16, rows)])]
    ppermute x4 -> x5, waiting for transfers between devices: 3.08 us -> 3.08 us  [moved_by(): return lax.ppermute(value, axis, pairs)]
  transfers between devices with their start and end apart: 5 -> 6, of which waited for: 2 -> 2; matrix products, arithmetic and copies ran while one was open for 0% -> 0% of each run, Pallas kernels for 2% -> 3%
where the time goes in v4:
time: 90.7 us; the launch traced here: 90.3 us
  starting transfers between devices  37.9 us (42%)
  blocking collectives  32.5 us (36%)
  waiting for transfers between devices  8.58 us (9%)
  Pallas kernels  7.64 us (8%)
  between operations  2.09 us (2%)
  local copies, waits for them, and re-layouts  1.6 us (2%)
    ppermute x5, starting transfers between devices, moved_by(): return lax.ppermute(value, axis, pairs)  19 us
    all_to_all x1, starting transfers between devices, body(): energy = lax.all_to_all(energy, 'blk', 0, 0, tiled=True)  18.9 us
    all_to_all x1, blocking collectives, body(): even = lax.all_to_all(even, 'aux', 0, 0, tiled=True)  12.3 us
    all_to_all x1, blocking collectives, body(): odd = lax.all_to_all(odd, 'aux', 0, 0, tiled=True)  11.4 us
    all_to_all x1, blocking collectives, body(): far = lax.all_to_all(far, 'aux', 0, 0, tiled=True)  8.78 us
    all_to_all x1, waiting for transfers between devices, body(): energy = lax.all_to_all(energy, 'blk', 0, 0, tiled=True)  5.5 us
    ppermute x5, waiting for transfers between devices, moved_by(): return lax.ppermute(value, axis, pairs)  3.08 us
    pallas_call x1, Pallas kernels, align(): pl.pallas_call(functools.partial(align_kernel, CHUNKS), in_specs=[spec(pl...  2.06 us
  transfers between devices with their start and end apart: 6, of which 2 were waited for; matrix products, arithmetic and copies ran while one was open for 0% of the time, Pallas kernels for 3%

profile of v4, /device:TPU:1, one launch (start us, length us, event | category | flops | bytes accessed | tf_op | source)
XLA Modules:
  0.0 90.3 jit_solution(15712719854834732770)
XLA Ops:
  0.6 0.0 copy-start.3
  1.9 0.0 copy-start
  2.0 1.6 %copy-done = bf16[256,32,128]{2,1,0:T(8,128)(2,1)S(1)} copy-done((bf16[256,32,128]{2,1,0:T(8,128)(2,1)S(1)}, bf16[256,32,128]{2,1,0:T(8,128)(2,1)}, u32[]{:S(2)}) %copy-start) | copy-done | bytes 2097176
  3.5 0.0 copy-start.1
  3.5 0.0 copy-start.2
  3.5 2.1 %shard_map.86 = (bf16[2,256,1024]{2,1,0:T(8,128)(2,1)S(1)}, bf16[2,256,1024]{2,1,0:T(8,128)(2,1)S(1)}, bf16[3,256,1024]{2,1,0:T(8,128)(2,1)S(1)}) custom-call(s32[1]{0:T(128)S(6)} %copy.9.start_hbm, s32[1]{0:T(128)S(6)} %copy.10.count_hbm, bf16[256,32,128]{2,1,0:T(8,128)(2,1)S(1)} %copy-done), custom_call_target="tpu_custom_call" | custom-call | tf_op jit(solution)/shard_map/pallas_call | solution.py:76
  5.6 1.3 %collective-permute-start.2 = (bf16[3,256,1024]{2,1,0:T(8,128)(2,1)S(1)}, bf16[3,256,1024]{2,1,0:T(8,128)(2,1)S(1)}, u32[]{:S(2)}, u32[]{:S(2)}) collective-permute-start(bf16[3,256,1024]{2,1,0:T(8,128)(2,1)S(1)} %get-tuple-element.21.low_ref), channel_id=1, source_target_pairs={{2,0},{3,1},{4,2},{5,3},{6,4},{7,5},{8,6},{9,7},{10,8},{11,9},{12,... | collective-permute-start | bytes 4718600 | tf_op jit(solution)/shard_map/ppermute | solution.py:25
  6.9 11.0 %collective-permute-start = (bf16[2,256,1024]{2,1,0:T(8,128)(2,1)S(1)}, bf16[2,256,1024]{2,1,0:T(8,128)(2,1)S(1)}, u32[]{:S(2)}, u32[]{:S(2)}) collective-permute-start(bf16[2,256,1024]{2,1,0:T(8,128)(2,1)S(1)} %get-tuple-element.18.mid_ref), channel_id=1, source_target_pairs={{0,1},{1,2},{2,3},{3,4},{4,5},{5,6},{6,7},{7,8},{8,9},{9,10},{10,1... | collective-permute-start | bytes 3145736 | tf_op jit(solution)/shard_map/ppermute | solution.py:25
  18.0 1.9 %collective-permute-start.1 = (bf16[2,256,1024]{2,1,0:T(8,128)(2,1)S(1)}, bf16[2,256,1024]{2,1,0:T(8,128)(2,1)S(1)}, u32[]{:S(2)}, u32[]{:S(2)}) collective-permute-start(bf16[2,256,1024]{2,1,0:T(8,128)(2,1)S(1)} %get-tuple-element.19.top_ref), channel_id=1, source_target_pairs={{0,1},{1,2},{2,3},{3,4},{4,5},{5,6},{6,7},{7,8},{8,9},{9,10},{10,1... | collective-permute-start | bytes 3145736 | tf_op jit(solution)/shard_map/ppermute | solution.py:25
  19.9 0.0 copy-done.3
  19.9 0.0 copy-done.1
  19.9 0.0 copy-done.2
  19.9 0.7 shard_map.87
  20.7 11.4 %all_to_all.20 = bf16[4,4,64,256]{3,2,1,0:T(8,128)(2,1)S(1)} all-to-all(bf16[4,4,64,256]{3,2,1,0:T(8,128)(2,1)S(1)} %get-tuple-element.28), channel_id=1, replica_groups=mesh['aux'=4,'blk'=128] {'aux'}, dimensions={0} | all-to-all | bytes 1048576 | tf_op jit(solution)/shard_map/all_to_all | solution.py:248
  32.1 1.9 %collective-permute-start.3 = (bf16[4,4,64,256]{3,2,1,0:T(8,128)(2,1)S(1)}, bf16[4,4,64,256]{3,2,1,0:T(8,128)(2,1)S(1)}, u32[]{:S(2)}, u32[]{:S(2)}) collective-permute-start(bf16[4,4,64,256]{3,2,1,0:T(8,128)(2,1)S(1)} %all_to_all.20), channel_id=1, source_target_pairs={{0,1},{1,2},{2,3},{3,4},{4,5},{5,6},{6,7},{7,8},{8,9},{9,10},{10,1... | collective-permute-start | bytes 1572872 | tf_op jit(solution)/shard_map/ppermute | solution.py:25
  34.0 0.9 shard_map.88
  34.9 12.3 %all_to_all.21.even_ref = bf16[4,5,64,256]{3,2,1,0:T(8,128)(2,1)S(1)} all-to-all(bf16[4,5,64,256]{3,2,1,0:T(8,128)(2,1)S(1)} %get-tuple-element.26), channel_id=1, replica_groups=mesh['aux'=4,'blk'=128] {'aux'}, dimensions={0} | all-to-all | bytes 1310720 | tf_op jit(solution)/shard_map/all_to_all | solution.py:254
  47.2 0.0 collective-permute-done.before_mid_ref
  47.2 0.0 collective-permute-done.1.before_top_ref.before_ref
  47.2 0.8 shard_map.89
  48.0 0.0 collective-permute-done.3.odd_ref
  48.0 0.0 collective-permute-done.2.after_ref
  48.0 0.0 copy-start.4
  48.0 1.1 %shard_map.90 = bf16[4,208,256]{2,1,0:T(8,128)(2,1)S(1)} custom-call(bf16[2,256,1024]{2,1,0:T(8,128)(2,1)S(1)} %get-tuple-element.18.mid_ref, bf16[2,256,1024]{2,1,0:T(8,128)(2,1)S(1)} %get-tuple-element.19.top_ref, bf16[2,256,1024]{2,1,0:T(8,128)(2,1)S(1)} %collective-permute-done.1.before_top_ref.before_ref, ...), custom_call_target="tpu_custom_call" | custom-call | tf_op jit(solution)/shard_map/pallas_call | solution.py:258
  49.2 8.8 %all_to_all.22.parts_ref = bf16[4,208,256]{2,1,0:T(8,128)(2,1)S(1)} all-to-all(bf16[4,208,256]{2,1,0:T(8,128)(2,1)S(1)} %shard_map.90), channel_id=1, replica_groups=mesh['aux'=4,'blk'=128] {'aux'}, dimensions={0} | all-to-all | bytes 851968 | tf_op jit(solution)/shard_map/all_to_all | solution.py:261
  58.0 0.7 shard_map.91
  58.6 18.9 %all-to-all-start.3 = ((f32[128,1,128]{2,1,0:T(1,128)}), f32[128,1,128]{2,1,0:T(1,128)S(1)}, u32[]{:S(2)}, u32[]{:S(2)}) async-start(f32[128,1,128]{2,1,0:T(1,128)} %get-tuple-element.33), calls=%async_computation.3 | async-start | bytes 131072 | tf_op jit(solution)/shard_map/all_to_all | solution.py:266
  77.5 2.8 %collective-permute-start.4 = (bf16[2,64,256]{2,1,0:T(8,128)(2,1)S(1)}, bf16[2,64,256]{2,1,0:T(8,128)(2,1)S(1)}, u32[]{:S(2)}, u32[]{:S(2)}) collective-permute-start(bf16[2,64,256]{2,1,0:T(8,128)(2,1)S(1)} %get-tuple-element.32), channel_id=1, source_target_pairs={{1,0},{2,1},{3,2},{4,3},{5,4},{6,5},{7,6},{8,7},{9,8},{10,9},{11,1... | collective-permute-start | bytes 196616 | tf_op jit(solution)/shard_map/ppermute | solution.py:25
  80.4 3.1 %collective-permute-done.4.odd_ref = bf16[2,64,256]{2,1,0:T(8,128)(2,1)S(1)} collective-permute-done((bf16[2,64,256]{2,1,0:T(8,128)(2,1)S(1)}, bf16[2,64,256]{2,1,0:T(8,128)(2,1)S(1)}, u32[]{:S(2)}, u32[]{:S(2)}) %collective-permute-start.4) | collective-permute-done | bytes 65568 | tf_op jit(solution)/shard_map/ppermute | solution.py:25
  83.4 5.5 %all-to-all-done.3.energy_ref = f32[128,1,128]{2,1,0:T(1,128)S(1)} async-done(((f32[128,1,128]{2,1,0:T(1,128)}), f32[128,1,128]{2,1,0:T(1,128)S(1)}, u32[]{:S(2)}, u32[]{:S(2)}) %all-to-all-start.3) | async-done | bytes 65568 | tf_op jit(solution)/shard_map/all_to_all | solution.py:266
  88.9 0.0 copy-done.4
  88.9 1.4 %shard_map.92 = (bf16[1,4,64,256]{3,2,1,0:T(8,128)(2,1)}, f32[3]{0:T(128)}) custom-call(s32[1,4]{1,0:T(1,128)S(1)} %copy-done.3, f32[3]{0:T(128)S(1)} %copy-done.4, bf16[64,256]{1,0:T(8,128)(2,1)S(1)} %get-tuple-element.27.t0_ref, bf16[64,256]{1,0:T(8,128)(2,1)S(1)} %get-tuple-element.31.t2_ref, bf16[2,64,256]{2,1,0:T(8,128)(2,1)S(1)} %collective-permute-done.4.odd_ref, ...), custom_call_target="tpu_custom_call" | custom-call | tf_op jit(solution)/shard_map/pallas_call | solution.py:269
Async XLA Ops:
  0.6 19.3 %copy-start.3 = (s32[1,4]{1,0:T(1,128)S(1)}, s32[1,4]{1,0:T(1,128)}, u32[]{:S(2)}) copy-start(s32[1,4]{1,0:T(1,128)} %row_ref.3) | copy-start | bytes 52
  1.9 1.6 %copy-start = (bf16[256,32,128]{2,1,0:T(8,128)(2,1)S(1)}, bf16[256,32,128]{2,1,0:T(8,128)(2,1)}, u32[]{:S(2)}) copy-start(bf16[256,32,128]{2,1,0:T(8,128)(2,1)} %slab_ref.1) | copy-start | bytes 6291460
  3.5 16.4 %copy-start.1 = (bf16[1,4,64,256]{3,2,1,0:T(8,128)(2,1)S(1)}, bf16[1,4,64,256]{3,2,1,0:T(8,128)(2,1)}, u32[]{:S(2)}) copy-start(bf16[1,4,64,256]{3,2,1,0:T(8,128)(2,1)} %density_ref) | copy-start | bytes 393220
  3.5 16.4 %copy-start.2 = (bf16[1,4,64,256]{3,2,1,0:T(8,128)(2,1)S(1)}, bf16[1,4,64,256]{3,2,1,0:T(8,128)(2,1)}, u32[]{:S(2)}) copy-start(bf16[1,4,64,256]{3,2,1,0:T(8,128)(2,1)} %direction_ref) | copy-start | bytes 393220
  5.6 42.4 %collective-permute-start.2 = (bf16[3,256,1024]{2,1,0:T(8,128)(2,1)S(1)}, bf16[3,256,1024]{2,1,0:T(8,128)(2,1)S(1)}, u32[]{:S(2)}, u32[]{:S(2)}) collective-permute-start(bf16[3,256,1024]{2,1,0:T(8,128)(2,1)S(1)} %get-tuple-element.21.low_ref), channel_id=1, source_target_pairs={{2,0},{3,1},{4,2},{5,3},{6,4},{7,5},{8,6},{9,7},{10,8},{11,9},{12,... | collective-permute-start | bytes 4718600 | tf_op jit(solution)/shard_map/ppermute | solution.py:25
  6.9 40.3 %collective-permute-start = (bf16[2,256,1024]{2,1,0:T(8,128)(2,1)S(1)}, bf16[2,256,1024]{2,1,0:T(8,128)(2,1)S(1)}, u32[]{:S(2)}, u32[]{:S(2)}) collective-permute-start(bf16[2,256,1024]{2,1,0:T(8,128)(2,1)S(1)} %get-tuple-element.18.mid_ref), channel_id=1, source_target_pairs={{0,1},{1,2},{2,3},{3,4},{4,5},{5,6},{6,7},{7,8},{8,9},{9,10},{10,1... | collective-permute-start | bytes 3145736 | tf_op jit(solution)/shard_map/ppermute | solution.py:25
  18.0 29.3 %collective-permute-start.1 = (bf16[2,256,1024]{2,1,0:T(8,128)(2,1)S(1)}, bf16[2,256,1024]{2,1,0:T(8,128)(2,1)S(1)}, u32[]{:S(2)}, u32[]{:S(2)}) collective-permute-start(bf16[2,256,1024]{2,1,0:T(8,128)(2,1)S(1)} %get-tuple-element.19.top_ref), channel_id=1, source_target_pairs={{0,1},{1,2},{2,3},{3,4},{4,5},{5,6},{6,7},{7,8},{8,9},{9,10},{10,1... | collective-permute-start | bytes 3145736 | tf_op jit(solution)/shard_map/ppermute | solution.py:25
  32.1 15.9 %collective-permute-start.3 = (bf16[4,4,64,256]{3,2,1,0:T(8,128)(2,1)S(1)}, bf16[4,4,64,256]{3,2,1,0:T(8,128)(2,1)S(1)}, u32[]{:S(2)}, u32[]{:S(2)}) collective-permute-start(bf16[4,4,64,256]{3,2,1,0:T(8,128)(2,1)S(1)} %all_to_all.20), channel_id=1, source_target_pairs={{0,1},{1,2},{2,3},{3,4},{4,5},{5,6},{6,7},{7,8},{8,9},{9,10},{10,1... | collective-permute-start | bytes 1572872 | tf_op jit(solution)/shard_map/ppermute | solution.py:25
  48.0 40.9 %copy-start.4 = (f32[3]{0:T(128)S(1)}, f32[3]{0:T(128)}, u32[]{:S(2)}) copy-start(f32[3]{0:T(128)} %steps_ref.1) | copy-start | bytes 40
  58.6 30.3 %all-to-all-start.3 = ((f32[128,1,128]{2,1,0:T(1,128)}), f32[128,1,128]{2,1,0:T(1,128)S(1)}, u32[]{:S(2)}, u32[]{:S(2)}) async-start(f32[128,1,128]{2,1,0:T(1,128)} %get-tuple-element.33), calls=%async_computation.3 | async-start | bytes 131072 | tf_op jit(solution)/shard_map/all_to_all | solution.py:266
  77.5 5.9 %collective-permute-start.4 = (bf16[2,64,256]{2,1,0:T(8,128)(2,1)S(1)}, bf16[2,64,256]{2,1,0:T(8,128)(2,1)S(1)}, u32[]{:S(2)}, u32[]{:S(2)}) collective-permute-start(bf16[2,64,256]{2,1,0:T(8,128)(2,1)S(1)} %get-tuple-element.32), channel_id=1, source_target_pairs={{1,0},{2,1},{3,2},{4,3},{5,4},{6,5},{7,6},{8,7},{9,8},{10,9},{11,1... | collective-permute-start | bytes 196616 | tf_op jit(solution)/shard_map/ppermute | solution.py:25

commit v5 on v4

--- a/solution.py
+++ b/solution.py
@@ -12,7 +12,7 @@
 SMEM = pltpu.SMEM
 NT = (((1,), (1,)), ((), ()))
 MIB = 1024 * 1024
-CHUNKS = (64, 128, 64)
+CHUNKS = (64, 96, 96)
 
 
 def spec(space):
@@ -25,17 +25,18 @@
     return lax.ppermute(value, axis, pairs)
 
 
-def align_kernel(chunks, start_hbm, count_hbm, slab_ref, mid_ref, top_ref, low_ref, start_ref, count_ref, select_ref, sem):
+def align_kernel(
+    chunks, start_ref, count_ref, slab_hbm, mid_ref, top_ref, low_ref, slab_ref, select_ref, sem
+):
     _, auxb, _ = slab_ref.shape
     bf16 = jnp.bfloat16
-    small = [
-        pltpu.make_async_copy(source, target, sem.at[n])
-        for n, (source, target) in enumerate(((start_hbm, start_ref), (count_hbm, count_ref)))
+    begins = [sum(chunks[:n]) for n in range(len(chunks))]
+    loads = [
+        pltpu.make_async_copy(slab_hbm.at[pl.ds(begin, chunk)], slab_ref.at[pl.ds(begin, chunk)], sem.at[n])
+        for n, (begin, chunk) in enumerate(zip(begins, chunks))
     ]
-    for copy in small:
+    for copy in loads:
         copy.start()
-    for copy in small:
-        copy.wait()
     shift = start_ref[0] & 31
     count = count_ref[0]
     a = lax.broadcasted_iota(jnp.int32, (128, 256), 0)
@@ -43,12 +44,11 @@
     hit = (a < count) & (((a + shift) & 127) == ((to >> 6) << 5) + (to & 31))
     for m in range(2):
         select_ref[m * 128:(m + 1) * 128] = jnp.where(hit & (((to >> 5) & 1) == m), 1.0, 0.0).astype(bf16)
-    begin = 0
-    for chunk in chunks:
+    for load, begin, chunk in zip(loads, begins, chunks):
         first = (lax.broadcasted_iota(jnp.int32, (chunk, 128), 1) & 31) >= shift
         zero = jnp.zeros((chunk, 128), bf16)
         rows = slice(begin, begin + chunk)
-        begin += chunk
+        load.wait()
         by_function = jnp.swapaxes(slab_ref[rows], 0, 1)
         pairs = [jnp.concatenate([by_function[p], by_function[p + 1]], axis=1) for p in range(0, auxb, 2)]
         placed = jnp.dot(jnp.concatenate(pairs, axis=0), select_ref[...], preferred_element_type=jnp.float32)
@@ -75,16 +75,15 @@
     bf16 = jnp.bfloat16
     return pl.pallas_call(
         functools.partial(align_kernel, CHUNKS),
-        in_specs=[spec(pl.ANY)] * 2 + [spec(VMEM)],
+        in_specs=[spec(SMEM)] * 2 + [spec(pl.ANY)],
         out_specs=[spec(VMEM)] * 3,
         out_shape=[jax.ShapeDtypeStruct((groups, rows, depth), bf16) for groups in (2, 2, 3)],
         scratch_shapes=[
-            SMEM((1,), jnp.int32),
-            SMEM((1,), jnp.int32),
+            VMEM(slabs.shape, bf16),
             VMEM((256, 256), bf16),
-            pltpu.SemaphoreType.DMA((2,)),
+            pltpu.SemaphoreType.DMA((len(CHUNKS),)),
         ],
-        compiler_params=pltpu.CompilerParams(vmem_limit_bytes=24 * MIB),
+        compiler_params=pltpu.CompilerParams(vmem_limit_bytes=49 * MIB),
     )(start, count, slabs)
 
 
@@ -208,10 +207,8 @@
             total = jnp.where(chosen, tiles[k].astype(jnp.float32), total)
         tiles_ref[0, s] = total.astype(jnp.bfloat16)
     total = jnp.sum(energy_ref[...], axis=0)
-    first = total[0, 0]
-    second = total[0, 64]
-    for n in range(3):
-        out_ref[n] = -0.5 * (first + steps_ref[n] * second) * scale
+    first, second = total[:, :3], total[:, 64:67]
+    out_ref[...] = -0.5 * (first + steps_ref[...] * second) * scale
 
 
 def kernel_call(kernel, in_specs, out_shape, limit=16, out_specs=None):
@@ -266,12 +263,12 @@
     energy = lax.all_to_all(energy, "blk", 0, 0, tiled=True)
 
     scale = 1.0 / (rows * math.sqrt(blocks * slots))
-    return kernel_call(
+    tiles, energies = kernel_call(
         functools.partial(finish_kernel, scale),
-        [spec(SMEM)] * 2 + [spec(VMEM)] * 4,
-        [half(1, slots, part, rows), single(3)],
-        out_specs=[spec(VMEM), spec(SMEM)],
-    )(partners, step_lengths, t0, t2, odd, energy)
+        [spec(SMEM)] + [spec(VMEM)] * 5,
+        [half(1, slots, part, rows), single(1, 3)],
+    )(partners, step_lengths[None], t0, t2, odd, energy)
+    return tiles, energies[0]
 
 
 def solution(mesh):

time: 90.7 us -> 90 us (level)
  local copies, waits for them, and re-layouts: 1.6 us -> 0.02 us
    unnamed x10 -> x8, local copies, waits for them, and re-layouts: 1.6 us -> 0.02 us
where the time goes in v5:
time: 90 us; the launch traced here: 89.5 us
  starting transfers between devices  37.9 us (42%)
  blocking collectives  32.5 us (36%)
  waiting for transfers between devices  8.58 us (10%)
  Pallas kernels  8.41 us (9%)
  between operations  2.12 us (2%)
    ppermute x5, starting transfers between devices, moved_by(): return lax.ppermute(value, axis, pairs)  19 us
    all_to_all x1, starting transfers between devices, body(): energy = lax.all_to_all(energy, 'blk', 0, 0, tiled=True)  18.9 us
    all_to_all x1, blocking collectives, body(): even = lax.all_to_all(even, 'aux', 0, 0, tiled=True)  12.3 us
    all_to_all x1, blocking collectives, body(): odd = lax.all_to_all(odd, 'aux', 0, 0, tiled=True)  11.4 us
    all_to_all x1, blocking collectives, body(): far = lax.all_to_all(far, 'aux', 0, 0, tiled=True)  8.78 us
    all_to_all x1, waiting for transfers between devices, body(): energy = lax.all_to_all(energy, 'blk', 0, 0, tiled=True)  5.5 us
    ppermute x5, waiting for transfers between devices, moved_by(): return lax.ppermute(value, axis, pairs)  3.08 us
    pallas_call x1, Pallas kernels, align(): pl.pallas_call(functools.partial(align_kernel, CHUNKS), in_specs=[spec(SM...  2.87 us
  transfers between devices with their start and end apart: 6, of which 2 were waited for; matrix products, arithmetic and copies ran while one was open for 0% of the time, Pallas kernels for 3%

profile of v5, /device:TPU:1, one launch (start us, length us, event | category | flops | bytes accessed | tf_op | source)
XLA Modules:
  0.0 89.5 jit_solution(5659965780249854054)
XLA Ops:
  0.6 0.0 copy-start.1
  0.6 0.0 copy-start
  0.7 0.0 copy-start.2
  2.0 2.9 %shard_map.86 = (bf16[2,256,1024]{2,1,0:T(8,128)(2,1)S(1)}, bf16[2,256,1024]{2,1,0:T(8,128)(2,1)S(1)}, bf16[3,256,1024]{2,1,0:T(8,128)(2,1)S(1)}) custom-call(s32[1]{0:T(128)S(6)} %copy.9.start_ref, s32[1]{0:T(128)S(6)} %copy.10.count_ref, bf16[256,32,128]{2,1,0:T(8,128)(2,1)} %slab_hbm.1), custom_call_target="tpu_custom_call" | custom-call | tf_op jit(solution)/shard_map/pallas_call | solution.py:76
  4.9 1.3 %collective-permute-start.2 = (bf16[3,256,1024]{2,1,0:T(8,128)(2,1)S(1)}, bf16[3,256,1024]{2,1,0:T(8,128)(2,1)S(1)}, u32[]{:S(2)}, u32[]{:S(2)}) collective-permute-start(bf16[3,256,1024]{2,1,0:T(8,128)(2,1)S(1)} %get-tuple-element.23.low_ref), channel_id=1, source_target_pairs={{2,0},{3,1},{4,2},{5,3},{6,4},{7,5},{8,6},{9,7},{10,8},{11,9},{12,... | collective-permute-start | bytes 4718600 | tf_op jit(solution)/shard_map/ppermute | solution.py:25
  6.2 11.0 %collective-permute-start = (bf16[2,256,1024]{2,1,0:T(8,128)(2,1)S(1)}, bf16[2,256,1024]{2,1,0:T(8,128)(2,1)S(1)}, u32[]{:S(2)}, u32[]{:S(2)}) collective-permute-start(bf16[2,256,1024]{2,1,0:T(8,128)(2,1)S(1)} %get-tuple-element.20.mid_ref), channel_id=1, source_target_pairs={{0,1},{1,2},{2,3},{3,4},{4,5},{5,6},{6,7},{7,8},{8,9},{9,10},{10,1... | collective-permute-start | bytes 3145736 | tf_op jit(solution)/shard_map/ppermute | solution.py:25
  17.2 1.9 %collective-permute-start.1 = (bf16[2,256,1024]{2,1,0:T(8,128)(2,1)S(1)}, bf16[2,256,1024]{2,1,0:T(8,128)(2,1)S(1)}, u32[]{:S(2)}, u32[]{:S(2)}) collective-permute-start(bf16[2,256,1024]{2,1,0:T(8,128)(2,1)S(1)} %get-tuple-element.21.top_ref), channel_id=1, source_target_pairs={{0,1},{1,2},{2,3},{3,4},{4,5},{5,6},{6,7},{7,8},{8,9},{9,10},{10,1... | collective-permute-start | bytes 3145736 | tf_op jit(solution)/shard_map/ppermute | solution.py:25
  19.1 0.0 copy-done.1
  19.2 0.0 copy-done
  19.2 0.0 copy-done.2
  19.2 0.7 shard_map.87
  19.9 11.4 %all_to_all.20 = bf16[4,4,64,256]{3,2,1,0:T(8,128)(2,1)S(1)} all-to-all(bf16[4,4,64,256]{3,2,1,0:T(8,128)(2,1)S(1)} %get-tuple-element.30), channel_id=1, replica_groups=mesh['aux'=4,'blk'=128] {'aux'}, dimensions={0} | all-to-all | bytes 1048576 | tf_op jit(solution)/shard_map/all_to_all | solution.py:245
  31.3 1.9 %collective-permute-start.3 = (bf16[4,4,64,256]{3,2,1,0:T(8,128)(2,1)S(1)}, bf16[4,4,64,256]{3,2,1,0:T(8,128)(2,1)S(1)}, u32[]{:S(2)}, u32[]{:S(2)}) collective-permute-start(bf16[4,4,64,256]{3,2,1,0:T(8,128)(2,1)S(1)} %all_to_all.20), channel_id=1, source_target_pairs={{0,1},{1,2},{2,3},{3,4},{4,5},{5,6},{6,7},{7,8},{8,9},{9,10},{10,1... | collective-permute-start | bytes 1572872 | tf_op jit(solution)/shard_map/ppermute | solution.py:25
  33.3 0.9 shard_map.88
  34.1 12.3 %all_to_all.21.even_ref = bf16[4,5,64,256]{3,2,1,0:T(8,128)(2,1)S(1)} all-to-all(bf16[4,5,64,256]{3,2,1,0:T(8,128)(2,1)S(1)} %get-tuple-element.28), channel_id=1, replica_groups=mesh['aux'=4,'blk'=128] {'aux'}, dimensions={0} | all-to-all | bytes 1310720 | tf_op jit(solution)/shard_map/all_to_all | solution.py:251
  46.5 0.0 collective-permute-done.before_mid_ref
  46.5 0.0 collective-permute-done.1.before_top_ref.before_ref
  46.5 0.8 shard_map.89
  47.3 0.0 collective-permute-done.3.odd_ref
  47.3 0.0 collective-permute-done.2.after_ref
  47.3 0.0 copy-start.3
  47.3 1.1 %shard_map.90 = bf16[4,208,256]{2,1,0:T(8,128)(2,1)S(1)} custom-call(bf16[2,256,1024]{2,1,0:T(8,128)(2,1)S(1)} %get-tuple-element.20.mid_ref, bf16[2,256,1024]{2,1,0:T(8,128)(2,1)S(1)} %get-tuple-element.21.top_ref, bf16[2,256,1024]{2,1,0:T(8,128)(2,1)S(1)} %collective-permute-done.1.before_top_ref.before_ref, ...), custom_call_target="tpu_custom_call" | custom-call | tf_op jit(solution)/shard_map/pallas_call | solution.py:255
  48.4 8.8 %all_to_all.22.parts_ref = bf16[4,208,256]{2,1,0:T(8,128)(2,1)S(1)} all-to-all(bf16[4,208,256]{2,1,0:T(8,128)(2,1)S(1)} %shard_map.90), channel_id=1, replica_groups=mesh['aux'=4,'blk'=128] {'aux'}, dimensions={0} | all-to-all | bytes 851968 | tf_op jit(solution)/shard_map/all_to_all | solution.py:258
  57.2 0.7 shard_map.91
  57.9 18.9 %all-to-all-start.3 = ((f32[128,1,128]{2,1,0:T(1,128)}), f32[128,1,128]{2,1,0:T(1,128)S(1)}, u32[]{:S(2)}, u32[]{:S(2)}) async-start(f32[128,1,128]{2,1,0:T(1,128)} %get-tuple-element.35), calls=%async_computation.3 | async-start | bytes 131072 | tf_op jit(solution)/shard_map/all_to_all | solution.py:263
  76.8 2.8 %collective-permute-start.4 = (bf16[2,64,256]{2,1,0:T(8,128)(2,1)S(1)}, bf16[2,64,256]{2,1,0:T(8,128)(2,1)S(1)}, u32[]{:S(2)}, u32[]{:S(2)}) collective-permute-start(bf16[2,64,256]{2,1,0:T(8,128)(2,1)S(1)} %get-tuple-element.34), channel_id=1, source_target_pairs={{1,0},{2,1},{3,2},{4,3},{5,4},{6,5},{7,6},{8,7},{9,8},{10,9},{11,1... | collective-permute-start | bytes 196616 | tf_op jit(solution)/shard_map/ppermute | solution.py:25
  79.6 3.1 %collective-permute-done.4.odd_ref = bf16[2,64,256]{2,1,0:T(8,128)(2,1)S(1)} collective-permute-done((bf16[2,64,256]{2,1,0:T(8,128)(2,1)S(1)}, bf16[2,64,256]{2,1,0:T(8,128)(2,1)S(1)}, u32[]{:S(2)}, u32[]{:S(2)}) %collective-permute-start.4) | collective-permute-done | bytes 65568 | tf_op jit(solution)/shard_map/ppermute | solution.py:25
  82.7 5.5 %all-to-all-done.3.energy_ref = f32[128,1,128]{2,1,0:T(1,128)S(1)} async-done(((f32[128,1,128]{2,1,0:T(1,128)}), f32[128,1,128]{2,1,0:T(1,128)S(1)}, u32[]{:S(2)}, u32[]{:S(2)}) %all-to-all-start.3) | async-done | bytes 65568 | tf_op jit(solution)/shard_map/all_to_all | solution.py:263
  88.2 0.0 copy-done.3
  88.2 1.4 %shard_map.92 = (bf16[1,4,64,256]{3,2,1,0:T(8,128)(2,1)}, f32[1,3]{1,0:T(1,128)}) custom-call(s32[1,4]{1,0:T(1,128)S(1)} %copy-done.2, f32[1,3]{1,0:T(1,128)S(1)} %bitcast.2, bf16[64,256]{1,0:T(8,128)(2,1)S(1)} %get-tuple-element.29.t0_ref, bf16[64,256]{1,0:T(8,128)(2,1)S(1)} %get-tuple-element.33.t2_ref, ...), custom_call_target="tpu_custom_call" | custom-call | tf_op jit(solution)/shard_map/pallas_call | solution.py:266
Async XLA Ops:
  0.6 18.5 %copy-start.1 = (bf16[1,4,64,256]{3,2,1,0:T(8,128)(2,1)S(1)}, bf16[1,4,64,256]{3,2,1,0:T(8,128)(2,1)}, u32[]{:S(2)}) copy-start(bf16[1,4,64,256]{3,2,1,0:T(8,128)(2,1)} %direction_ref) | copy-start | bytes 393220
  0.6 18.5 %copy-start = (bf16[1,4,64,256]{3,2,1,0:T(8,128)(2,1)S(1)}, bf16[1,4,64,256]{3,2,1,0:T(8,128)(2,1)}, u32[]{:S(2)}) copy-start(bf16[1,4,64,256]{3,2,1,0:T(8,128)(2,1)} %density_ref) | copy-start | bytes 393220
  0.7 18.5 %copy-start.2 = (s32[1,4]{1,0:T(1,128)S(1)}, s32[1,4]{1,0:T(1,128)}, u32[]{:S(2)}) copy-start(s32[1,4]{1,0:T(1,128)} %row_ref.3) | copy-start | bytes 52
  4.9 42.4 %collective-permute-start.2 = (bf16[3,256,1024]{2,1,0:T(8,128)(2,1)S(1)}, bf16[3,256,1024]{2,1,0:T(8,128)(2,1)S(1)}, u32[]{:S(2)}, u32[]{:S(2)}) collective-permute-start(bf16[3,256,1024]{2,1,0:T(8,128)(2,1)S(1)} %get-tuple-element.23.low_ref), channel_id=1, source_target_pairs={{2,0},{3,1},{4,2},{5,3},{6,4},{7,5},{8,6},{9,7},{10,8},{11,9},{12,... | collective-permute-start | bytes 4718600 | tf_op jit(solution)/shard_map/ppermute | solution.py:25
  6.2 40.3 %collective-permute-start = (bf16[2,256,1024]{2,1,0:T(8,128)(2,1)S(1)}, bf16[2,256,1024]{2,1,0:T(8,128)(2,1)S(1)}, u32[]{:S(2)}, u32[]{:S(2)}) collective-permute-start(bf16[2,256,1024]{2,1,0:T(8,128)(2,1)S(1)} %get-tuple-element.20.mid_ref), channel_id=1, source_target_pairs={{0,1},{1,2},{2,3},{3,4},{4,5},{5,6},{6,7},{7,8},{8,9},{9,10},{10,1... | collective-permute-start | bytes 3145736 | tf_op jit(solution)/shard_map/ppermute | solution.py:25
  17.2 29.3 %collective-permute-start.1 = (bf16[2,256,1024]{2,1,0:T(8,128)(2,1)S(1)}, bf16[2,256,1024]{2,1,0:T(8,128)(2,1)S(1)}, u32[]{:S(2)}, u32[]{:S(2)}) collective-permute-start(bf16[2,256,1024]{2,1,0:T(8,128)(2,1)S(1)} %get-tuple-element.21.top_ref), channel_id=1, source_target_pairs={{0,1},{1,2},{2,3},{3,4},{4,5},{5,6},{6,7},{7,8},{8,9},{9,10},{10,1... | collective-permute-start | bytes 3145736 | tf_op jit(solution)/shard_map/ppermute | solution.py:25
  31.3 15.9 %collective-permute-start.3 = (bf16[4,4,64,256]{3,2,1,0:T(8,128)(2,1)S(1)}, bf16[4,4,64,256]{3,2,1,0:T(8,128)(2,1)S(1)}, u32[]{:S(2)}, u32[]{:S(2)}) collective-permute-start(bf16[4,4,64,256]{3,2,1,0:T(8,128)(2,1)S(1)} %all_to_all.20), channel_id=1, source_target_pairs={{0,1},{1,2},{2,3},{3,4},{4,5},{5,6},{6,7},{7,8},{8,9},{9,10},{10,1... | collective-permute-start | bytes 1572872 | tf_op jit(solution)/shard_map/ppermute | solution.py:25
  47.3 40.9 %copy-start.3 = (f32[3]{0:T(128)S(1)}, f32[3]{0:T(128)}, u32[]{:S(2)}) copy-start(f32[3]{0:T(128)} %param.13) | copy-start | bytes 40
  57.9 30.3 %all-to-all-start.3 = ((f32[128,1,128]{2,1,0:T(1,128)}), f32[128,1,128]{2,1,0:T(1,128)S(1)}, u32[]{:S(2)}, u32[]{:S(2)}) async-start(f32[128,1,128]{2,1,0:T(1,128)} %get-tuple-element.35), calls=%async_computation.3 | async-start | bytes 131072 | tf_op jit(solution)/shard_map/all_to_all | solution.py:263
  76.8 5.9 %collective-permute-start.4 = (bf16[2,64,256]{2,1,0:T(8,128)(2,1)S(1)}, bf16[2,64,256]{2,1,0:T(8,128)(2,1)S(1)}, u32[]{:S(2)}, u32[]{:S(2)}) collective-permute-start(bf16[2,64,256]{2,1,0:T(8,128)(2,1)S(1)} %get-tuple-element.34), channel_id=1, source_target_pairs={{1,0},{2,1},{3,2},{4,3},{5,4},{6,5},{7,6},{8,7},{9,8},{10,9},{11,1... | collective-permute-start | bytes 196616 | tf_op jit(solution)/shard_map/ppermute | solution.py:25

commit v6 on v5

--- a/solution.py
+++ b/solution.py
@@ -98,12 +98,11 @@
                 weight = jnp.where((other >= 0) & (other - block == k), full, 0.0)
                 total = total + weight * source[0, s].astype(jnp.float32)
             total = total.astype(jnp.bfloat16)
-            place = k // 2 * 2 + which
             if k % 2 == 0:
-                even_ref[place] = total
+                even_ref[k // 2 * 2 + which] = total
             else:
                 for to in range(4):
-                    odd_ref[to, place] = total
+                    odd_ref[to, k // 2 * 2 + which] = total
 
 
 def product(left, right):
@@ -126,26 +125,29 @@
     return parts
 
 
-def own_kernel(mid_ref, top_ref, low_ref, even_ref, tile_ref, out_ref):
+def own_kernel(mid_ref, top_ref, low_ref, even_ref, out_ref):
     own = [low_ref[0], mid_ref[0], mid_ref[1], top_ref[0], top_ref[1]]
     tile = product(own, own)
-    tile_ref[...] = tile
+    high = tile.astype(jnp.bfloat16)
+    rest = (tile - high.astype(jnp.float32)).astype(jnp.bfloat16)
     for to in range(4):
-        out_ref[to, 0:4] = even_ref[...]
-        out_ref[to, 4] = tile[to * 64:(to + 1) * 64].astype(jnp.bfloat16)
-
-
-def near_kernel(mid_ref, top_ref, low_ref, before_mid_ref, before_top_ref, tile_ref, even_ref, out_ref, own_ref, sums_ref):
+        part = slice(to * 64, (to + 1) * 64)
+        out_ref[to, 0] = even_ref[2]
+        out_ref[to, 1] = even_ref[3]
+        out_ref[to, 2] = high[part]
+        out_ref[to, 3] = rest[part]
+
+
+def near_kernel(mid_ref, top_ref, low_ref, before_mid_ref, before_top_ref, even_ref, local_ref, out_ref, own_ref, sums_ref):
     own = [low_ref[0], mid_ref[0], mid_ref[1], top_ref[0]]
     before = [before_mid_ref[0], before_mid_ref[1], before_top_ref[0], before_top_ref[1]]
     out_ref[...] = product(before, own)
-    sums = tile_sums(tile_ref, 0, even_ref)
+    total = even_ref[0, 2].astype(jnp.float32) + even_ref[0, 3].astype(jnp.float32)
+    for source in range(1, 4):
+        total = total + even_ref[source, 2].astype(jnp.float32) + even_ref[source, 3].astype(jnp.float32)
+    own_ref[...] = total.astype(jnp.bfloat16)
     for which in range(2):
-        sums_ref[which] = sums[which]
-    total = even_ref[0, 4].astype(jnp.float32)
-    for source in range(1, 4):
-        total = total + even_ref[source, 4].astype(jnp.float32)
-    own_ref[...] = total.astype(jnp.bfloat16)
+        sums_ref[which] = jnp.sum((local_ref[which].astype(jnp.float32) * total).reshape(8, 8, 256), axis=0)
 
 
 def far_kernel(mid_ref, top_ref, before_ref, after_ref, even_ref, odd_ref, near_ref, sums_in_ref, out_ref):
@@ -153,7 +155,7 @@
     t2 = product([mid_ref[1], top_ref[0], top_ref[1]], after)
     t3 = product([before_ref[q] for q in range(2)], after)
     sums = [sums_in_ref[0], sums_in_ref[1]]
-    for tile, place, weights_ref in ((near_ref, 0, odd_ref), (t2, 1, even_ref), (t3, 1, odd_ref)):
+    for tile, place, weights_ref in ((near_ref, 0, odd_ref), (t2, 0, even_ref), (t3, 1, odd_ref)):
         sums = [a + b for a, b in zip(sums, tile_sums(tile, place, weights_ref))]
     for to in range(4):
         part = slice(to * 64, (to + 1) * 64)
@@ -245,13 +247,12 @@
     odd = lax.all_to_all(odd, "aux", 0, 0, tiled=True)
     odd = moved_by(odd, "blk", 1)
 
-    t0, even = kernel_call(own_kernel, [spec(VMEM)] * 4, [single(rows, rows), half(aux, 5, part, rows)])(
-        mid, top, low, even
-    )
+    local = even
+    (even,) = kernel_call(own_kernel, [spec(VMEM)] * 4, [half(aux, 4, part, rows)])(mid, top, low, local)
     even = lax.all_to_all(even, "aux", 0, 0, tiled=True)
     t1, t0, sums = kernel_call(
         near_kernel, [spec(VMEM)] * 7, [single(rows, rows), half(part, rows), single(2, 8, rows)]
-    )(mid, top, low, before_mid, before_top, t0, even)
+    )(mid, top, low, before_mid, before_top, even, local)
     (far,) = kernel_call(far_kernel, [spec(VMEM)] * 8, [half(aux, 3 * part + 16, rows)])(
         mid, top, before_top, after, even, odd, t1, sums
     )

time: 90 us -> 88.5 us (0.983)
  blocking collectives: 32.5 us -> 31.1 us
    all_to_all x1, blocking collectives: 12.3 us -> 10.9 us  [body(): even = lax.all_to_all(even, 'aux', 0, 0, tiled=True)]
where the time goes in v6:
time: 88.5 us; the launch traced here: 88.1 us
  starting transfers between devices  37.9 us (43%)
  blocking collectives  31.1 us (35%)
  waiting for transfers between devices  8.58 us (10%)
  Pallas kernels  8.41 us (10%)
  between operations  2.12 us (2%)
    ppermute x5, starting transfers between devices, moved_by(): return lax.ppermute(value, axis, pairs)  19 us
    all_to_all x1, starting transfers between devices, body(): energy = lax.all_to_all(energy, 'blk', 0, 0, tiled=True)  18.9 us
    all_to_all x1, blocking collectives, body(): odd = lax.all_to_all(odd, 'aux', 0, 0, tiled=True)  11.4 us
    all_to_all x1, blocking collectives, body(): even = lax.all_to_all(even, 'aux', 0, 0, tiled=True)  10.9 us
    all_to_all x1, blocking collectives, body(): far = lax.all_to_all(far, 'aux', 0, 0, tiled=True)  8.78 us
    all_to_all x1, waiting for transfers between devices, body(): energy = lax.all_to_all(energy, 'blk', 0, 0, tiled=True)  5.5 us
    ppermute x5, waiting for transfers between devices, moved_by(): return lax.ppermute(value, axis, pairs)  3.08 us
    pallas_call x1, Pallas kernels, align(): pl.pallas_call(functools.partial(align_kernel, CHUNKS), in_specs=[spec(SM...  2.87 us
  transfers between devices with their start and end apart: 6, of which 2 were waited for; matrix products, arithmetic and copies ran while one was open for 0% of the time, Pallas kernels for 3%

profile of v6, /device:TPU:1, one launch (start us, length us, event | category | flops | bytes accessed | tf_op | source)
XLA Modules:
  0.0 88.1 jit_solution(5879302373294204950)
XLA Ops:
  0.6 0.0 copy-start.1
  0.6 0.0 copy-start
  0.7 0.0 copy-start.2
  2.0 2.9 %shard_map.86 = (bf16[2,256,1024]{2,1,0:T(8,128)(2,1)S(1)}, bf16[2,256,1024]{2,1,0:T(8,128)(2,1)S(1)}, bf16[3,256,1024]{2,1,0:T(8,128)(2,1)S(1)}) custom-call(s32[1]{0:T(128)S(6)} %copy.9.start_ref, s32[1]{0:T(128)S(6)} %copy.10.count_ref, bf16[256,32,128]{2,1,0:T(8,128)(2,1)} %slab_hbm.1), custom_call_target="tpu_custom_call" | custom-call | tf_op jit(solution)/shard_map/pallas_call | solution.py:76
  4.9 1.3 %collective-permute-start.2 = (bf16[3,256,1024]{2,1,0:T(8,128)(2,1)S(1)}, bf16[3,256,1024]{2,1,0:T(8,128)(2,1)S(1)}, u32[]{:S(2)}, u32[]{:S(2)}) collective-permute-start(bf16[3,256,1024]{2,1,0:T(8,128)(2,1)S(1)} %get-tuple-element.21.low_ref), channel_id=1, source_target_pairs={{2,0},{3,1},{4,2},{5,3},{6,4},{7,5},{8,6},{9,7},{10,8},{11,9},{12,... | collective-permute-start | bytes 4718600 | tf_op jit(solution)/shard_map/ppermute | solution.py:25
  6.2 11.0 %collective-permute-start = (bf16[2,256,1024]{2,1,0:T(8,128)(2,1)S(1)}, bf16[2,256,1024]{2,1,0:T(8,128)(2,1)S(1)}, u32[]{:S(2)}, u32[]{:S(2)}) collective-permute-start(bf16[2,256,1024]{2,1,0:T(8,128)(2,1)S(1)} %get-tuple-element.18.mid_ref), channel_id=1, source_target_pairs={{0,1},{1,2},{2,3},{3,4},{4,5},{5,6},{6,7},{7,8},{8,9},{9,10},{10,1... | collective-permute-start | bytes 3145736 | tf_op jit(solution)/shard_map/ppermute | solution.py:25
  17.2 1.9 %collective-permute-start.1 = (bf16[2,256,1024]{2,1,0:T(8,128)(2,1)S(1)}, bf16[2,256,1024]{2,1,0:T(8,128)(2,1)S(1)}, u32[]{:S(2)}, u32[]{:S(2)}) collective-permute-start(bf16[2,256,1024]{2,1,0:T(8,128)(2,1)S(1)} %get-tuple-element.19.top_ref), channel_id=1, source_target_pairs={{0,1},{1,2},{2,3},{3,4},{4,5},{5,6},{6,7},{7,8},{8,9},{9,10},{10,1... | collective-permute-start | bytes 3145736 | tf_op jit(solution)/shard_map/ppermute | solution.py:25
  19.1 0.0 copy-done.1
  19.2 0.0 copy-done
  19.2 0.0 copy-done.2
  19.2 0.7 shard_map.87
  19.9 11.4 %all_to_all.20 = bf16[4,4,64,256]{3,2,1,0:T(8,128)(2,1)S(1)} all-to-all(bf16[4,4,64,256]{3,2,1,0:T(8,128)(2,1)S(1)} %get-tuple-element.26), channel_id=1, replica_groups=mesh['aux'=4,'blk'=128] {'aux'}, dimensions={0} | all-to-all | bytes 1048576 | tf_op jit(solution)/shard_map/all_to_all | solution.py:247
  31.3 1.9 %collective-permute-start.3 = (bf16[4,4,64,256]{3,2,1,0:T(8,128)(2,1)S(1)}, bf16[4,4,64,256]{3,2,1,0:T(8,128)(2,1)S(1)}, u32[]{:S(2)}, u32[]{:S(2)}) collective-permute-start(bf16[4,4,64,256]{3,2,1,0:T(8,128)(2,1)S(1)} %all_to_all.20), channel_id=1, source_target_pairs={{0,1},{1,2},{2,3},{3,4},{4,5},{5,6},{6,7},{7,8},{8,9},{9,10},{10,1... | collective-permute-start | bytes 1572872 | tf_op jit(solution)/shard_map/ppermute | solution.py:25
  33.3 0.9 shard_map.88
  34.1 10.9 %all_to_all.21.even_ref = bf16[4,4,64,256]{3,2,1,0:T(8,128)(2,1)S(1)} all-to-all(bf16[4,4,64,256]{3,2,1,0:T(8,128)(2,1)S(1)} %shard_map.88), channel_id=1, replica_groups=mesh['aux'=4,'blk'=128] {'aux'}, dimensions={0} | all-to-all | bytes 1048576 | tf_op jit(solution)/shard_map/all_to_all | solution.py:252
  45.1 0.0 collective-permute-done.before_mid_ref
  45.1 0.0 collective-permute-done.1.before_top_ref.before_ref
  45.1 0.8 shard_map.89
  45.8 0.0 collective-permute-done.3.odd_ref
  45.9 0.0 collective-permute-done.2.after_ref
  45.9 0.0 copy-start.3
  45.9 1.1 %shard_map.90 = bf16[4,208,256]{2,1,0:T(8,128)(2,1)S(1)} custom-call(bf16[2,256,1024]{2,1,0:T(8,128)(2,1)S(1)} %get-tuple-element.18.mid_ref, bf16[2,256,1024]{2,1,0:T(8,128)(2,1)S(1)} %get-tuple-element.19.top_ref, bf16[2,256,1024]{2,1,0:T(8,128)(2,1)S(1)} %collective-permute-done.1.before_top_ref.before_ref, ...), custom_call_target="tpu_custom_call" | custom-call | tf_op jit(solution)/shard_map/pallas_call | solution.py:256
  47.0 8.8 %all_to_all.22.parts_ref = bf16[4,208,256]{2,1,0:T(8,128)(2,1)S(1)} all-to-all(bf16[4,208,256]{2,1,0:T(8,128)(2,1)S(1)} %shard_map.90), channel_id=1, replica_groups=mesh['aux'=4,'blk'=128] {'aux'}, dimensions={0} | all-to-all | bytes 851968 | tf_op jit(solution)/shard_map/all_to_all | solution.py:259
  55.8 0.7 shard_map.91
  56.5 18.9 %all-to-all-start.3 = ((f32[128,1,128]{2,1,0:T(1,128)}), f32[128,1,128]{2,1,0:T(1,128)S(1)}, u32[]{:S(2)}, u32[]{:S(2)}) async-start(f32[128,1,128]{2,1,0:T(1,128)} %get-tuple-element.31), calls=%async_computation.3 | async-start | bytes 131072 | tf_op jit(solution)/shard_map/all_to_all | solution.py:264
  75.4 2.8 %collective-permute-start.4 = (bf16[2,64,256]{2,1,0:T(8,128)(2,1)S(1)}, bf16[2,64,256]{2,1,0:T(8,128)(2,1)S(1)}, u32[]{:S(2)}, u32[]{:S(2)}) collective-permute-start(bf16[2,64,256]{2,1,0:T(8,128)(2,1)S(1)} %get-tuple-element.30), channel_id=1, source_target_pairs={{1,0},{2,1},{3,2},{4,3},{5,4},{6,5},{7,6},{8,7},{9,8},{10,9},{11,1... | collective-permute-start | bytes 196616 | tf_op jit(solution)/shard_map/ppermute | solution.py:25
  78.2 3.1 %collective-permute-done.4.odd_ref = bf16[2,64,256]{2,1,0:T(8,128)(2,1)S(1)} collective-permute-done((bf16[2,64,256]{2,1,0:T(8,128)(2,1)S(1)}, bf16[2,64,256]{2,1,0:T(8,128)(2,1)S(1)}, u32[]{:S(2)}, u32[]{:S(2)}) %collective-permute-start.4) | collective-permute-done | bytes 65568 | tf_op jit(solution)/shard_map/ppermute | solution.py:25
  81.3 5.5 %all-to-all-done.3.energy_ref = f32[128,1,128]{2,1,0:T(1,128)S(1)} async-done(((f32[128,1,128]{2,1,0:T(1,128)}), f32[128,1,128]{2,1,0:T(1,128)S(1)}, u32[]{:S(2)}, u32[]{:S(2)}) %all-to-all-start.3) | async-done | bytes 65568 | tf_op jit(solution)/shard_map/all_to_all | solution.py:264
  86.8 0.0 copy-done.3
  86.8 1.4 %shard_map.92 = (bf16[1,4,64,256]{3,2,1,0:T(8,128)(2,1)}, f32[1,3]{1,0:T(1,128)}) custom-call(s32[1,4]{1,0:T(1,128)S(1)} %copy-done.2, f32[1,3]{1,0:T(1,128)S(1)} %bitcast.2, bf16[64,256]{1,0:T(8,128)(2,1)S(1)} %get-tuple-element.25.t0_ref, bf16[64,256]{1,0:T(8,128)(2,1)S(1)} %get-tuple-element.29.t2_ref, ...), custom_call_target="tpu_custom_call" | custom-call | tf_op jit(solution)/shard_map/pallas_call | solution.py:267
Async XLA Ops:
  0.6 18.5 %copy-start.1 = (bf16[1,4,64,256]{3,2,1,0:T(8,128)(2,1)S(1)}, bf16[1,4,64,256]{3,2,1,0:T(8,128)(2,1)}, u32[]{:S(2)}) copy-start(bf16[1,4,64,256]{3,2,1,0:T(8,128)(2,1)} %direction_ref) | copy-start | bytes 393220
  0.6 18.5 %copy-start = (bf16[1,4,64,256]{3,2,1,0:T(8,128)(2,1)S(1)}, bf16[1,4,64,256]{3,2,1,0:T(8,128)(2,1)}, u32[]{:S(2)}) copy-start(bf16[1,4,64,256]{3,2,1,0:T(8,128)(2,1)} %density_ref) | copy-start | bytes 393220
  0.7 18.5 %copy-start.2 = (s32[1,4]{1,0:T(1,128)S(1)}, s32[1,4]{1,0:T(1,128)}, u32[]{:S(2)}) copy-start(s32[1,4]{1,0:T(1,128)} %row_ref.3) | copy-start | bytes 52
  4.9 41.0 %collective-permute-start.2 = (bf16[3,256,1024]{2,1,0:T(8,128)(2,1)S(1)}, bf16[3,256,1024]{2,1,0:T(8,128)(2,1)S(1)}, u32[]{:S(2)}, u32[]{:S(2)}) collective-permute-start(bf16[3,256,1024]{2,1,0:T(8,128)(2,1)S(1)} %get-tuple-element.21.low_ref), channel_id=1, source_target_pairs={{2,0},{3,1},{4,2},{5,3},{6,4},{7,5},{8,6},{9,7},{10,8},{11,9},{12,... | collective-permute-start | bytes 4718600 | tf_op jit(solution)/shard_map/ppermute | solution.py:25
  6.2 38.9 %collective-permute-start = (bf16[2,256,1024]{2,1,0:T(8,128)(2,1)S(1)}, bf16[2,256,1024]{2,1,0:T(8,128)(2,1)S(1)}, u32[]{:S(2)}, u32[]{:S(2)}) collective-permute-start(bf16[2,256,1024]{2,1,0:T(8,128)(2,1)S(1)} %get-tuple-element.18.mid_ref), channel_id=1, source_target_pairs={{0,1},{1,2},{2,3},{3,4},{4,5},{5,6},{6,7},{7,8},{8,9},{9,10},{10,1... | collective-permute-start | bytes 3145736 | tf_op jit(solution)/shard_map/ppermute | solution.py:25
  17.2 27.9 %collective-permute-start.1 = (bf16[2,256,1024]{2,1,0:T(8,128)(2,1)S(1)}, bf16[2,256,1024]{2,1,0:T(8,128)(2,1)S(1)}, u32[]{:S(2)}, u32[]{:S(2)}) collective-permute-start(bf16[2,256,1024]{2,1,0:T(8,128)(2,1)S(1)} %get-tuple-element.19.top_ref), channel_id=1, source_target_pairs={{0,1},{1,2},{2,3},{3,4},{4,5},{5,6},{6,7},{7,8},{8,9},{9,10},{10,1... | collective-permute-start | bytes 3145736 | tf_op jit(solution)/shard_map/ppermute | solution.py:25
  31.3 14.5 %collective-permute-start.3 = (bf16[4,4,64,256]{3,2,1,0:T(8,128)(2,1)S(1)}, bf16[4,4,64,256]{3,2,1,0:T(8,128)(2,1)S(1)}, u32[]{:S(2)}, u32[]{:S(2)}) collective-permute-start(bf16[4,4,64,256]{3,2,1,0:T(8,128)(2,1)S(1)} %all_to_all.20), channel_id=1, source_target_pairs={{0,1},{1,2},{2,3},{3,4},{4,5},{5,6},{6,7},{7,8},{8,9},{9,10},{10,1... | collective-permute-start | bytes 1572872 | tf_op jit(solution)/shard_map/ppermute | solution.py:25
  45.9 40.9 %copy-start.3 = (f32[3]{0:T(128)S(1)}, f32[3]{0:T(128)}, u32[]{:S(2)}) copy-start(f32[3]{0:T(128)} %param.13) | copy-start | bytes 40
  56.5 30.3 %all-to-all-start.3 = ((f32[128,1,128]{2,1,0:T(1,128)}), f32[128,1,128]{2,1,0:T(1,128)S(1)}, u32[]{:S(2)}, u32[]{:S(2)}) async-start(f32[128,1,128]{2,1,0:T(1,128)} %get-tuple-element.31), calls=%async_computation.3 | async-start | bytes 131072 | tf_op jit(solution)/shard_map/all_to_all | solution.py:264
  75.4 5.9 %collective-permute-start.4 = (bf16[2,64,256]{2,1,0:T(8,128)(2,1)S(1)}, bf16[2,64,256]{2,1,0:T(8,128)(2,1)S(1)}, u32[]{:S(2)}, u32[]{:S(2)}) collective-permute-start(bf16[2,64,256]{2,1,0:T(8,128)(2,1)S(1)} %get-tuple-element.30), channel_id=1, source_target_pairs={{1,0},{2,1},{3,2},{4,3},{5,4},{6,5},{7,6},{8,7},{9,8},{10,9},{11,1... | collective-permute-start | bytes 196616 | tf_op jit(solution)/shard_map/ppermute | solution.py:25

commit v7 on v6

--- a/solution.py
+++ b/solution.py
@@ -87,7 +87,27 @@
     )(start, count, slabs)
 
 
-def by_offset_kernel(row_ref, density_ref, direction_ref, even_ref, odd_ref):
+def product(left, right):
+    total = None
+    for a, b in zip(left, right):
+        term = lax.dot_general(a, b, NT, preferred_element_type=jnp.float32)
+        total = term if total is None else total + term
+    return total
+
+
+def tile_sums(tile, place, weights_ref):
+    parts = []
+    for which in range(2):
+        total = jnp.zeros((8, 256), jnp.float32)
+        for source in range(4):
+            weight = weights_ref[source, place * 2 + which].astype(jnp.float32)
+            piece = weight * tile[source * 64:(source + 1) * 64]
+            total = total + jnp.sum(piece.reshape(8, 8, 256), axis=0)
+        parts.append(total)
+    return parts
+
+
+def own_kernel(row_ref, density_ref, direction_ref, mid_ref, top_ref, low_ref, local_ref, odd_ref, even_ref):
     block = row_ref[0, 0]
     for k in range(4):
         for which, source in enumerate((density_ref, direction_ref)):
@@ -98,44 +118,22 @@
                 weight = jnp.where((other >= 0) & (other - block == k), full, 0.0)
                 total = total + weight * source[0, s].astype(jnp.float32)
             total = total.astype(jnp.bfloat16)
-            if k % 2 == 0:
-                even_ref[k // 2 * 2 + which] = total
-            else:
-                for to in range(4):
+            if k == 0:
+                local_ref[which] = total
+                continue
+            for to in range(4):
+                if k == 2:
+                    even_ref[to, which] = total
+                else:
                     odd_ref[to, k // 2 * 2 + which] = total
-
-
-def product(left, right):
-    total = None
-    for a, b in zip(left, right):
-        term = lax.dot_general(a, b, NT, preferred_element_type=jnp.float32)
-        total = term if total is None else total + term
-    return total
-
-
-def tile_sums(tile, place, weights_ref):
-    parts = []
-    for which in range(2):
-        total = jnp.zeros((8, 256), jnp.float32)
-        for source in range(4):
-            weight = weights_ref[source, place * 2 + which].astype(jnp.float32)
-            piece = weight * tile[source * 64:(source + 1) * 64]
-            total = total + jnp.sum(piece.reshape(8, 8, 256), axis=0)
-        parts.append(total)
-    return parts
-
-
-def own_kernel(mid_ref, top_ref, low_ref, even_ref, out_ref):
     own = [low_ref[0], mid_ref[0], mid_ref[1], top_ref[0], top_ref[1]]
     tile = product(own, own)
     high = tile.astype(jnp.bfloat16)
     rest = (tile - high.astype(jnp.float32)).astype(jnp.bfloat16)
     for to in range(4):
         part = slice(to * 64, (to + 1) * 64)
-        out_ref[to, 0] = even_ref[2]
-        out_ref[to, 1] = even_ref[3]
-        out_ref[to, 2] = high[part]
-        out_ref[to, 3] = rest[part]
+        even_ref[to, 2] = high[part]
+        even_ref[to, 3] = rest[part]
 
 
 def near_kernel(mid_ref, top_ref, low_ref, before_mid_ref, before_top_ref, even_ref, local_ref, out_ref, own_ref, sums_ref):
@@ -240,15 +238,14 @@
     after = moved_by(low, "blk", -2)
     before_mid = moved_by(mid, "blk", 1)
     before_top = moved_by(top, "blk", 1)
-    low, density, direction = lax.optimization_barrier((low, density, direction))
-    even, odd = kernel_call(by_offset_kernel, [spec(SMEM)] + [spec(VMEM)] * 2, [half(4, part, rows), half(aux, 4, part, rows)])(
-        partners, density, direction
-    )
+    local, odd, even = kernel_call(
+        own_kernel,
+        [spec(SMEM)] + [spec(VMEM)] * 5,
+        [half(2, part, rows), half(aux, 4, part, rows), half(aux, 4, part, rows)],
+    )(partners, density, direction, mid, top, low)
     odd = lax.all_to_all(odd, "aux", 0, 0, tiled=True)
     odd = moved_by(odd, "blk", 1)
 
-    local = even
-    (even,) = kernel_call(own_kernel, [spec(VMEM)] * 4, [half(aux, 4, part, rows)])(mid, top, low, local)
     even = lax.all_to_all(even, "aux", 0, 0, tiled=True)
     t1, t0, sums = kernel_call(
         near_kernel, [spec(VMEM)] * 7, [single(rows, rows), half(part, rows), single(2, 8, rows)]

time: 88.5 us -> 88.5 us (level)
  no operation moved by 1% of the time
where the time goes in v7:
time: 88.5 us; the launch traced here: 88.1 us
  starting transfers between devices  37.9 us (43%)
  blocking collectives  31.1 us (35%)
  waiting for transfers between devices  8.58 us (10%)
  Pallas kernels  8.38 us (9%)
  between operations  2.11 us (2%)
    ppermute x5, starting transfers between devices, moved_by(): return lax.ppermute(value, axis, pairs)  19 us
    all_to_all x1, starting transfers between devices, body(): energy = lax.all_to_all(energy, 'blk', 0, 0, tiled=True)  18.9 us
    all_to_all x1, blocking collectives, body(): odd = lax.all_to_all(odd, 'aux', 0, 0, tiled=True)  11.4 us
    all_to_all x1, blocking collectives, body(): even = lax.all_to_all(even, 'aux', 0, 0, tiled=True)  10.9 us
    all_to_all x1, blocking collectives, body(): far = lax.all_to_all(far, 'aux', 0, 0, tiled=True)  8.78 us
    all_to_all x1, waiting for transfers between devices, body(): energy = lax.all_to_all(energy, 'blk', 0, 0, tiled=True)  5.5 us
    ppermute x5, waiting for transfers between devices, moved_by(): return lax.ppermute(value, axis, pairs)  3.08 us
    pallas_call x1, Pallas kernels, align(): pl.pallas_call(functools.partial(align_kernel, CHUNKS), in_specs=[spec(SM...  2.87 us
  transfers between devices with their start and end apart: 6, of which 2 were waited for; matrix products, arithmetic and copies ran while one was open for 0% of the time, Pallas kernels for 3%

profile of v7, /device:TPU:1, one launch (start us, length us, event | category | flops | bytes accessed | tf_op | source)
XLA Modules:
  0.0 88.1 jit_solution(8102015338680028271)
XLA Ops:
  0.6 0.0 copy-start.2
  0.6 0.0 copy-start.1
  0.7 0.0 copy-start
  2.0 2.9 %shard_map.86 = (bf16[2,256,1024]{2,1,0:T(8,128)(2,1)S(1)}, bf16[2,256,1024]{2,1,0:T(8,128)(2,1)S(1)}, bf16[3,256,1024]{2,1,0:T(8,128)(2,1)S(1)}) custom-call(s32[1]{0:T(128)S(6)} %copy.9.start_ref, s32[1]{0:T(128)S(6)} %copy.10.count_ref, bf16[256,32,128]{2,1,0:T(8,128)(2,1)} %slab_hbm.1), custom_call_target="tpu_custom_call" | custom-call | tf_op jit(solution)/shard_map/pallas_call | solution.py:76
  4.9 1.3 %collective-permute-start.2 = (bf16[3,256,1024]{2,1,0:T(8,128)(2,1)S(1)}, bf16[3,256,1024]{2,1,0:T(8,128)(2,1)S(1)}, u32[]{:S(2)}, u32[]{:S(2)}) collective-permute-start(bf16[3,256,1024]{2,1,0:T(8,128)(2,1)S(1)} %get-tuple-element.18.low_ref), channel_id=1, source_target_pairs={{2,0},{3,1},{4,2},{5,3},{6,4},{7,5},{8,6},{9,7},{10,8},{11,9},{12,... | collective-permute-start | bytes 4718600 | tf_op jit(solution)/shard_map/ppermute | solution.py:25
  6.2 11.0 %collective-permute-start = (bf16[2,256,1024]{2,1,0:T(8,128)(2,1)S(1)}, bf16[2,256,1024]{2,1,0:T(8,128)(2,1)S(1)}, u32[]{:S(2)}, u32[]{:S(2)}) collective-permute-start(bf16[2,256,1024]{2,1,0:T(8,128)(2,1)S(1)} %get-tuple-element.16.mid_ref), channel_id=1, source_target_pairs={{0,1},{1,2},{2,3},{3,4},{4,5},{5,6},{6,7},{7,8},{8,9},{9,10},{10,1... | collective-permute-start | bytes 3145736 | tf_op jit(solution)/shard_map/ppermute | solution.py:25
  17.2 1.9 %collective-permute-start.1 = (bf16[2,256,1024]{2,1,0:T(8,128)(2,1)S(1)}, bf16[2,256,1024]{2,1,0:T(8,128)(2,1)S(1)}, u32[]{:S(2)}, u32[]{:S(2)}) collective-permute-start(bf16[2,256,1024]{2,1,0:T(8,128)(2,1)S(1)} %get-tuple-element.17.top_ref), channel_id=1, source_target_pairs={{0,1},{1,2},{2,3},{3,4},{4,5},{5,6},{6,7},{7,8},{8,9},{9,10},{10,1... | collective-permute-start | bytes 3145736 | tf_op jit(solution)/shard_map/ppermute | solution.py:25
  19.1 0.0 copy-done.2
  19.2 0.0 copy-done.1
  19.2 0.0 copy-done
  19.2 1.6 %shard_map.87 = (bf16[2,64,256]{2,1,0:T(8,128)(2,1)S(1)}, bf16[4,4,64,256]{3,2,1,0:T(8,128)(2,1)S(1)}, bf16[4,4,64,256]{3,2,1,0:T(8,128)(2,1)S(1)}) custom-call(s32[1,4]{1,0:T(1,128)S(1)} %copy-done.2, bf16[1,4,64,256]{3,2,1,0:T(8,128)(2,1)S(1)} %copy-done, bf16[1,4,64,256]{3,2,1,0:T(8,128)(2,1)S(1)} %copy-done.1, ...), custom_call_target="tpu_custom_call" | custom-call | tf_op jit(solution)/shard_map/pallas_call | solution.py:241
  20.8 11.4 %all_to_all.20 = bf16[4,4,64,256]{3,2,1,0:T(8,128)(2,1)S(1)} all-to-all(bf16[4,4,64,256]{3,2,1,0:T(8,128)(2,1)S(1)} %get-tuple-element.22), channel_id=1, replica_groups=mesh['aux'=4,'blk'=128] {'aux'}, dimensions={0} | all-to-all | bytes 1048576 | tf_op jit(solution)/shard_map/all_to_all | solution.py:246
  32.2 1.9 %collective-permute-start.3 = (bf16[4,4,64,256]{3,2,1,0:T(8,128)(2,1)S(1)}, bf16[4,4,64,256]{3,2,1,0:T(8,128)(2,1)S(1)}, u32[]{:S(2)}, u32[]{:S(2)}) collective-permute-start(bf16[4,4,64,256]{3,2,1,0:T(8,128)(2,1)S(1)} %all_to_all.20), channel_id=1, source_target_pairs={{0,1},{1,2},{2,3},{3,4},{4,5},{5,6},{6,7},{7,8},{8,9},{9,10},{10,1... | collective-permute-start | bytes 1572872 | tf_op jit(solution)/shard_map/ppermute | solution.py:25
  34.1 10.9 %all_to_all.21.even_ref = bf16[4,4,64,256]{3,2,1,0:T(8,128)(2,1)S(1)} all-to-all(bf16[4,4,64,256]{3,2,1,0:T(8,128)(2,1)S(1)} %get-tuple-element.19), channel_id=1, replica_groups=mesh['aux'=4,'blk'=128] {'aux'}, dimensions={0} | all-to-all | bytes 1048576 | tf_op jit(solution)/shard_map/all_to_all | solution.py:249
  45.1 0.0 collective-permute-done.before_mid_ref
  45.1 0.0 collective-permute-done.1.before_top_ref.before_ref
  45.1 0.7 shard_map.88
  45.8 0.0 collective-permute-done.3.odd_ref
  45.8 0.0 collective-permute-done.2.after_ref
  45.8 0.0 copy-start.3
  45.9 1.1 %shard_map.89 = bf16[4,208,256]{2,1,0:T(8,128)(2,1)S(1)} custom-call(bf16[2,256,1024]{2,1,0:T(8,128)(2,1)S(1)} %get-tuple-element.16.mid_ref, bf16[2,256,1024]{2,1,0:T(8,128)(2,1)S(1)} %get-tuple-element.17.top_ref, bf16[2,256,1024]{2,1,0:T(8,128)(2,1)S(1)} %collective-permute-done.1.before_top_ref.before_ref, ...), custom_call_target="tpu_custom_call" | custom-call | tf_op jit(solution)/shard_map/pallas_call | solution.py:253
  47.0 8.8 %all_to_all.22.parts_ref = bf16[4,208,256]{2,1,0:T(8,128)(2,1)S(1)} all-to-all(bf16[4,208,256]{2,1,0:T(8,128)(2,1)S(1)} %shard_map.89), channel_id=1, replica_groups=mesh['aux'=4,'blk'=128] {'aux'}, dimensions={0} | all-to-all | bytes 851968 | tf_op jit(solution)/shard_map/all_to_all | solution.py:256
  55.8 0.7 shard_map.90
  56.4 18.9 %all-to-all-start.3 = ((f32[128,1,128]{2,1,0:T(1,128)}), f32[128,1,128]{2,1,0:T(1,128)S(1)}, u32[]{:S(2)}, u32[]{:S(2)}) async-start(f32[128,1,128]{2,1,0:T(1,128)} %get-tuple-element.27), calls=%async_computation.3 | async-start | bytes 131072 | tf_op jit(solution)/shard_map/all_to_all | solution.py:261
  75.4 2.8 %collective-permute-start.4 = (bf16[2,64,256]{2,1,0:T(8,128)(2,1)S(1)}, bf16[2,64,256]{2,1,0:T(8,128)(2,1)S(1)}, u32[]{:S(2)}, u32[]{:S(2)}) collective-permute-start(bf16[2,64,256]{2,1,0:T(8,128)(2,1)S(1)} %get-tuple-element.26), channel_id=1, source_target_pairs={{1,0},{2,1},{3,2},{4,3},{5,4},{6,5},{7,6},{8,7},{9,8},{10,9},{11,1... | collective-permute-start | bytes 196616 | tf_op jit(solution)/shard_map/ppermute | solution.py:25
  78.2 3.1 %collective-permute-done.4.odd_ref = bf16[2,64,256]{2,1,0:T(8,128)(2,1)S(1)} collective-permute-done((bf16[2,64,256]{2,1,0:T(8,128)(2,1)S(1)}, bf16[2,64,256]{2,1,0:T(8,128)(2,1)S(1)}, u32[]{:S(2)}, u32[]{:S(2)}) %collective-permute-start.4) | collective-permute-done | bytes 65568 | tf_op jit(solution)/shard_map/ppermute | solution.py:25
  81.2 5.5 %all-to-all-done.3.energy_ref = f32[128,1,128]{2,1,0:T(1,128)S(1)} async-done(((f32[128,1,128]{2,1,0:T(1,128)}), f32[128,1,128]{2,1,0:T(1,128)S(1)}, u32[]{:S(2)}, u32[]{:S(2)}) %all-to-all-start.3) | async-done | bytes 65568 | tf_op jit(solution)/shard_map/all_to_all | solution.py:261
  86.7 0.0 copy-done.3
  86.7 1.4 %shard_map.91 = (bf16[1,4,64,256]{3,2,1,0:T(8,128)(2,1)}, f32[1,3]{1,0:T(1,128)}) custom-call(s32[1,4]{1,0:T(1,128)S(1)} %copy-done.2, f32[1,3]{1,0:T(1,128)S(1)} %bitcast.2, bf16[64,256]{1,0:T(8,128)(2,1)S(1)} %get-tuple-element.21.t0_ref, bf16[64,256]{1,0:T(8,128)(2,1)S(1)} %get-tuple-element.25.t2_ref, ...), custom_call_target="tpu_custom_call" | custom-call | tf_op jit(solution)/shard_map/pallas_call | solution.py:264
Async XLA Ops:
  0.6 18.5 %copy-start.2 = (s32[1,4]{1,0:T(1,128)S(1)}, s32[1,4]{1,0:T(1,128)}, u32[]{:S(2)}) copy-start(s32[1,4]{1,0:T(1,128)} %row_ref.3) | copy-start | bytes 52
  0.6 18.5 %copy-start.1 = (bf16[1,4,64,256]{3,2,1,0:T(8,128)(2,1)S(1)}, bf16[1,4,64,256]{3,2,1,0:T(8,128)(2,1)}, u32[]{:S(2)}) copy-start(bf16[1,4,64,256]{3,2,1,0:T(8,128)(2,1)} %direction_ref.1) | copy-start | bytes 393220
  0.7 18.5 %copy-start = (bf16[1,4,64,256]{3,2,1,0:T(8,128)(2,1)S(1)}, bf16[1,4,64,256]{3,2,1,0:T(8,128)(2,1)}, u32[]{:S(2)}) copy-start(bf16[1,4,64,256]{3,2,1,0:T(8,128)(2,1)} %density_ref.1) | copy-start | bytes 393220
  4.9 41.0 %collective-permute-start.2 = (bf16[3,256,1024]{2,1,0:T(8,128)(2,1)S(1)}, bf16[3,256,1024]{2,1,0:T(8,128)(2,1)S(1)}, u32[]{:S(2)}, u32[]{:S(2)}) collective-permute-start(bf16[3,256,1024]{2,1,0:T(8,128)(2,1)S(1)} %get-tuple-element.18.low_ref), channel_id=1, source_target_pairs={{2,0},{3,1},{4,2},{5,3},{6,4},{7,5},{8,6},{9,7},{10,8},{11,9},{12,... | collective-permute-start | bytes 4718600 | tf_op jit(solution)/shard_map/ppermute | solution.py:25
  6.2 38.9 %collective-permute-start = (bf16[2,256,1024]{2,1,0:T(8,128)(2,1)S(1)}, bf16[2,256,1024]{2,1,0:T(8,128)(2,1)S(1)}, u32[]{:S(2)}, u32[]{:S(2)}) collective-permute-start(bf16[2,256,1024]{2,1,0:T(8,128)(2,1)S(1)} %get-tuple-element.16.mid_ref), channel_id=1, source_target_pairs={{0,1},{1,2},{2,3},{3,4},{4,5},{5,6},{6,7},{7,8},{8,9},{9,10},{10,1... | collective-permute-start | bytes 3145736 | tf_op jit(solution)/shard_map/ppermute | solution.py:25
  17.2 27.9 %collective-permute-start.1 = (bf16[2,256,1024]{2,1,0:T(8,128)(2,1)S(1)}, bf16[2,256,1024]{2,1,0:T(8,128)(2,1)S(1)}, u32[]{:S(2)}, u32[]{:S(2)}) collective-permute-start(bf16[2,256,1024]{2,1,0:T(8,128)(2,1)S(1)} %get-tuple-element.17.top_ref), channel_id=1, source_target_pairs={{0,1},{1,2},{2,3},{3,4},{4,5},{5,6},{6,7},{7,8},{8,9},{9,10},{10,1... | collective-permute-start | bytes 3145736 | tf_op jit(solution)/shard_map/ppermute | solution.py:25
  32.2 13.6 %collective-permute-start.3 = (bf16[4,4,64,256]{3,2,1,0:T(8,128)(2,1)S(1)}, bf16[4,4,64,256]{3,2,1,0:T(8,128)(2,1)S(1)}, u32[]{:S(2)}, u32[]{:S(2)}) collective-permute-start(bf16[4,4,64,256]{3,2,1,0:T(8,128)(2,1)S(1)} %all_to_all.20), channel_id=1, source_target_pairs={{0,1},{1,2},{2,3},{3,4},{4,5},{5,6},{6,7},{7,8},{8,9},{9,10},{10,1... | collective-permute-start | bytes 1572872 | tf_op jit(solution)/shard_map/ppermute | solution.py:25
  45.8 40.9 %copy-start.3 = (f32[3]{0:T(128)S(1)}, f32[3]{0:T(128)}, u32[]{:S(2)}) copy-start(f32[3]{0:T(128)} %param.13) | copy-start | bytes 40
  56.4 30.3 %all-to-all-start.3 = ((f32[128,1,128]{2,1,0:T(1,128)}), f32[128,1,128]{2,1,0:T(1,128)S(1)}, u32[]{:S(2)}, u32[]{:S(2)}) async-start(f32[128,1,128]{2,1,0:T(1,128)} %get-tuple-element.27), calls=%async_computation.3 | async-start | bytes 131072 | tf_op jit(solution)/shard_map/all_to_all | solution.py:261
  75.4 5.9 %collective-permute-start.4 = (bf16[2,64,256]{2,1,0:T(8,128)(2,1)S(1)}, bf16[2,64,256]{2,1,0:T(8,128)(2,1)S(1)}, u32[]{:S(2)}, u32[]{:S(2)}) collective-permute-start(bf16[2,64,256]{2,1,0:T(8,128)(2,1)S(1)} %get-tuple-element.26), channel_id=1, source_target_pairs={{1,0},{2,1},{3,2},{4,3},{5,4},{6,5},{7,6},{8,7},{9,8},{10,9},{11,1... | collective-permute-start | bytes 196616 | tf_op jit(solution)/shard_map/ppermute | solution.py:25

commit v8 on v7

--- a/solution.py
+++ b/solution.py
@@ -196,7 +196,7 @@
     energy_ref[...] = jnp.broadcast_to(both[None], energy_ref.shape)
 
 
-def finish_kernel(scale, row_ref, steps_ref, t0_ref, t2_ref, odd_ref, energy_ref, tiles_ref, out_ref):
+def finish_kernel(scale, row_ref, steps_ref, t0_ref, t2_ref, odd_ref, energy_ref, tiles_hbm, out_ref, tiles_ref, sem):
     block = row_ref[0, 0]
     tiles = [t0_ref[...], odd_ref[0], t2_ref[...], odd_ref[1]]
     for s in range(4):
@@ -206,17 +206,21 @@
             chosen = (other >= 0) & (other - block == k)
             total = jnp.where(chosen, tiles[k].astype(jnp.float32), total)
         tiles_ref[0, s] = total.astype(jnp.bfloat16)
+    copy = pltpu.make_async_copy(tiles_ref, tiles_hbm, sem)
+    copy.start()
     total = jnp.sum(energy_ref[...], axis=0)
     first, second = total[:, :3], total[:, 64:67]
     out_ref[...] = -0.5 * (first + steps_ref[...] * second) * scale
-
-
-def kernel_call(kernel, in_specs, out_shape, limit=16, out_specs=None):
+    copy.wait()
+
+
+def kernel_call(kernel, in_specs, out_shape, limit=16, out_specs=None, scratch=()):
     return pl.pallas_call(
         kernel,
         in_specs=in_specs,
         out_specs=out_specs or [spec(VMEM)] * len(out_shape),
         out_shape=out_shape,
+        scratch_shapes=list(scratch),
         compiler_params=pltpu.CompilerParams(vmem_limit_bytes=limit * MIB),
     )
 
@@ -265,6 +269,8 @@
         functools.partial(finish_kernel, scale),
         [spec(SMEM)] + [spec(VMEM)] * 5,
         [half(1, slots, part, rows), single(1, 3)],
+        out_specs=[spec(pl.ANY), spec(VMEM)],
+        scratch=[VMEM((1, slots, part, rows), jnp.bfloat16), pltpu.SemaphoreType.DMA(())],
     )(partners, step_lengths[None], t0, t2, odd, energy)
     return tiles, energies[0]
 

time: 88.5 us -> 89 us (level)
  no operation moved by 1% of the time
where the time goes in v8:
time: 89 us; the launch traced here: 88.6 us
  starting transfers between devices  37.9 us (43%)
  blocking collectives  31.1 us (35%)
  Pallas kernels  8.92 us (10%)
  waiting for transfers between devices  8.58 us (10%)
  between operations  2.11 us (2%)
    ppermute x5, starting transfers between devices, moved_by(): return lax.ppermute(value, axis, pairs)  19 us
    all_to_all x1, starting transfers between devices, body(): energy = lax.all_to_all(energy, 'blk', 0, 0, tiled=True)  18.9 us
    all_to_all x1, blocking collectives, body(): odd = lax.all_to_all(odd, 'aux', 0, 0, tiled=True)  11.4 us
    all_to_all x1, blocking collectives, body(): even = lax.all_to_all(even, 'aux', 0, 0, tiled=True)  10.9 us
    all_to_all x1, blocking collectives, body(): far = lax.all_to_all(far, 'aux', 0, 0, tiled=True)  8.78 us
    all_to_all x1, waiting for transfers between devices, body(): energy = lax.all_to_all(energy, 'blk', 0, 0, tiled=True)  5.5 us
    ppermute x5, waiting for transfers between devices, moved_by(): return lax.ppermute(value, axis, pairs)  3.08 us
    pallas_call x1, Pallas kernels, align(): pl.pallas_call(functools.partial(align_kernel, CHUNKS), in_specs=[spec(SM...  2.87 us
  transfers between devices with their start and end apart: 6, of which 2 were waited for; matrix products, arithmetic and copies ran while one was open for 0% of the time, Pallas kernels for 3%

profile of v8, /device:TPU:1, one launch (start us, length us, event | category | flops | bytes accessed | tf_op | source)
XLA Modules:
  0.0 88.6 jit_solution(11616912893600878271)
XLA Ops:
  0.6 0.0 copy-start.2
  0.6 0.0 copy-start.1
  0.7 0.0 copy-start
  2.0 2.9 %shard_map.86 = (bf16[2,256,1024]{2,1,0:T(8,128)(2,1)S(1)}, bf16[2,256,1024]{2,1,0:T(8,128)(2,1)S(1)}, bf16[3,256,1024]{2,1,0:T(8,128)(2,1)S(1)}) custom-call(s32[1]{0:T(128)S(6)} %copy.9.start_ref, s32[1]{0:T(128)S(6)} %copy.10.count_ref, bf16[256,32,128]{2,1,0:T(8,128)(2,1)} %slab_hbm.1), custom_call_target="tpu_custom_call" | custom-call | tf_op jit(solution)/shard_map/pallas_call | solution.py:76
  4.9 1.3 %collective-permute-start.2 = (bf16[3,256,1024]{2,1,0:T(8,128)(2,1)S(1)}, bf16[3,256,1024]{2,1,0:T(8,128)(2,1)S(1)}, u32[]{:S(2)}, u32[]{:S(2)}) collective-permute-start(bf16[3,256,1024]{2,1,0:T(8,128)(2,1)S(1)} %get-tuple-element.18.low_ref), channel_id=1, source_target_pairs={{2,0},{3,1},{4,2},{5,3},{6,4},{7,5},{8,6},{9,7},{10,8},{11,9},{12,... | collective-permute-start | bytes 4718600 | tf_op jit(solution)/shard_map/ppermute | solution.py:25
  6.2 11.0 %collective-permute-start = (bf16[2,256,1024]{2,1,0:T(8,128)(2,1)S(1)}, bf16[2,256,1024]{2,1,0:T(8,128)(2,1)S(1)}, u32[]{:S(2)}, u32[]{:S(2)}) collective-permute-start(bf16[2,256,1024]{2,1,0:T(8,128)(2,1)S(1)} %get-tuple-element.16.mid_ref), channel_id=1, source_target_pairs={{0,1},{1,2},{2,3},{3,4},{4,5},{5,6},{6,7},{7,8},{8,9},{9,10},{10,1... | collective-permute-start | bytes 3145736 | tf_op jit(solution)/shard_map/ppermute | solution.py:25
  17.2 1.9 %collective-permute-start.1 = (bf16[2,256,1024]{2,1,0:T(8,128)(2,1)S(1)}, bf16[2,256,1024]{2,1,0:T(8,128)(2,1)S(1)}, u32[]{:S(2)}, u32[]{:S(2)}) collective-permute-start(bf16[2,256,1024]{2,1,0:T(8,128)(2,1)S(1)} %get-tuple-element.17.top_ref), channel_id=1, source_target_pairs={{0,1},{1,2},{2,3},{3,4},{4,5},{5,6},{6,7},{7,8},{8,9},{9,10},{10,1... | collective-permute-start | bytes 3145736 | tf_op jit(solution)/shard_map/ppermute | solution.py:25
  19.1 0.0 copy-done.2
  19.2 0.0 copy-done.1
  19.2 0.0 copy-done
  19.2 1.6 %shard_map.87 = (bf16[2,64,256]{2,1,0:T(8,128)(2,1)S(1)}, bf16[4,4,64,256]{3,2,1,0:T(8,128)(2,1)S(1)}, bf16[4,4,64,256]{3,2,1,0:T(8,128)(2,1)S(1)}) custom-call(s32[1,4]{1,0:T(1,128)S(1)} %copy-done.2, bf16[1,4,64,256]{3,2,1,0:T(8,128)(2,1)S(1)} %copy-done, bf16[1,4,64,256]{3,2,1,0:T(8,128)(2,1)S(1)} %copy-done.1, ...), custom_call_target="tpu_custom_call" | custom-call | tf_op jit(solution)/shard_map/pallas_call | solution.py:245
  20.8 11.4 %all_to_all.20 = bf16[4,4,64,256]{3,2,1,0:T(8,128)(2,1)S(1)} all-to-all(bf16[4,4,64,256]{3,2,1,0:T(8,128)(2,1)S(1)} %get-tuple-element.22), channel_id=1, replica_groups=mesh['aux'=4,'blk'=128] {'aux'}, dimensions={0} | all-to-all | bytes 1048576 | tf_op jit(solution)/shard_map/all_to_all | solution.py:250
  32.2 1.9 %collective-permute-start.3 = (bf16[4,4,64,256]{3,2,1,0:T(8,128)(2,1)S(1)}, bf16[4,4,64,256]{3,2,1,0:T(8,128)(2,1)S(1)}, u32[]{:S(2)}, u32[]{:S(2)}) collective-permute-start(bf16[4,4,64,256]{3,2,1,0:T(8,128)(2,1)S(1)} %all_to_all.20), channel_id=1, source_target_pairs={{0,1},{1,2},{2,3},{3,4},{4,5},{5,6},{6,7},{7,8},{8,9},{9,10},{10,1... | collective-permute-start | bytes 1572872 | tf_op jit(solution)/shard_map/ppermute | solution.py:25
  34.1 10.9 %all_to_all.21.even_ref = bf16[4,4,64,256]{3,2,1,0:T(8,128)(2,1)S(1)} all-to-all(bf16[4,4,64,256]{3,2,1,0:T(8,128)(2,1)S(1)} %get-tuple-element.19), channel_id=1, replica_groups=mesh['aux'=4,'blk'=128] {'aux'}, dimensions={0} | all-to-all | bytes 1048576 | tf_op jit(solution)/shard_map/all_to_all | solution.py:253
  45.1 0.0 collective-permute-done.before_mid_ref
  45.1 0.0 collective-permute-done.1.before_top_ref.before_ref
  45.1 0.7 shard_map.88
  45.8 0.0 collective-permute-done.3.odd_ref
  45.8 0.0 collective-permute-done.2.after_ref
  45.8 0.0 copy-start.3
  45.9 1.1 %shard_map.89 = bf16[4,208,256]{2,1,0:T(8,128)(2,1)S(1)} custom-call(bf16[2,256,1024]{2,1,0:T(8,128)(2,1)S(1)} %get-tuple-element.16.mid_ref, bf16[2,256,1024]{2,1,0:T(8,128)(2,1)S(1)} %get-tuple-element.17.top_ref, bf16[2,256,1024]{2,1,0:T(8,128)(2,1)S(1)} %collective-permute-done.1.before_top_ref.before_ref, ...), custom_call_target="tpu_custom_call" | custom-call | tf_op jit(solution)/shard_map/pallas_call | solution.py:257
  47.0 8.8 %all_to_all.22.parts_ref = bf16[4,208,256]{2,1,0:T(8,128)(2,1)S(1)} all-to-all(bf16[4,208,256]{2,1,0:T(8,128)(2,1)S(1)} %shard_map.89), channel_id=1, replica_groups=mesh['aux'=4,'blk'=128] {'aux'}, dimensions={0} | all-to-all | bytes 851968 | tf_op jit(solution)/shard_map/all_to_all | solution.py:260
  55.8 0.7 shard_map.90
  56.4 18.9 %all-to-all-start.3 = ((f32[128,1,128]{2,1,0:T(1,128)}), f32[128,1,128]{2,1,0:T(1,128)S(1)}, u32[]{:S(2)}, u32[]{:S(2)}) async-start(f32[128,1,128]{2,1,0:T(1,128)} %get-tuple-element.27), calls=%async_computation.3 | async-start | bytes 131072 | tf_op jit(solution)/shard_map/all_to_all | solution.py:265
  75.4 2.8 %collective-permute-start.4 = (bf16[2,64,256]{2,1,0:T(8,128)(2,1)S(1)}, bf16[2,64,256]{2,1,0:T(8,128)(2,1)S(1)}, u32[]{:S(2)}, u32[]{:S(2)}) collective-permute-start(bf16[2,64,256]{2,1,0:T(8,128)(2,1)S(1)} %get-tuple-element.26), channel_id=1, source_target_pairs={{1,0},{2,1},{3,2},{4,3},{5,4},{6,5},{7,6},{8,7},{9,8},{10,9},{11,1... | collective-permute-start | bytes 196616 | tf_op jit(solution)/shard_map/ppermute | solution.py:25
  78.2 3.1 %collective-permute-done.4.odd_ref = bf16[2,64,256]{2,1,0:T(8,128)(2,1)S(1)} collective-permute-done((bf16[2,64,256]{2,1,0:T(8,128)(2,1)S(1)}, bf16[2,64,256]{2,1,0:T(8,128)(2,1)S(1)}, u32[]{:S(2)}, u32[]{:S(2)}) %collective-permute-start.4) | collective-permute-done | bytes 65568 | tf_op jit(solution)/shard_map/ppermute | solution.py:25
  81.2 5.5 %all-to-all-done.3.energy_ref = f32[128,1,128]{2,1,0:T(1,128)S(1)} async-done(((f32[128,1,128]{2,1,0:T(1,128)}), f32[128,1,128]{2,1,0:T(1,128)S(1)}, u32[]{:S(2)}, u32[]{:S(2)}) %all-to-all-start.3) | async-done | bytes 65568 | tf_op jit(solution)/shard_map/all_to_all | solution.py:265
  86.7 0.0 copy-done.3
  86.7 1.9 %shard_map.91 = (bf16[1,4,64,256]{3,2,1,0:T(8,128)(2,1)}, f32[1,3]{1,0:T(1,128)}) custom-call(s32[1,4]{1,0:T(1,128)S(1)} %copy-done.2, f32[1,3]{1,0:T(1,128)S(1)} %bitcast.2, bf16[64,256]{1,0:T(8,128)(2,1)S(1)} %get-tuple-element.21.t0_ref, bf16[64,256]{1,0:T(8,128)(2,1)S(1)} %get-tuple-element.25.t2_ref, ...), custom_call_target="tpu_custom_call" | custom-call | tf_op jit(solution)/shard_map/pallas_call | solution.py:268
Async XLA Ops:
  0.6 18.5 %copy-start.2 = (s32[1,4]{1,0:T(1,128)S(1)}, s32[1,4]{1,0:T(1,128)}, u32[]{:S(2)}) copy-start(s32[1,4]{1,0:T(1,128)} %row_ref.3) | copy-start | bytes 52
  0.6 18.5 %copy-start.1 = (bf16[1,4,64,256]{3,2,1,0:T(8,128)(2,1)S(1)}, bf16[1,4,64,256]{3,2,1,0:T(8,128)(2,1)}, u32[]{:S(2)}) copy-start(bf16[1,4,64,256]{3,2,1,0:T(8,128)(2,1)} %direction_ref.1) | copy-start | bytes 393220
  0.7 18.5 %copy-start = (bf16[1,4,64,256]{3,2,1,0:T(8,128)(2,1)S(1)}, bf16[1,4,64,256]{3,2,1,0:T(8,128)(2,1)}, u32[]{:S(2)}) copy-start(bf16[1,4,64,256]{3,2,1,0:T(8,128)(2,1)} %density_ref.1) | copy-start | bytes 393220
  4.9 41.0 %collective-permute-start.2 = (bf16[3,256,1024]{2,1,0:T(8,128)(2,1)S(1)}, bf16[3,256,1024]{2,1,0:T(8,128)(2,1)S(1)}, u32[]{:S(2)}, u32[]{:S(2)}) collective-permute-start(bf16[3,256,1024]{2,1,0:T(8,128)(2,1)S(1)} %get-tuple-element.18.low_ref), channel_id=1, source_target_pairs={{2,0},{3,1},{4,2},{5,3},{6,4},{7,5},{8,6},{9,7},{10,8},{11,9},{12,... | collective-permute-start | bytes 4718600 | tf_op jit(solution)/shard_map/ppermute | solution.py:25
  6.2 38.9 %collective-permute-start = (bf16[2,256,1024]{2,1,0:T(8,128)(2,1)S(1)}, bf16[2,256,1024]{2,1,0:T(8,128)(2,1)S(1)}, u32[]{:S(2)}, u32[]{:S(2)}) collective-permute-start(bf16[2,256,1024]{2,1,0:T(8,128)(2,1)S(1)} %get-tuple-element.16.mid_ref), channel_id=1, source_target_pairs={{0,1},{1,2},{2,3},{3,4},{4,5},{5,6},{6,7},{7,8},{8,9},{9,10},{10,1... | collective-permute-start | bytes 3145736 | tf_op jit(solution)/shard_map/ppermute | solution.py:25
  17.2 27.9 %collective-permute-start.1 = (bf16[2,256,1024]{2,1,0:T(8,128)(2,1)S(1)}, bf16[2,256,1024]{2,1,0:T(8,128)(2,1)S(1)}, u32[]{:S(2)}, u32[]{:S(2)}) collective-permute-start(bf16[2,256,1024]{2,1,0:T(8,128)(2,1)S(1)} %get-tuple-element.17.top_ref), channel_id=1, source_target_pairs={{0,1},{1,2},{2,3},{3,4},{4,5},{5,6},{6,7},{7,8},{8,9},{9,10},{10,1... | collective-permute-start | bytes 3145736 | tf_op jit(solution)/shard_map/ppermute | solution.py:25
  32.2 13.6 %collective-permute-start.3 = (bf16[4,4,64,256]{3,2,1,0:T(8,128)(2,1)S(1)}, bf16[4,4,64,256]{3,2,1,0:T(8,128)(2,1)S(1)}, u32[]{:S(2)}, u32[]{:S(2)}) collective-permute-start(bf16[4,4,64,256]{3,2,1,0:T(8,128)(2,1)S(1)} %all_to_all.20), channel_id=1, source_target_pairs={{0,1},{1,2},{2,3},{3,4},{4,5},{5,6},{6,7},{7,8},{8,9},{9,10},{10,1... | collective-permute-start | bytes 1572872 | tf_op jit(solution)/shard_map/ppermute | solution.py:25
  45.8 40.9 %copy-start.3 = (f32[3]{0:T(128)S(1)}, f32[3]{0:T(128)}, u32[]{:S(2)}) copy-start(f32[3]{0:T(128)} %param.13) | copy-start | bytes 40
  56.4 30.3 %all-to-all-start.3 = ((f32[128,1,128]{2,1,0:T(1,128)}), f32[128,1,128]{2,1,0:T(1,128)S(1)}, u32[]{:S(2)}, u32[]{:S(2)}) async-start(f32[128,1,128]{2,1,0:T(1,128)} %get-tuple-element.27), calls=%async_computation.3 | async-start | bytes 131072 | tf_op jit(solution)/shard_map/all_to_all | solution.py:265
  75.4 5.9 %collective-permute-start.4 = (bf16[2,64,256]{2,1,0:T(8,128)(2,1)S(1)}, bf16[2,64,256]{2,1,0:T(8,128)(2,1)S(1)}, u32[]{:S(2)}, u32[]{:S(2)}) collective-permute-start(bf16[2,64,256]{2,1,0:T(8,128)(2,1)S(1)} %get-tuple-element.26), channel_id=1, source_target_pairs={{1,0},{2,1},{3,2},{4,3},{5,4},{6,5},{7,6},{8,7},{9,8},{10,9},{11,1... | collective-permute-start | bytes 196616 | tf_op jit(solution)/shard_map/ppermute | solution.py:25

commit v9 on v6

--- a/solution.py
+++ b/solution.py
@@ -12,7 +12,7 @@
 SMEM = pltpu.SMEM
 NT = (((1,), (1,)), ((), ()))
 MIB = 1024 * 1024
-CHUNKS = (64, 96, 96)
+CHUNKS = (32, 96, 128)
 
 
 def spec(space):

time: 88.5 us -> 88.5 us (level)
  no operation moved by 1% of the time
where the time goes in v9:
time: 88.5 us; the launch traced here: 88.1 us
  starting transfers between devices  37.9 us (43%)
  blocking collectives  31.1 us (35%)
  waiting for transfers between devices  8.58 us (10%)
  Pallas kernels  8.4 us (9%)
  between operations  2.12 us (2%)
    ppermute x5, starting transfers between devices, moved_by(): return lax.ppermute(value, axis, pairs)  19 us
    all_to_all x1, starting transfers between devices, body(): energy = lax.all_to_all(energy, 'blk', 0, 0, tiled=True)  18.9 us
    all_to_all x1, blocking collectives, body(): odd = lax.all_to_all(odd, 'aux', 0, 0, tiled=True)  11.4 us
    all_to_all x1, blocking collectives, body(): even = lax.all_to_all(even, 'aux', 0, 0, tiled=True)  10.9 us
    all_to_all x1, blocking collectives, body(): far = lax.all_to_all(far, 'aux', 0, 0, tiled=True)  8.78 us
    all_to_all x1, waiting for transfers between devices, body(): energy = lax.all_to_all(energy, 'blk', 0, 0, tiled=True)  5.5 us
    ppermute x5, waiting for transfers between devices, moved_by(): return lax.ppermute(value, axis, pairs)  3.08 us
    pallas_call x1, Pallas kernels, align(): pl.pallas_call(functools.partial(align_kernel, CHUNKS), in_specs=[spec(SM...  2.86 us
  transfers between devices with their start and end apart: 6, of which 2 were waited for; matrix products, arithmetic and copies ran while one was open for 0% of the time, Pallas kernels for 3%

profile of v9, /device:TPU:1, one launch (start us, length us, event | category | flops | bytes accessed | tf_op | source)
XLA Modules:
  0.0 88.1 jit_solution(10339971081593599302)
XLA Ops:
  0.6 0.0 copy-start.1
  0.6 0.0 copy-start
  0.7 0.0 copy-start.2
  2.0 2.9 %shard_map.86 = (bf16[2,256,1024]{2,1,0:T(8,128)(2,1)S(1)}, bf16[2,256,1024]{2,1,0:T(8,128)(2,1)S(1)}, bf16[3,256,1024]{2,1,0:T(8,128)(2,1)S(1)}) custom-call(s32[1]{0:T(128)S(6)} %copy.9.start_ref, s32[1]{0:T(128)S(6)} %copy.10.count_ref, bf16[256,32,128]{2,1,0:T(8,128)(2,1)} %slab_hbm.1), custom_call_target="tpu_custom_call" | custom-call | tf_op jit(solution)/shard_map/pallas_call | solution.py:76
  4.9 1.3 %collective-permute-start.2 = (bf16[3,256,1024]{2,1,0:T(8,128)(2,1)S(1)}, bf16[3,256,1024]{2,1,0:T(8,128)(2,1)S(1)}, u32[]{:S(2)}, u32[]{:S(2)}) collective-permute-start(bf16[3,256,1024]{2,1,0:T(8,128)(2,1)S(1)} %get-tuple-element.21.low_ref), channel_id=1, source_target_pairs={{2,0},{3,1},{4,2},{5,3},{6,4},{7,5},{8,6},{9,7},{10,8},{11,9},{12,... | collective-permute-start | bytes 4718600 | tf_op jit(solution)/shard_map/ppermute | solution.py:25
  6.2 11.0 %collective-permute-start = (bf16[2,256,1024]{2,1,0:T(8,128)(2,1)S(1)}, bf16[2,256,1024]{2,1,0:T(8,128)(2,1)S(1)}, u32[]{:S(2)}, u32[]{:S(2)}) collective-permute-start(bf16[2,256,1024]{2,1,0:T(8,128)(2,1)S(1)} %get-tuple-element.18.mid_ref), channel_id=1, source_target_pairs={{0,1},{1,2},{2,3},{3,4},{4,5},{5,6},{6,7},{7,8},{8,9},{9,10},{10,1... | collective-permute-start | bytes 3145736 | tf_op jit(solution)/shard_map/ppermute | solution.py:25
  17.2 1.9 %collective-permute-start.1 = (bf16[2,256,1024]{2,1,0:T(8,128)(2,1)S(1)}, bf16[2,256,1024]{2,1,0:T(8,128)(2,1)S(1)}, u32[]{:S(2)}, u32[]{:S(2)}) collective-permute-start(bf16[2,256,1024]{2,1,0:T(8,128)(2,1)S(1)} %get-tuple-element.19.top_ref), channel_id=1, source_target_pairs={{0,1},{1,2},{2,3},{3,4},{4,5},{5,6},{6,7},{7,8},{8,9},{9,10},{10,1... | collective-permute-start | bytes 3145736 | tf_op jit(solution)/shard_map/ppermute | solution.py:25
  19.1 0.0 copy-done.1
  19.1 0.0 copy-done
  19.2 0.0 copy-done.2
  19.2 0.7 shard_map.87
  19.9 11.4 %all_to_all.20 = bf16[4,4,64,256]{3,2,1,0:T(8,128)(2,1)S(1)} all-to-all(bf16[4,4,64,256]{3,2,1,0:T(8,128)(2,1)S(1)} %get-tuple-element.26), channel_id=1, replica_groups=mesh['aux'=4,'blk'=128] {'aux'}, dimensions={0} | all-to-all | bytes 1048576 | tf_op jit(solution)/shard_map/all_to_all | solution.py:247
  31.3 1.9 %collective-permute-start.3 = (bf16[4,4,64,256]{3,2,1,0:T(8,128)(2,1)S(1)}, bf16[4,4,64,256]{3,2,1,0:T(8,128)(2,1)S(1)}, u32[]{:S(2)}, u32[]{:S(2)}) collective-permute-start(bf16[4,4,64,256]{3,2,1,0:T(8,128)(2,1)S(1)} %all_to_all.20), channel_id=1, source_target_pairs={{0,1},{1,2},{2,3},{3,4},{4,5},{5,6},{6,7},{7,8},{8,9},{9,10},{10,1... | collective-permute-start | bytes 1572872 | tf_op jit(solution)/shard_map/ppermute | solution.py:25
  33.2 0.9 shard_map.88
  34.1 10.9 %all_to_all.21.even_ref = bf16[4,4,64,256]{3,2,1,0:T(8,128)(2,1)S(1)} all-to-all(bf16[4,4,64,256]{3,2,1,0:T(8,128)(2,1)S(1)} %shard_map.88), channel_id=1, replica_groups=mesh['aux'=4,'blk'=128] {'aux'}, dimensions={0} | all-to-all | bytes 1048576 | tf_op jit(solution)/shard_map/all_to_all | solution.py:252
  45.1 0.0 collective-permute-done.before_mid_ref
  45.1 0.0 collective-permute-done.1.before_top_ref.before_ref
  45.1 0.8 shard_map.89
  45.8 0.0 collective-permute-done.3.odd_ref
  45.8 0.0 collective-permute-done.2.after_ref
  45.9 0.0 copy-start.3
  45.9 1.1 %shard_map.90 = bf16[4,208,256]{2,1,0:T(8,128)(2,1)S(1)} custom-call(bf16[2,256,1024]{2,1,0:T(8,128)(2,1)S(1)} %get-tuple-element.18.mid_ref, bf16[2,256,1024]{2,1,0:T(8,128)(2,1)S(1)} %get-tuple-element.19.top_ref, bf16[2,256,1024]{2,1,0:T(8,128)(2,1)S(1)} %collective-permute-done.1.before_top_ref.before_ref, ...), custom_call_target="tpu_custom_call" | custom-call | tf_op jit(solution)/shard_map/pallas_call | solution.py:256
  47.0 8.8 %all_to_all.22.parts_ref = bf16[4,208,256]{2,1,0:T(8,128)(2,1)S(1)} all-to-all(bf16[4,208,256]{2,1,0:T(8,128)(2,1)S(1)} %shard_map.90), channel_id=1, replica_groups=mesh['aux'=4,'blk'=128] {'aux'}, dimensions={0} | all-to-all | bytes 851968 | tf_op jit(solution)/shard_map/all_to_all | solution.py:259
  55.8 0.7 shard_map.91
  56.5 18.9 %all-to-all-start.3 = ((f32[128,1,128]{2,1,0:T(1,128)}), f32[128,1,128]{2,1,0:T(1,128)S(1)}, u32[]{:S(2)}, u32[]{:S(2)}) async-start(f32[128,1,128]{2,1,0:T(1,128)} %get-tuple-element.31), calls=%async_computation.3 | async-start | bytes 131072 | tf_op jit(solution)/shard_map/all_to_all | solution.py:264
  75.4 2.8 %collective-permute-start.4 = (bf16[2,64,256]{2,1,0:T(8,128)(2,1)S(1)}, bf16[2,64,256]{2,1,0:T(8,128)(2,1)S(1)}, u32[]{:S(2)}, u32[]{:S(2)}) collective-permute-start(bf16[2,64,256]{2,1,0:T(8,128)(2,1)S(1)} %get-tuple-element.30), channel_id=1, source_target_pairs={{1,0},{2,1},{3,2},{4,3},{5,4},{6,5},{7,6},{8,7},{9,8},{10,9},{11,1... | collective-permute-start | bytes 196616 | tf_op jit(solution)/shard_map/ppermute | solution.py:25
  78.2 3.1 %collective-permute-done.4.odd_ref = bf16[2,64,256]{2,1,0:T(8,128)(2,1)S(1)} collective-permute-done((bf16[2,64,256]{2,1,0:T(8,128)(2,1)S(1)}, bf16[2,64,256]{2,1,0:T(8,128)(2,1)S(1)}, u32[]{:S(2)}, u32[]{:S(2)}) %collective-permute-start.4) | collective-permute-done | bytes 65568 | tf_op jit(solution)/shard_map/ppermute | solution.py:25
  81.3 5.5 %all-to-all-done.3.energy_ref = f32[128,1,128]{2,1,0:T(1,128)S(1)} async-done(((f32[128,1,128]{2,1,0:T(1,128)}), f32[128,1,128]{2,1,0:T(1,128)S(1)}, u32[]{:S(2)}, u32[]{:S(2)}) %all-to-all-start.3) | async-done | bytes 65568 | tf_op jit(solution)/shard_map/all_to_all | solution.py:264
  86.8 0.0 copy-done.3
  86.8 1.4 %shard_map.92 = (bf16[1,4,64,256]{3,2,1,0:T(8,128)(2,1)}, f32[1,3]{1,0:T(1,128)}) custom-call(s32[1,4]{1,0:T(1,128)S(1)} %copy-done.2, f32[1,3]{1,0:T(1,128)S(1)} %bitcast.2, bf16[64,256]{1,0:T(8,128)(2,1)S(1)} %get-tuple-element.25.t0_ref, bf16[64,256]{1,0:T(8,128)(2,1)S(1)} %get-tuple-element.29.t2_ref, ...), custom_call_target="tpu_custom_call" | custom-call | tf_op jit(solution)/shard_map/pallas_call | solution.py:267
Async XLA Ops:
  0.6 18.5 %copy-start.1 = (bf16[1,4,64,256]{3,2,1,0:T(8,128)(2,1)S(1)}, bf16[1,4,64,256]{3,2,1,0:T(8,128)(2,1)}, u32[]{:S(2)}) copy-start(bf16[1,4,64,256]{3,2,1,0:T(8,128)(2,1)} %direction_ref) | copy-start | bytes 393220
  0.6 18.5 %copy-start = (bf16[1,4,64,256]{3,2,1,0:T(8,128)(2,1)S(1)}, bf16[1,4,64,256]{3,2,1,0:T(8,128)(2,1)}, u32[]{:S(2)}) copy-start(bf16[1,4,64,256]{3,2,1,0:T(8,128)(2,1)} %density_ref) | copy-start | bytes 393220
  0.7 18.5 %copy-start.2 = (s32[1,4]{1,0:T(1,128)S(1)}, s32[1,4]{1,0:T(1,128)}, u32[]{:S(2)}) copy-start(s32[1,4]{1,0:T(1,128)} %row_ref.3) | copy-start | bytes 52
  4.9 41.0 %collective-permute-start.2 = (bf16[3,256,1024]{2,1,0:T(8,128)(2,1)S(1)}, bf16[3,256,1024]{2,1,0:T(8,128)(2,1)S(1)}, u32[]{:S(2)}, u32[]{:S(2)}) collective-permute-start(bf16[3,256,1024]{2,1,0:T(8,128)(2,1)S(1)} %get-tuple-element.21.low_ref), channel_id=1, source_target_pairs={{2,0},{3,1},{4,2},{5,3},{6,4},{7,5},{8,6},{9,7},{10,8},{11,9},{12,... | collective-permute-start | bytes 4718600 | tf_op jit(solution)/shard_map/ppermute | solution.py:25
  6.2 38.9 %collective-permute-start = (bf16[2,256,1024]{2,1,0:T(8,128)(2,1)S(1)}, bf16[2,256,1024]{2,1,0:T(8,128)(2,1)S(1)}, u32[]{:S(2)}, u32[]{:S(2)}) collective-permute-start(bf16[2,256,1024]{2,1,0:T(8,128)(2,1)S(1)} %get-tuple-element.18.mid_ref), channel_id=1, source_target_pairs={{0,1},{1,2},{2,3},{3,4},{4,5},{5,6},{6,7},{7,8},{8,9},{9,10},{10,1... | collective-permute-start | bytes 3145736 | tf_op jit(solution)/shard_map/ppermute | solution.py:25
  17.2 27.9 %collective-permute-start.1 = (bf16[2,256,1024]{2,1,0:T(8,128)(2,1)S(1)}, bf16[2,256,1024]{2,1,0:T(8,128)(2,1)S(1)}, u32[]{:S(2)}, u32[]{:S(2)}) collective-permute-start(bf16[2,256,1024]{2,1,0:T(8,128)(2,1)S(1)} %get-tuple-element.19.top_ref), channel_id=1, source_target_pairs={{0,1},{1,2},{2,3},{3,4},{4,5},{5,6},{6,7},{7,8},{8,9},{9,10},{10,1... | collective-permute-start | bytes 3145736 | tf_op jit(solution)/shard_map/ppermute | solution.py:25
  31.3 14.5 %collective-permute-start.3 = (bf16[4,4,64,256]{3,2,1,0:T(8,128)(2,1)S(1)}, bf16[4,4,64,256]{3,2,1,0:T(8,128)(2,1)S(1)}, u32[]{:S(2)}, u32[]{:S(2)}) collective-permute-start(bf16[4,4,64,256]{3,2,1,0:T(8,128)(2,1)S(1)} %all_to_all.20), channel_id=1, source_target_pairs={{0,1},{1,2},{2,3},{3,4},{4,5},{5,6},{6,7},{7,8},{8,9},{9,10},{10,1... | collective-permute-start | bytes 1572872 | tf_op jit(solution)/shard_map/ppermute | solution.py:25
  45.9 40.9 %copy-start.3 = (f32[3]{0:T(128)S(1)}, f32[3]{0:T(128)}, u32[]{:S(2)}) copy-start(f32[3]{0:T(128)} %param.13) | copy-start | bytes 40
  56.5 30.3 %all-to-all-start.3 = ((f32[128,1,128]{2,1,0:T(1,128)}), f32[128,1,128]{2,1,0:T(1,128)S(1)}, u32[]{:S(2)}, u32[]{:S(2)}) async-start(f32[128,1,128]{2,1,0:T(1,128)} %get-tuple-element.31), calls=%async_computation.3 | async-start | bytes 131072 | tf_op jit(solution)/shard_map/all_to_all | solution.py:264
  75.4 5.9 %collective-permute-start.4 = (bf16[2,64,256]{2,1,0:T(8,128)(2,1)S(1)}, bf16[2,64,256]{2,1,0:T(8,128)(2,1)S(1)}, u32[]{:S(2)}, u32[]{:S(2)}) collective-permute-start(bf16[2,64,256]{2,1,0:T(8,128)(2,1)S(1)} %get-tuple-element.30), channel_id=1, source_target_pairs={{1,0},{2,1},{3,2},{4,3},{5,4},{6,5},{7,6},{8,7},{9,8},{10,9},{11,1... | collective-permute-start | bytes 196616 | tf_op jit(solution)/shard_map/ppermute | solution.py:25
